TPU v7x, 32 devices: a whole 2x2x4 slice. The times are simulated.
32 devices in a mesh: seq: 4 (over z), fsdp: 8 (over y, x, core).
Axes of the slice: x: 2, y: 2, z: 4, core: 2. Of those that a mesh axis runs over, the one named last changes fastest.
Arguments:
- tokens: bfloat16 [8, 1024, 1024], P('fsdp', 'seq'), may hold values from -6 to 6
- routes: int32 [8, 1024, 8], P('fsdp', 'seq'), may hold values from 0 to 31, all different within a row; in each aligned block of 256 rows (0 to 255, 256 to 511, ..., all dimensions but the last counted through in order) at most 96 rows name the same one
- cotangent: bfloat16 [8, 1024, 1024], P('fsdp', 'seq'), may hold values from -6 to 6
- norm_gains: float32 [2, 1024], P(None, 'fsdp'), may hold values from 0.5 to 1.5
- qkv_weight: float32 [1024, 2048], P('fsdp'), may hold values from -4 to 4
- out_weight: float32 [1024, 1024], P('fsdp'), may hold values from -3 to 3
- router_weight: float32 [1024, 32], P('fsdp'), may hold values from -1 to 1
- expert_up: float32 [32, 1024, 1024], P('seq', 'fsdp'), may hold values from -0.1875 to 0.1875
- expert_down: float32 [32, 512, 1024], P('seq', 'fsdp'), may hold values from -1 to 1
- mean_gains: float32 [2, 1024], P(None, 'fsdp')
- square_gains: float32 [2, 1024], P(None, 'fsdp'), as said below
- mean_qkv: float32 [1024, 2048], P('fsdp')
- square_qkv: float32 [1024, 2048], P('fsdp'), as said below
- mean_out: float32 [1024, 1024], P('fsdp')
- square_out: float32 [1024, 1024], P('fsdp'), as said below
- mean_router: float32 [1024, 32], P('fsdp')
- square_router: float32 [1024, 32], P('fsdp'), as said below
- mean_up: float32 [32, 1024, 1024], P('seq', 'fsdp')
- square_up: float32 [32, 1024, 1024], P('seq', 'fsdp'), as said below
- mean_down: float32 [32, 512, 1024], P('seq', 'fsdp')
- square_down: float32 [32, 512, 1024], P('seq', 'fsdp'), as said below
Outputs:
- output: bfloat16 [8, 1024, 1024], P('fsdp', 'seq')
- tokens_grad: float32 [8, 1024, 1024], P('fsdp', 'seq')
- grad_gains: float32 [2, 1024], P(None, 'fsdp')
- grad_qkv: float32 [1024, 2048], P('fsdp')
- grad_out: float32 [1024, 1024], P('fsdp')
- grad_router: float32 [1024, 32], P('fsdp')
- grad_up: float32 [32, 1024, 1024], P('seq', 'fsdp')
- grad_down: float32 [32, 512, 1024], P('seq', 'fsdp')
- fresh_gains: float32 [2, 1024], P(None, 'fsdp')
- fresh_qkv: float32 [1024, 2048], P('fsdp')
- fresh_out: float32 [1024, 1024], P('fsdp')
- fresh_router: float32 [1024, 32], P('fsdp')
- fresh_up: float32 [32, 1024, 1024], P('seq', 'fsdp')
- fresh_down: float32 [32, 512, 1024], P('seq', 'fsdp')
- momentum_gains: float32 [2, 1024], P(None, 'fsdp')
- momentum_qkv: float32 [1024, 2048], P('fsdp')
- momentum_out: float32 [1024, 1024], P('fsdp')
- momentum_router: float32 [1024, 32], P('fsdp')
- momentum_up: float32 [32, 1024, 1024], P('seq', 'fsdp')
- momentum_down: float32 [32, 512, 1024], P('seq', 'fsdp')
- variance_gains: float32 [2, 1024], P(None, 'fsdp')
- variance_qkv: float32 [1024, 2048], P('fsdp')
- variance_out: float32 [1024, 1024], P('fsdp')
- variance_router: float32 [1024, 32], P('fsdp')
- variance_up: float32 [32, 1024, 1024], P('seq', 'fsdp')
- variance_down: float32 [32, 512, 1024], P('seq', 'fsdp')
Inputs may be any that keep to these rules, and one draw needn't show every extreme that they name: `routes`: each token names 8 different experts; among the 256 tokens of one device no expert is named more than 96 times. `square_gains`: positive. `square_qkv`: positive. `square_out`: positive. `square_router`: positive. `square_up`: positive. `square_down`: positive.
All inputs are finite; a program needn't handle non-finite values.
Results may differ from a plain program's by a relative error of at most 0.02.
Values may be sent and summed in bfloat16 or wider, within the bound.
No kernel may reach another device: no remote copies, remote signals or barrier semaphores. Data moves between devices by JAX's collectives and lax.ppermute only.
A program may use at most 256 MiB of HBM per device.

v0:
```python
import jax
import jax.numpy as jnp
from jax import lax
from jax.sharding import PartitionSpec as P

MODEL_WIDTH = 1024
QUERY_HEADS = 16
KEY_VALUE_HEADS = 8
HEAD_SIZE = 64
EXPERTS = 32
FF = 512
TOP = 8
STEP = 3
CAP = 96


epsilon = 1e-06
res_scale = 0.22
att_scale = 0.015625
beta_one = 0.9
beta_two = 0.95
adam_eps = 1e-08
weight_decay = 0.1
learn_rates = (0.4, 0.04, 0.2, 0.01, 0.01, 0.05)


def rope_tables(length_total, offset):
    position = (offset + jnp.arange(length_total)).astype(jnp.float32)
    frequency = 10000.0 ** (-(jnp.arange(HEAD_SIZE // 2).astype(jnp.float32) * 2.0 / HEAD_SIZE))
    angles = position[:, None] * frequency[None, :]
    angles = jnp.concatenate([angles, angles], axis=1)
    return (jnp.cos(angles)[:, None, :], jnp.sin(angles)[:, None, :])


def rotate(values, cosine_table, sine_table):
    middle = values.shape[-1] // 2
    turned = jnp.concatenate([-values[..., middle:], values[..., :middle]], axis=-1)
    return values * cosine_table + turned * sine_table


def rotate_back(gradient, cosine_table, sine_table):
    middle = gradient.shape[-1] // 2
    scaled = gradient * sine_table
    turned = jnp.concatenate([scaled[..., middle:], -scaled[..., :middle]], axis=-1)
    return gradient * cosine_table + turned


def split_heads(projected_input, cosine_table, sine_table):
    length_total = projected_input.shape[0]
    query_rows_all = rotate(
        projected_input[:, : QUERY_HEADS * HEAD_SIZE].reshape(length_total, QUERY_HEADS, HEAD_SIZE),
        cosine_table,
        sine_table,
    )
    paired_values = projected_input[:, QUERY_HEADS * HEAD_SIZE :].reshape(
        length_total, KEY_VALUE_HEADS, 2, HEAD_SIZE
    )
    rotated_keys = rotate(paired_values[:, :, 0], cosine_table, sine_table)
    paired_values = jnp.stack([rotated_keys, paired_values[:, :, 1]], axis=2)
    return (
        query_rows_all.reshape(length_total, QUERY_HEADS * HEAD_SIZE),
        paired_values.reshape(length_total, KEY_VALUE_HEADS * 2 * HEAD_SIZE),
    )


def norm_forward(values, gain_row):
    scale_inv = lax.rsqrt(jnp.mean(values * values, axis=-1, keepdims=True) + epsilon)
    return (values * scale_inv * gain_row, scale_inv)


def norm_backward(upstream, values, scale_inv, gain_row):
    normed = values * scale_inv
    scaled = upstream * gain_row
    inner_mean = jnp.mean(scaled * normed, axis=-1, keepdims=True)
    return (scale_inv * (scaled - normed * inner_mean), jnp.sum(upstream * normed, axis=0))


def adam_update(weight, gradient, first, second, rate):
    first_new = beta_one * first + (1.0 - beta_one) * gradient
    second_new = beta_two * second + (1.0 - beta_two) * gradient * gradient
    first_hat = first_new / (1.0 - beta_one**STEP)
    second_hat = second_new / (1.0 - beta_two**STEP)
    fresh = weight - rate * (first_hat / (jnp.sqrt(second_hat) + adam_eps) + weight_decay * weight)
    return (fresh, first_new, second_new)


def owners_of(block_routes, pair_count):
    expert_ids = jnp.arange(EXPERTS, dtype=jnp.int32)
    flat_routes = block_routes.reshape(-1)
    expert_hits = (flat_routes[:, None] == expert_ids[None, :]).astype(jnp.int32)
    before = jnp.cumsum(expert_hits, axis=0) - expert_hits
    slot_rank = jnp.sum(before * expert_hits, axis=-1)
    slot_index = flat_routes * CAP + slot_rank
    slot_owner = (
        jnp.full((EXPERTS * CAP,), pair_count, jnp.int32)
        .at[slot_index]
        .set(jnp.arange(pair_count, dtype=jnp.int32))
    )
    return (slot_index, slot_owner)


def shards(
    tokens,
    routes,
    cotangent,
    norm_gains,
    qkv_weight,
    out_weight,
    router_weight,
    expert_up,
    expert_down,
    mean_gains,
    square_gains,
    mean_qkv,
    square_qkv,
    mean_out,
    square_out,
    mean_router,
    square_router,
    mean_up,
    square_up,
    mean_down,
    square_down,
):
    token_row_list = tokens.shape[1]
    sequence_members = lax.axis_size("seq")
    seq_length = token_row_list * sequence_members
    resident_heads = KEY_VALUE_HEADS // sequence_members
    head_grouping = QUERY_HEADS // KEY_VALUE_HEADS
    block_rows = min(512, seq_length)
    block_count = seq_length // block_rows
    pair_count = token_row_list * TOP
    gains_half, qkv_half, out_half, router_half, up_half, down_half = (
        lax.all_gather(norm_gains.astype(jnp.bfloat16), "fsdp", axis=1, tiled=True),
        lax.all_gather(qkv_weight.astype(jnp.bfloat16), "fsdp", axis=0, tiled=True),
        lax.all_gather(out_weight.astype(jnp.bfloat16), "fsdp", axis=0, tiled=True),
        lax.all_gather(router_weight.astype(jnp.bfloat16), "fsdp", axis=0, tiled=True),
        lax.all_gather(expert_up.astype(jnp.bfloat16), "fsdp", axis=1, tiled=True),
        lax.all_gather(expert_down.astype(jnp.bfloat16), "fsdp", axis=1, tiled=True),
    )
    gain_one = gains_half[0].astype(jnp.float32)
    gain_two = gains_half[1].astype(jnp.float32)
    source = tokens[0].astype(jnp.float32)
    normed_one, inv_one = norm_forward(source, gain_one)
    normed_first = normed_one.astype(jnp.bfloat16)
    projected_input = jnp.dot(normed_first, qkv_half, preferred_element_type=jnp.float32)
    cosine_table, sine_table = rope_tables(token_row_list, lax.axis_index("seq") * token_row_list)
    query_rows_all, paired_values = split_heads(projected_input, cosine_table, sine_table)
    packed = jnp.stack([query_rows_all, paired_values], axis=1).astype(jnp.bfloat16)
    by_head = lax.all_to_all(packed, "seq", split_axis=2, concat_axis=0, tiled=True)
    query_per_head = by_head[:, 0].reshape(seq_length, resident_heads, head_grouping, HEAD_SIZE)
    paired_heads = by_head[:, 1].reshape(seq_length, resident_heads, 2, HEAD_SIZE)
    key_part = paired_heads[:, :, 0]
    value_part = paired_heads[:, :, 1]
    key_columns = jnp.arange(seq_length)

    def scores_for(block_index):
        row_start = block_index * block_rows
        query_block = lax.dynamic_slice_in_dim(query_per_head, row_start, block_rows, 0)
        scores = (
            jnp.einsum("qhgd,khd->hgqk", query_block, key_part, preferred_element_type=jnp.float32)
            * att_scale
        )
        causal = (row_start + jnp.arange(block_rows))[:, None] >= key_columns[None, :]
        return (query_block, jnp.where(causal, scores, -jnp.inf))

    def attend_block(running, block_index):
        query_block, scores = scores_for(block_index)
        top_score = jnp.max(scores, axis=-1, keepdims=True)
        logsum = top_score + jnp.log(jnp.sum(jnp.exp(scores - top_score), axis=-1, keepdims=True))
        weights = jnp.exp(scores - logsum).astype(jnp.bfloat16)
        outputs = jnp.einsum(
            "hgqk,khd->qhgd", weights, value_part, preferred_element_type=jnp.float32
        )
        return (running, (outputs.astype(jnp.bfloat16), logsum[..., 0]))

    unused, (attended, logsums) = lax.scan(attend_block, 0, jnp.arange(block_count))
    attended_heads = attended.reshape(seq_length, resident_heads * head_grouping * HEAD_SIZE)
    back = lax.all_to_all(attended_heads, "seq", split_axis=0, concat_axis=1, tiled=True)
    resid = source + res_scale * jnp.dot(back, out_half, preferred_element_type=jnp.float32)
    normed_two, inv_two = norm_forward(resid, gain_two)
    normed_second = normed_two.astype(jnp.bfloat16)
    logits = jnp.dot(normed_second, router_half, preferred_element_type=jnp.float32)
    local_routes = routes[0]
    expert_ids = jnp.arange(EXPERTS, dtype=jnp.int32)
    choose = (local_routes[:, :, None] == expert_ids[None, None, :]).astype(jnp.float32)
    picked = jnp.sum(choose * logits[:, None, :], axis=-1)
    gate_probs = jax.nn.softmax(picked, axis=-1)
    slot_index, slot_owner = owners_of(local_routes, pair_count)
    padded_normed = jnp.concatenate(
        [normed_second, jnp.zeros((1, MODEL_WIDTH), jnp.bfloat16)], axis=0
    )
    dispatch = padded_normed[slot_owner // TOP].reshape(EXPERTS, CAP, MODEL_WIDTH)
    arrived = lax.all_to_all(dispatch, "seq", split_axis=0, concat_axis=1, tiled=True)
    upgate = jnp.einsum("ecd,edf->ecf", arrived, up_half, preferred_element_type=jnp.float32)
    gate_part = upgate[..., :FF]
    up_part = upgate[..., FF:]
    sigmoid_gate = jax.nn.sigmoid(gate_part)
    swish_gate = gate_part * sigmoid_gate
    hidden = (swish_gate * up_part).astype(jnp.bfloat16)
    produced = jnp.einsum(
        "ecf,efd->ecd", hidden, down_half, preferred_element_type=jnp.float32
    ).astype(jnp.bfloat16)
    returned = lax.all_to_all(produced, "seq", split_axis=1, concat_axis=0, tiled=True)
    row_values = (
        returned.reshape(EXPERTS * CAP, MODEL_WIDTH)[slot_index]
        .astype(jnp.float32)
        .reshape(token_row_list, TOP, MODEL_WIDTH)
    )
    mixture = jnp.sum(gate_probs[:, :, None] * row_values, axis=1)
    output = (resid + res_scale * mixture).astype(jnp.bfloat16)[None]
    upstream = cotangent[0].astype(jnp.float32)
    branch = res_scale * upstream
    gate_grad = jnp.sum(row_values * branch[:, None, :], axis=-1)
    slot_values = (
        (gate_probs[:, :, None] * branch[:, None, :])
        .astype(jnp.bfloat16)
        .reshape(pair_count, MODEL_WIDTH)
    )
    slot_padded = jnp.concatenate([slot_values, jnp.zeros((1, MODEL_WIDTH), jnp.bfloat16)], axis=0)
    outgoing = slot_padded[slot_owner].reshape(EXPERTS, CAP, MODEL_WIDTH)
    incoming = lax.all_to_all(outgoing, "seq", split_axis=0, concat_axis=1, tiled=True)
    hidden_grad = jnp.einsum(
        "ecd,efd->ecf", incoming, down_half, preferred_element_type=jnp.float32
    )
    grad_down = jnp.einsum("ecf,ecd->efd", hidden, incoming, preferred_element_type=jnp.float32)
    swish_grad = sigmoid_gate * (1.0 + gate_part * (1.0 - sigmoid_gate))
    upgate_grad = jnp.concatenate(
        [hidden_grad * up_part * swish_grad, hidden_grad * swish_gate], axis=-1
    ).astype(jnp.bfloat16)
    grad_up = jnp.einsum("ecd,ecf->edf", arrived, upgate_grad, preferred_element_type=jnp.float32)
    input_slots = jnp.einsum(
        "ecf,edf->ecd", upgate_grad, up_half, preferred_element_type=jnp.float32
    ).astype(jnp.bfloat16)
    sent_back = lax.all_to_all(input_slots, "seq", split_axis=1, concat_axis=0, tiled=True)
    normed_grad = jnp.sum(
        sent_back.reshape(EXPERTS * CAP, MODEL_WIDTH)[slot_index]
        .astype(jnp.float32)
        .reshape(token_row_list, TOP, MODEL_WIDTH),
        axis=1,
    )
    picked_grad = gate_probs * (gate_grad - jnp.sum(gate_probs * gate_grad, axis=-1, keepdims=True))
    logit_grad = jnp.sum(picked_grad[:, :, None] * choose, axis=1).astype(jnp.bfloat16)
    grad_router = jnp.dot(normed_second.T, logit_grad, preferred_element_type=jnp.float32)
    normed_grad = normed_grad + jnp.dot(
        logit_grad, router_half.T, preferred_element_type=jnp.float32
    )
    part_two, gain_grad_two = norm_backward(normed_grad, resid, inv_two, gain_two)
    resid_grad = upstream + part_two
    attn_grad = (res_scale * resid_grad).astype(jnp.bfloat16)
    grad_out = jnp.dot(back.T, attn_grad, preferred_element_type=jnp.float32)
    returned_gradient = jnp.dot(attn_grad, out_half.T, preferred_element_type=jnp.float32).astype(
        jnp.bfloat16
    )
    head_grad = lax.all_to_all(
        returned_gradient, "seq", split_axis=1, concat_axis=0, tiled=True
    ).reshape(seq_length, resident_heads, head_grouping, HEAD_SIZE)
    row_inner = jnp.sum(
        head_grad.astype(jnp.float32)
        * attended.reshape(seq_length, resident_heads, head_grouping, HEAD_SIZE).astype(
            jnp.float32
        ),
        axis=-1,
    )

    def grad_block(running, block_index):
        key_grad, value_grad = running
        row_start = block_index * block_rows
        query_block, scores = scores_for(block_index)
        grad_slice = lax.dynamic_slice_in_dim(head_grad, row_start, block_rows, 0)
        inner_slice = jnp.transpose(
            lax.dynamic_slice_in_dim(row_inner, row_start, block_rows, 0), (1, 2, 0)
        )
        weights = jnp.exp(scores - logsums[block_index][..., None])
        prob_grad = jnp.einsum(
            "qhgd,khd->hgqk", grad_slice, value_part, preferred_element_type=jnp.float32
        )
        score_grad = (weights * (prob_grad - inner_slice[..., None])).astype(jnp.bfloat16)
        query_grad = att_scale * jnp.einsum(
            "hgqk,khd->qhgd", score_grad, key_part, preferred_element_type=jnp.float32
        )
        key_grad = key_grad + att_scale * jnp.einsum(
            "hgqk,qhgd->khd", score_grad, query_block, preferred_element_type=jnp.float32
        )
        value_grad = value_grad + jnp.einsum(
            "hgqk,qhgd->khd",
            weights.astype(jnp.bfloat16),
            grad_slice,
            preferred_element_type=jnp.float32,
        )
        return ((key_grad, value_grad), query_grad.astype(jnp.bfloat16))

    zero_keys = jnp.zeros((seq_length, resident_heads, HEAD_SIZE), jnp.float32)
    (key_grad, value_grad), query_grads = lax.scan(
        grad_block, (zero_keys, zero_keys), jnp.arange(block_count)
    )
    query_grads = query_grads.reshape(seq_length, resident_heads * head_grouping * HEAD_SIZE)
    kv_grads = (
        jnp.stack([key_grad, value_grad], axis=2)
        .astype(jnp.bfloat16)
        .reshape(seq_length, resident_heads * 2 * HEAD_SIZE)
    )
    packed_grad = jnp.stack([query_grads, kv_grads], axis=1)
    token_gradient = lax.all_to_all(packed_grad, "seq", split_axis=0, concat_axis=2, tiled=True)
    query_tok = rotate_back(
        token_gradient[:, 0].astype(jnp.float32).reshape(token_row_list, QUERY_HEADS, HEAD_SIZE),
        cosine_table,
        sine_table,
    )
    key_value_token = (
        token_gradient[:, 1]
        .astype(jnp.float32)
        .reshape(token_row_list, KEY_VALUE_HEADS, 2, HEAD_SIZE)
    )
    key_token = rotate_back(key_value_token[:, :, 0], cosine_table, sine_table)
    key_value_token = jnp.stack([key_token, key_value_token[:, :, 1]], axis=2).reshape(
        token_row_list, KEY_VALUE_HEADS * 2 * HEAD_SIZE
    )
    projected_grad = jnp.concatenate(
        [query_tok.reshape(token_row_list, QUERY_HEADS * HEAD_SIZE), key_value_token], axis=1
    ).astype(jnp.bfloat16)
    grad_qkv = jnp.dot(normed_first.T, projected_grad, preferred_element_type=jnp.float32)
    normed_one_grad = jnp.dot(projected_grad, qkv_half.T, preferred_element_type=jnp.float32)
    part_one, gain_grad_one = norm_backward(normed_one_grad, source, inv_one, gain_one)
    tokens_grad = (resid_grad + part_one)[None]
    grad_gains = jnp.stack([gain_grad_one, gain_grad_two])
    shard_gains, shard_qkv, shard_out, shard_router, shard_up, shard_down = (
        lax.psum_scatter(
            grad_gains.astype(jnp.bfloat16), "fsdp", scatter_dimension=1, tiled=True
        ).astype(jnp.float32),
        lax.psum_scatter(
            grad_qkv.astype(jnp.bfloat16), "fsdp", scatter_dimension=0, tiled=True
        ).astype(jnp.float32),
        lax.psum_scatter(
            grad_out.astype(jnp.bfloat16), "fsdp", scatter_dimension=0, tiled=True
        ).astype(jnp.float32),
        lax.psum_scatter(
            grad_router.astype(jnp.bfloat16), "fsdp", scatter_dimension=0, tiled=True
        ).astype(jnp.float32),
        lax.psum_scatter(
            grad_up.astype(jnp.bfloat16), "fsdp", scatter_dimension=1, tiled=True
        ).astype(jnp.float32),
        lax.psum_scatter(
            grad_down.astype(jnp.bfloat16), "fsdp", scatter_dimension=1, tiled=True
        ).astype(jnp.float32),
    )
    shard_gains, shard_qkv, shard_out, shard_router = (
        lax.psum(shard_gains.astype(jnp.bfloat16), "seq").astype(jnp.float32),
        lax.psum(shard_qkv.astype(jnp.bfloat16), "seq").astype(jnp.float32),
        lax.psum(shard_out.astype(jnp.bfloat16), "seq").astype(jnp.float32),
        lax.psum(shard_router.astype(jnp.bfloat16), "seq").astype(jnp.float32),
    )
    fresh_gains, momentum_gains, variance_gains = adam_update(
        norm_gains, shard_gains, mean_gains, square_gains, learn_rates[0]
    )
    fresh_qkv, momentum_qkv, variance_qkv = adam_update(
        qkv_weight, shard_qkv, mean_qkv, square_qkv, learn_rates[1]
    )
    fresh_out, momentum_out, variance_out = adam_update(
        out_weight, shard_out, mean_out, square_out, learn_rates[2]
    )
    fresh_router, momentum_router, variance_router = adam_update(
        router_weight, shard_router, mean_router, square_router, learn_rates[3]
    )
    fresh_up, momentum_up, variance_up = adam_update(
        expert_up, shard_up, mean_up, square_up, learn_rates[4]
    )
    fresh_down, momentum_down, variance_down = adam_update(
        expert_down, shard_down, mean_down, square_down, learn_rates[5]
    )
    return (
        output,
        tokens_grad,
        shard_gains,
        shard_qkv,
        shard_out,
        shard_router,
        shard_up,
        shard_down,
        fresh_gains,
        fresh_qkv,
        fresh_out,
        fresh_router,
        fresh_up,
        fresh_down,
        momentum_gains,
        momentum_qkv,
        momentum_out,
        momentum_router,
        momentum_up,
        momentum_down,
        variance_gains,
        variance_qkv,
        variance_out,
        variance_router,
        variance_up,
        variance_down,
    )


def solution(mesh):
    return jax.shard_map(
        shards,
        mesh=mesh,
        in_specs=(
            P("fsdp", "seq", None),
            P("fsdp", "seq", None),
            P("fsdp", "seq", None),
            P(None, "fsdp"),
            P("fsdp", None),
            P("fsdp", None),
            P("fsdp", None),
            P("seq", "fsdp", None),
            P("seq", "fsdp", None),
            P(None, "fsdp"),
            P(None, "fsdp"),
            P("fsdp", None),
            P("fsdp", None),
            P("fsdp", None),
            P("fsdp", None),
            P("fsdp", None),
            P("fsdp", None),
            P("seq", "fsdp", None),
            P("seq", "fsdp", None),
            P("seq", "fsdp", None),
            P("seq", "fsdp", None),
        ),
        out_specs=(
            P("fsdp", "seq", None),
            P("fsdp", "seq", None),
            P(None, "fsdp"),
            P("fsdp", None),
            P("fsdp", None),
            P("fsdp", None),
            P("seq", "fsdp", None),
            P("seq", "fsdp", None),
            P(None, "fsdp"),
            P("fsdp", None),
            P("fsdp", None),
            P("fsdp", None),
            P("seq", "fsdp", None),
            P("seq", "fsdp", None),
            P(None, "fsdp"),
            P("fsdp", None),
            P("fsdp", None),
            P("fsdp", None),
            P("seq", "fsdp", None),
            P("seq", "fsdp", None),
            P(None, "fsdp"),
            P("fsdp", None),
            P("fsdp", None),
            P("fsdp", None),
            P("seq", "fsdp", None),
            P("seq", "fsdp", None),
        ),
        check_vma=False,
    )
```

profile of v0, /device:TPU:12, one launch (start us, length us, event | category | flops | bytes accessed | tf_op | source)
XLA Modules:
  0.0 1337.5 jit_solution(8923424942856656237)
XLA Ops:
  25.8 22.4 %all-gather.5.cloned.1.call-done = bf16[1024,2048]{1,0:T(8,128)(2,1)} async-done(((bf16[128,2048]{1,0:T(8,128)(2,1)}), bf16[1024,2048]{1,0:T(8,128)(2,1)}) %all-gather.5.cloned.1.call-update) | async-done | bytes 4194320 | tf_op jit(solution)/shard_map/all_gather | solution.py:135
  82.9 12.4 all-to-all-done
  96.5 15.9 %while.28 = (s32[]{:T(128)}, bf16[2,512,2,2,64]{1,4,3,2,0:T(8,128)(2,1)S(1)}, f32[2,2,2,512]{3,2,1,0:T(2,128)S(1)}, s32[2]{0:T(128)S(1)}, bf16[1024,2,2,64]{0,3,...) while((s32[]{:T(128)}, ...), condition=%wide.region_4.5_spmd.clone, body=%wide.region_1.4_spmd.clone.sunk | while | flops 560593408 | bytes 28381376 | solution.py:177
  135.6 14.0 %gather_fusion = bf16[3072,1024]{1,0:T(8,128)(2,1)} fusion(bf16[257,1024]{1,0:T(8,128)(2,1)S(1)} %concatenate.60, s32[3072]{0:T(1024)S(1)} %get-tuple-element.319), kind=kCustom, calls=%fused_computation | custom fusion | bytes 12595200 | tf_op jit(solution)/shard_map/gather | solution.py:193
  173.2 18.7 %gather_fusion.2 = bf16[3072,1024]{1,0:T(8,128)(2,1)} fusion(bf16[2049,1024]{1,0:T(8,128)(2,1)} %concatenate.61, s32[3072]{0:T(1024)S(1)} %get-tuple-element.318), kind=kCustom, calls=%fused_computation.2 | custom fusion | bytes 12595200 | tf_op jit(solution)/shard_map/gather | solution.py:221
  191.9 100.5 %all-to-all-done.2 = bf16[32,96,1024]{2,1,0:T(8,128)(2,1)} async-done(((bf16[32,96,1024]{2,1,0:T(8,128)(2,1)}), bf16[32,96,1024]{2,1,0:T(8,128)(2,1)}, u32[]{:S(2)}, u32[]{:S(2)}) %all-to-all-start.2) | async-done | bytes 6291488 | tf_op jit(solution)/shard_map/all_to_all | solution.py:194
  307.5 127.7 %all-to-all-done.4 = bf16[32,96,1024]{2,1,0:T(8,128)(2,1)} async-done(((bf16[32,96,1024]{2,1,0:T(8,128)(2,1)}), bf16[32,96,1024]{2,1,0:T(8,128)(2,1)}, u32[]{:S(2)}, u32[]{:S(2)}) %all-to-all-start.4) | async-done | bytes 6291488 | tf_op jit(solution)/shard_map/all_to_all | solution.py:222
  441.8 16.2 %fusion.130 = f32[8,384,1024]{2,1,0:T(8,128)} fusion(bf16[8,384,1024]{2,1,0:T(8,128)(2,1)} %bitcast.346, bf16[8,1024,1024]{2,1,0:T(8,128)(2,1)} %all-gather.9.cloned.1.call-done), kind=kOutput, calls=%fused_computation.241 | convolution fusion | flops 6442450944 | bytes 35651584 | tf_op jit(solution)/shard_map/ecd,edf->ecf/dot_general | solution.py:195
  458.0 13.9 %multiply_convert_fusion.1 = (bf16[8,384,512]{2,1,0:T(8,128)(2,1)}, bf16[8,384,512]{2,1,0:T(8,128)(2,1)}, bf16[8,384,512]{2,1,0:T(8,128)(2,1)}) fusion(f32[8,384,1024]{2,1,0:T(8,128)} %fusion.130, bf16[8,384,1024]{2,1,0:T(8,128)(2,1)} %bitcast.339, bf16[8,512,1024]{2,1,0:T(8,128)(2,1)} %all-gather.11.cloned.1.call-done), kind=kOutput, calls=%fused_computation.79 | convolution fusion | flops 3244818432 | bytes 36700160 | tf_op jit(solution)/shard_map/ecd,efd->ecf/dot_general | solution.py:223
  472.0 13.1 fusion.66
  516.6 120.4 %all-to-all-done.5 = bf16[8,384,1024]{2,0,1:T(8,128)(2,1)} async-done(((bf16[8,384,1024]{2,0,1:T(8,128)(2,1)}), bf16[8,384,1024]{2,0,1:T(8,128)(2,1)}, u32[]{:S(2)}, u32[]{:S(2)}) %all-to-all-start.5) | async-done | bytes 6291488 | tf_op jit(solution)/shard_map/all_to_all | solution.py:235
  655.0 14.5 %gather_fusion.3 = bf16[2048,1024]{1,0:T(8,128)(2,1)} fusion(bf16[3072,1024]{1,0:T(8,128)(2,1)} %bitcast.338, s32[2048]{0:T(1024)S(1)} %broadcast_clamp_fusion), kind=kCustom, calls=%fused_computation.3 | custom fusion | bytes 8396800 | tf_op jit(solution)/shard_map/gather | solution.py:237
  674.9 105.3 %all-to-all-done.3 = bf16[8,384,1024]{2,0,1:T(8,128)(2,1)} async-done(((bf16[8,384,1024]{2,0,1:T(8,128)(2,1)}), bf16[8,384,1024]{2,0,1:T(8,128)(2,1)}, u32[]{:S(2)}, u32[]{:S(2)}) %all-to-all-start.3) | async-done | bytes 6291488 | tf_op jit(solution)/shard_map/all_to_all | solution.py:204
  789.2 14.5 %gather_fusion.1 = bf16[2048,1024]{1,0:T(8,128)(2,1)} fusion(bf16[3072,1024]{1,0:T(8,128)(2,1)} %bitcast.337, s32[2048]{0:T(1024)S(1)} %broadcast_clamp_fusion), kind=kCustom, calls=%fused_computation.1 | custom fusion | bytes 8396800 | tf_op jit(solution)/shard_map/gather | solution.py:206
  839.7 50.3 %while.29 = (s32[]{:T(128)}, f32[1024,2,64]{0,2,1:T(8,128)S(1)}, f32[1024,2,64]{0,2,1:T(8,128)}, bf16[2,512,2,2,64]{1,4,3,2,0:T(8,128)(2,1)}, s32[2]{0:T(128)S(1...) while((s32[]{:T(128)}, f32[1024,2,64]{0,2,1:T(8,128)S(1)}, ...), condition=%wide.region_21.22_spmd.clone, body=%wide.region_20.21_spmd.clone.sunk | while | flops 1364591104 | bytes 70840768 | solution.py:294
  906.0 19.8 %all-to-all-done.7 = bf16[1024,2,256]{2,1,0:T(2,128)(2,1)S(1)} async-done(((bf16[1024,2,256]{2,1,0:T(2,128)(2,1)}), bf16[1024,2,256]{2,1,0:T(2,128)(2,1)S(1)}, u32[]{:S(2)}, u32[]{:S(2)}) %all-to-all-start.7) | async-done | bytes 1048608 | tf_op jit(solution)/shard_map/all_to_all | solution.py:304
  940.6 11.6 convolution_convert_fusion.1
  952.3 53.0 %reduce-scatter.11.cloned.1.call-done = bf16[128,2048]{1,0:T(8,128)(2,1)} async-done(((bf16[1024,2048]{1,0:T(8,128)(2,1)}), bf16[128,2048]{1,0:T(8,128)(2,1)}) %reduce-scatter.11.cloned.1.call-update) | async-done | bytes 524304 | tf_op jit(solution)/shard_map/reduce_scatter | solution.py:331
  1005.4 16.4 %convolution_convert_fusion = bf16[8,1024,1024]{2,1,0:T(8,128)(2,1)} fusion(bf16[8,384,1024]{2,1,0:T(8,128)(2,1)} %bitcast.347, bf16[8,384,512]{2,1,0:T(8,128)(2,1)} %get-tuple-element.296, bf16[8,384,512]{2,1,0:T(8,128)(2,1)} %get-tuple-element.295), kind=kOutput, calls=%fused_computation.69 | convolution fusion | flops 6463422464 | bytes 29360128 | tf_op jit(solution)/shard_map/ecd,ecf->edf/dot_general | solution.py:231
  1021.9 20.7 %reduce-scatter.21.cloned.1.call-done = bf16[128,32]{1,0:T(8,128)(2,1)} async-done(((bf16[1024,32]{1,0:T(8,128)(2,1)}), bf16[128,32]{1,0:T(8,128)(2,1)}) %reduce-scatter.21.cloned.1.call-update) | async-done | bytes 8208
  1044.7 35.4 %reduce-scatter.19.cloned.1.call-done = bf16[128,2]{1,0:T(8,128)(2,1)} async-done(((bf16[1024,2]{1,0:T(8,128)(2,1)}), bf16[128,2]{1,0:T(8,128)(2,1)}) %reduce-scatter.19.cloned.1.call-update) | async-done | bytes 528
  1091.3 63.4 %reduce-scatter.17.cloned.1.call-done = bf16[8,64,1024]{2,1,0:T(8,128)(2,1)} async-done(((bf16[8,512,1024]{2,1,0:T(8,128)(2,1)}), bf16[8,64,1024]{2,1,0:T(8,128)(2,1)}) %reduce-scatter.17.cloned.1.call-update) | async-done | bytes 1048592 | tf_op jit(solution)/shard_map/reduce_scatter | solution.py:343
  1162.0 39.1 %all-reduce.6.cloned.1.call-done = (bf16[128,2048]{1,0:T(8,128)(2,1)}, bf16[128,1024]{1,0:T(8,128)(2,1)}) async-done(((bf16[128,2048]{1,0:T(8,128)(2,1)}, bf16[128,1024]{1,0:T(8,128)(2,1)}), (bf16[128,2048]{1,0:T(8,128)(2,1)}, bf16[128,1024]{1,0:T(8,128)(2,1)})) %all-reduce.6.cloned.1.call-update) | async-done | bytes 786448 | tf_op jit(solution)/shard_map/psum | solution.py:349
  1206.0 114.4 %reduce-scatter.15.cloned.1.call-done = bf16[8,128,1024]{2,1,0:T(8,128)(2,1)} async-done(((bf16[8,1024,1024]{2,1,0:T(8,128)(2,1)}), bf16[8,128,1024]{2,1,0:T(8,128)(2,1)}) %reduce-scatter.15.cloned.1.call-update) | async-done | bytes 2097168 | tf_op jit(solution)/shard_map/reduce_scatter | solution.py:340
  (323 shorter events, 347.7 us)
Async XLA Ops:
  7.2 41.0 %all-gather.5.cloned.1.call-start = ((), (), s32[]{:S(2)}) async-start(), calls=%async_computation.14 | async-start | bytes 4718592 | tf_op jit(solution)/shard_map/all_gather | solution.py:135
  9.4 120.8 %all-gather.7.cloned.1.call-start = ((), (), s32[]{:S(2)}) async-start(), calls=%async_computation.15 | async-start | bytes 2359296 | tf_op jit(solution)/shard_map/all_gather | solution.py:136
  11.2 430.6 %all-gather.9.cloned.1.call-start = ((), (), s32[]{:S(2)}) async-start(), calls=%async_computation.16 | async-start | bytes 18874368 | tf_op jit(solution)/shard_map/all_gather | solution.py:138
  67.3 28.0 %all-to-all-start = ((bf16[256,2,1024]{0,1,2:T(2,128)(2,1)}), bf16[256,2,1024]{0,1,2:T(2,128)(2,1)S(1)}, u32[]{:S(2)}, u32[]{:S(2)}) async-start(bf16[256,2,1024]{0,1,2:T(2,128)(2,1)} %copy.255), calls=%async_computation | async-start | bytes 2097152 | tf_op jit(solution)/shard_map/all_to_all | solution.py:150
  114.8 17.9 %all-to-all-start.1 = ((bf16[4,256,256]{1,2,0:T(8,128)(2,1)}), bf16[4,256,256]{1,2,0:T(8,128)(2,1)S(1)}, u32[]{:S(2)}, u32[]{:S(2)}) async-start(bf16[4,256,256]{1,2,0:T(8,128)(2,1)} %copy.261), calls=%async_computation.1 | async-start | bytes 1048576 | tf_op jit(solution)/shard_map/all_to_all | solution.py:179
  149.6 142.8 %all-to-all-start.2 = ((bf16[32,96,1024]{2,1,0:T(8,128)(2,1)}), bf16[32,96,1024]{2,1,0:T(8,128)(2,1)}, u32[]{:S(2)}, u32[]{:S(2)}) async-start(bf16[32,96,1024]{2,1,0:T(8,128)(2,1)} %bitcast.341), calls=%async_computation.2 | async-start | bytes 12582912 | tf_op jit(solution)/shard_map/all_to_all | solution.py:194
  158.1 300.0 %all-gather.11.cloned.1.call-start = ((), (), s32[]{:S(2)}) async-start(), calls=%async_computation.17 | async-start | bytes 9437184 | tf_op jit(solution)/shard_map/all_gather | solution.py:139
  292.4 142.9 %all-to-all-start.4 = ((bf16[32,96,1024]{2,1,0:T(8,128)(2,1)}), bf16[32,96,1024]{2,1,0:T(8,128)(2,1)}, u32[]{:S(2)}, u32[]{:S(2)}) async-start(bf16[32,96,1024]{2,1,0:T(8,128)(2,1)} %bitcast.342), calls=%async_computation.4 | async-start | bytes 12582912 | tf_op jit(solution)/shard_map/all_to_all | solution.py:222
  494.1 142.9 %all-to-all-start.5 = ((bf16[8,384,1024]{2,0,1:T(8,128)(2,1)}), bf16[8,384,1024]{2,0,1:T(8,128)(2,1)}, u32[]{:S(2)}, u32[]{:S(2)}) async-start(bf16[8,384,1024]{2,0,1:T(8,128)(2,1)} %copy.273), calls=%async_computation.5 | async-start | bytes 12582912 | tf_op jit(solution)/shard_map/all_to_all | solution.py:235
  637.0 143.3 %all-to-all-start.3 = ((bf16[8,384,1024]{2,0,1:T(8,128)(2,1)}), bf16[8,384,1024]{2,0,1:T(8,128)(2,1)}, u32[]{:S(2)}, u32[]{:S(2)}) async-start(bf16[8,384,1024]{2,0,1:T(8,128)(2,1)} %copy.269), calls=%async_computation.3 | async-start | bytes 12582912 | tf_op jit(solution)/shard_map/all_to_all | solution.py:204
  815.0 18.4 %all-to-all-start.6 = ((bf16[256,4,256]{2,0,1:T(8,128)(2,1)}), bf16[256,4,256]{2,0,1:T(8,128)(2,1)}, u32[]{:S(2)}, u32[]{:S(2)}) async-start(bf16[256,4,256]{2,0,1:T(8,128)(2,1)} %bitcast.289), calls=%async_computation.6 | async-start | bytes 1048576 | tf_op jit(solution)/shard_map/all_to_all | solution.py:255
  897.2 28.6 %all-to-all-start.7 = ((bf16[1024,2,256]{2,1,0:T(2,128)(2,1)}), bf16[1024,2,256]{2,1,0:T(2,128)(2,1)S(1)}, u32[]{:S(2)}, u32[]{:S(2)}) async-start(bf16[1024,2,256]{2,1,0:T(2,128)(2,1)} %copy.281), calls=%async_computation.7 | async-start | bytes 2097152 | tf_op jit(solution)/shard_map/all_to_all | solution.py:304
  903.8 48.4 %reduce-scatter.13.cloned.1.call-start = ((), (), s32[]{:S(2)}) async-start(), calls=%async_computation.19 | async-start | bytes 2359296 | tf_op jit(solution)/shard_map/reduce_scatter | solution.py:334
  905.9 99.4 %reduce-scatter.11.cloned.1.call-start = ((), (), s32[]{:S(2)}) async-start(), calls=%async_computation.18 | async-start | bytes 4718592 | tf_op jit(solution)/shard_map/reduce_scatter | solution.py:331
  933.8 108.8 %reduce-scatter.21.cloned.1.call-start = ((), (), s32[]{:S(2)}) async-start(), calls=%async_computation.23 | async-start | bytes 294912
  934.9 145.1 %reduce-scatter.19.cloned.1.call-start = ((), (), s32[]{:S(2)}) async-start(), calls=%async_computation.22 | async-start | bytes 294912
  940.6 214.2 %reduce-scatter.17.cloned.1.call-start = ((), (), s32[]{:S(2)}) async-start(), calls=%async_computation.21 | async-start | bytes 9437184 | tf_op jit(solution)/shard_map/reduce_scatter | solution.py:343
  952.2 248.8 %all-reduce.6.cloned.1.call-start = ((), (), s32[]{:S(2)}) async-start(), calls=%async_computation.24 | async-start | bytes 1572864 | tf_op jit(solution)/shard_map/psum | solution.py:349
  1005.3 315.1 %reduce-scatter.15.cloned.1.call-start = ((), (), s32[]{:S(2)}) async-start(), calls=%async_computation.20 | async-start | bytes 18874368 | tf_op jit(solution)/shard_map/reduce_scatter | solution.py:340
  1021.8 68.9 %copy-start.40 = (f32[128,32]{0,1:T(8,128)S(1)}, f32[128,32]{0,1:T(8,128)}, u32[]{:S(2)}) copy-start(f32[128,32]{0,1:T(8,128)} %param.31) | copy-start | bytes 49156
  1021.8 68.9 %copy-start.41 = (f32[128,32]{0,1:T(8,128)S(1)}, f32[128,32]{0,1:T(8,128)}, u32[]{:S(2)}) copy-start(f32[128,32]{0,1:T(8,128)} %param.40) | copy-start | bytes 49156
  1021.8 68.9 %copy-start.42 = (f32[128,32]{0,1:T(8,128)S(1)}, f32[128,32]{0,1:T(8,128)}, u32[]{:S(2)}) copy-start(f32[128,32]{0,1:T(8,128)} %param.41) | copy-start | bytes 49156
  1091.3 109.7 %copy-start.15 = (f32[128,1024]{1,0:T(8,128)S(1)}, f32[128,1024]{1,0:T(8,128)}, u32[]{:S(2)}) copy-start(f32[128,1024]{1,0:T(8,128)} %param.30) | copy-start | bytes 1572868
  1091.3 109.7 %copy-start.29 = (f32[128,1024]{1,0:T(8,128)S(1)}, f32[128,1024]{1,0:T(8,128)}, u32[]{:S(2)}) copy-start(f32[128,1024]{1,0:T(8,128)} %param.38) | copy-start | bytes 1572868
  (50 other events, 802.1 us)
Sparse Core Ops, SparseCore 0:
  10.5 37.6 all-gather.4
  50.7 27.9 all-gather.6
  81.2 89.4 all-gather.8
  173.0 54.7 all-gather.10
  908.2 41.5 reduce-scatter.12
  954.0 51.2 reduce-scatter.10
  1008.9 33.6 reduce-scatter.20
  1046.5 33.5 reduce-scatter.18
  1083.6 71.1 reduce-scatter.16
  1157.2 43.7 all-reduce.5
  1205.0 115.3 reduce-scatter.14
where the time goes:
time: 1350 us; the launch traced here: 1340 us
  waiting for transfers between devices  848 us (63%)
  local copies, waits for them, and re-layouts  157 us (12%)
  matrix products  146 us (11%)
  other arithmetic  76.8 us (6%)
  starting transfers between devices  61.4 us (5%)
  blocking collectives  26.2 us (2%)
  between operations  15.3 us (1%)
    all_to_all x1, waiting for transfers between devices, shards(): lax.all_to_all(outgoing, 'seq', split_axis=0, concat_axis=1, tiled=True)  128 us
    all_to_all x1, waiting for transfers between devices, shards(): lax.all_to_all(input_slots, 'seq', split_axis=1, concat_axis=0, tiled=True)  120 us
    reduce_scatter x1, waiting for transfers between devices, shards(): lax.psum_scatter(grad_up.astype(jnp.bfloat16), 'fsdp', scatter_dimension=...  114 us
    all_to_all x1, waiting for transfers between devices, shards(): lax.all_to_all(produced, 'seq', split_axis=1, concat_axis=0, tiled=True)  105 us
    all_to_all x1, waiting for transfers between devices, shards(): lax.all_to_all(dispatch, 'seq', split_axis=0, concat_axis=1, tiled=True)  101 us
    reduce_scatter x1, waiting for transfers between devices, shards(): lax.psum_scatter(grad_down.astype(jnp.bfloat16), 'fsdp', scatter_dimensio...  63.4 us
    unnamed x13, waiting for transfers between devices  56.3 us
    reduce_scatter x1, waiting for transfers between devices, shards(): lax.psum_scatter(grad_qkv.astype(jnp.bfloat16), 'fsdp', scatter_dimension...  53 us
  transfers between devices with their start and end apart: 19, of which 15 were waited for; matrix products, arithmetic and copies ran while one was open for 18% of the time, Pallas kernels for 0%

commit v1 on v0

v1 whole, which is shorter than its diff:
```python
import functools

import jax
import jax.numpy as jnp
from jax import lax
from jax.experimental import pallas as pl
from jax.experimental.pallas import tpu as pltpu
from jax.sharding import PartitionSpec as P

MODEL_WIDTH = 1024
QUERY_HEADS = 16
KEY_VALUE_HEADS = 8
HEAD_SIZE = 64
EXPERTS = 32
FF = 512
TOP = 8
STEP = 3
CAP = 96
LANES = 128
TILE = 256
CHUNKS = 2

epsilon = 1e-06
res_scale = 0.22
att_scale = 0.015625
beta_one = 0.9
beta_two = 0.95
adam_eps = 1e-08
weight_decay = 0.1
learn_rates = (0.4, 0.04, 0.2, 0.01, 0.01, 0.05)

bf16 = jnp.bfloat16
f32 = jnp.float32
WIDE = MODEL_WIDTH + LANES


def adam_update(weight, gradient, first, second, rate):
    first_new = beta_one * first + (1.0 - beta_one) * gradient
    second_new = beta_two * second + (1.0 - beta_two) * gradient * gradient
    first_hat = first_new / (1.0 - beta_one**STEP)
    second_hat = second_new / (1.0 - beta_two**STEP)
    fresh = weight - rate * (first_hat / (jnp.sqrt(second_hat) + adam_eps) + weight_decay * weight)
    return (fresh, first_new, second_new)


def dot_nn(a, b):
    return lax.dot_general(a, b, (((1,), (0,)), ((), ())), preferred_element_type=f32)


def dot_nt(a, b):
    return lax.dot_general(a, b, (((1,), (1,)), ((), ())), preferred_element_type=f32)


def dot_tn(a, b):
    return lax.dot_general(a, b, (((0,), (0,)), ((), ())), preferred_element_type=f32)


def lanes_of(shape):
    return lax.broadcasted_iota(jnp.int32, shape, len(shape) - 1)


def aligned(index, size):
    return pl.ds(pl.multiple_of(index, size), size)


def kernel_call(body, outs, ins, scalars, scratch=(), grid=None, in_specs=None, out_specs=None, flops=0, limit=48):
    in_specs = in_specs or [pl.BlockSpec(memory_space=pltpu.VMEM)] * len(ins)
    out_specs = out_specs or [pl.BlockSpec(memory_space=pltpu.VMEM)] * len(outs)
    moved = sum(a.size * a.dtype.itemsize for a in list(ins) + list(outs))
    return pl.pallas_call(
        body,
        out_shape=outs,
        grid_spec=pltpu.PrefetchScalarGridSpec(
            num_scalar_prefetch=1,
            grid=grid or (1,),
            in_specs=in_specs,
            out_specs=out_specs,
            scratch_shapes=list(scratch),
        ),
        compiler_params=pltpu.CompilerParams(vmem_limit_bytes=limit * 1024 * 1024),
        cost_estimate=pl.CostEstimate(flops=flops, bytes_accessed=moved, transcendentals=0),
    )(scalars, *ins)


def shape_of(shape, kind=bf16):
    return jax.ShapeDtypeStruct(shape, kind)


def xor_permute(value, axis, mask):
    return lax.ppermute(value, axis, [(i, i ^ mask) for i in range(lax.axis_size(axis))])


def shift_permute(value, axis, step):
    size = lax.axis_size(axis)
    return lax.ppermute(value, axis, [(i, (i + step) % size) for i in range(size)])


def gather_shards(value):
    count = lax.axis_size("fsdp")
    if count != 8:
        whole = lax.all_gather(value, "fsdp", axis=0)
        order = lax.axis_index("fsdp") ^ jnp.arange(count)
        whole = jnp.take(whole, order, axis=0)
        return [(r, 0, whole[r]) for r in range(count)]
    half = value.shape[-2] // 2
    over_x = xor_permute(value, "fsdp", 2)
    over_y = xor_permute(value, "fsdp", 4)
    far_a = xor_permute(over_x[..., :half, :], "fsdp", 4)
    far_b = xor_permute(over_y[..., half:, :], "fsdp", 2)
    pieces = [(0, 0, value), (2, 0, over_x), (4, 0, over_y), (6, 0, far_a), (6, half, far_b)]
    return pieces + [(r + 1, row, xor_permute(a, "fsdp", 1)) for r, row, a in pieces]


def scatter_sets(send, keep):
    count = lax.axis_size("fsdp")
    rows = keep.shape[-2]
    half = rows // 2
    if count != 8:
        both = jnp.stack([keep, send], axis=1).reshape((count,) + keep.shape[1:])
        both = jnp.take(both, lax.axis_index("fsdp") ^ jnp.arange(count), axis=0)
        total = lax.psum_scatter(both, "fsdp", scatter_dimension=0).astype(f32)
        return (total[..., :half, :], total[..., half:, :])
    got = xor_permute(send, "fsdp", 1)

    def pair(i, part):
        piece = slice(0, half) if part == 0 else slice(half, rows)
        return keep[i, ..., piece, :].astype(f32) + got[i, ..., piece, :].astype(f32)

    over_x = xor_permute(jnp.stack([pair(3, 0), pair(1, 0)]).astype(bf16), "fsdp", 2)
    over_y = xor_permute(jnp.stack([pair(3, 1), pair(2, 1)]).astype(bf16), "fsdp", 4)
    then_x = xor_permute((pair(1, 1) + over_y[0].astype(f32)).astype(bf16), "fsdp", 2)
    then_y = xor_permute((pair(2, 0) + over_x[0].astype(f32)).astype(bf16), "fsdp", 4)
    first = pair(0, 0) + over_x[1].astype(f32) + then_y.astype(f32)
    second = pair(0, 1) + over_y[1].astype(f32) + then_x.astype(f32)
    return (first, second)


def ring_gather(block):
    count = lax.axis_size("seq")
    if count != 4:
        whole = lax.all_gather(block, "seq", axis=0)
        whole = jnp.take(whole, (lax.axis_index("seq") - jnp.arange(count)) % count, axis=0)
        return [(k, 0, whole[k]) for k in range(count)]
    half = block.shape[0] // 2
    below = shift_permute(block, "seq", 1)
    above = shift_permute(block, "seq", -1)
    far_a = shift_permute(below[:half], "seq", 1)
    far_b = shift_permute(above[half:], "seq", -1)
    return [(0, 0, block), (1, 0, below), (3, 0, above), (2, 0, far_a), (2, half, far_b)]


def ring_shapes(count, rows, columns):
    if count != 4:
        return [shape_of((count, rows, columns))]
    half = rows // 2
    return [shape_of((r, columns)) for r in (rows, rows, rows, half, half)]


def ring_put(count, refs, k, rows, value):
    half = rows // 2
    width = value.shape[1]
    value = value.astype(bf16)
    if count != 4:
        refs[0][k, :, :width] = value
        return
    own, down, up, keep_down, keep_up = refs
    places = {
        0: ((own, 0), (own, half)),
        1: ((keep_down, 0), (down, half)),
        2: ((down, 0), (up, 0)),
        3: ((up, half), (keep_up, 0)),
    }
    for part, (ref, row) in enumerate(places[k]):
        ref[row : row + half, :width] = value[part * half : (part + 1) * half]


def ring_put_tail(count, refs, k, rows, value):
    half = rows // 2
    value = value.astype(bf16)
    if count != 4:
        refs[0][k, :, MODEL_WIDTH:] = value
        return
    own, down, up, keep_down, keep_up = refs
    places = {
        0: ((own, 0), (own, half)),
        1: ((keep_down, 0), (down, half)),
        2: ((down, 0), (up, 0)),
        3: ((up, half), (keep_up, 0)),
    }
    for part, (ref, row) in enumerate(places[k]):
        ref[row : row + half, MODEL_WIDTH:] = value[part * half : (part + 1) * half]


def ring_reduce(arrays):
    count = lax.axis_size("seq")
    if count != 4:
        whole = jnp.take(arrays[0], (lax.axis_index("seq") - jnp.arange(count)) % count, axis=0)
        return [lax.psum_scatter(whole, "seq", scatter_dimension=0)]
    own, down, up, keep_down, keep_up = arrays
    half = keep_down.shape[0]
    from_above = shift_permute(down, "seq", -1)
    from_below = shift_permute(up, "seq", 1)
    then_down = (keep_down.astype(f32) + from_above[:half].astype(f32)).astype(bf16)
    then_up = (keep_up.astype(f32) + from_below[:half].astype(f32)).astype(bf16)
    last_above = shift_permute(then_down, "seq", -1)
    last_below = shift_permute(then_up, "seq", 1)
    return [own, from_above, from_below, last_above, last_below]


def ring_total(refs):
    if len(refs) == 1:
        return refs[0][...].astype(f32)
    own, above, below, last_above, last_below = [r[...].astype(f32) for r in refs]
    half = own.shape[0] // 2
    first = own[:half] + below[half:] + last_above
    second = own[half:] + above[half:] + last_below
    return jnp.concatenate([first, second], axis=0)


def block_value(pieces, refs, k):
    found = sorted((row, ref) for (kk, row, _), ref in zip(pieces, refs) if kk == k)
    if len(found) == 1:
        return found[0][1][...]
    return jnp.concatenate([ref[...] for _, ref in found], axis=0)


def block_lanes(pieces, refs, k, lanes):
    found = [(row, ref) for (kk, row, _), ref in zip(pieces, refs) if kk == k]
    found.sort(key=lambda entry: entry[0])
    if len(found) == 1:
        return found[0][1][:, lanes]
    return jnp.concatenate([ref[:, lanes] for _, ref in found], axis=0)


def rotate_tile(tile, cosine, sine):
    first = lanes_of(tile.shape) % HEAD_SIZE < HEAD_SIZE // 2
    turned = jnp.where(first, pltpu.roll(tile, LANES - HEAD_SIZE // 2, 1), pltpu.roll(tile, HEAD_SIZE // 2, 1))
    return tile * cosine + turned * sine


def rotate_tile_back(tile, cosine, sine):
    return rotate_tile(tile, cosine, -sine)


def qkv_body(pieces, meta, x_ref, cos_ref, sin_ref, *refs):
    shards = refs[: len(pieces)]
    wq_ref, wkv_ref, wo_ref, extra_ref, normed_ref, q_ref, kv_ref, columns = refs[len(pieces) :]
    shard_rows = MODEL_WIDTH // max(r + 1 for r, _, _ in pieces)
    for (r, row, value), ref in zip(pieces, shards):
        rows = value.shape[0]
        place = pl.ds(pl.multiple_of(meta[r] * shard_rows + row, rows), rows)
        wq_ref[place, :] = ref[:, :MODEL_WIDTH]
        wkv_ref[place, :] = ref[:, MODEL_WIDTH : 2 * MODEL_WIDTH]
        wo_ref[place, :] = ref[:, 2 * MODEL_WIDTH : 3 * MODEL_WIDTH]
        columns[place, :] = ref[:, 3 * MODEL_WIDTH :].astype(f32)
    extra_ref[...] = columns[...].T
    source = x_ref[...].astype(f32)
    scale_inv = lax.rsqrt(jnp.mean(source * source, axis=-1, keepdims=True) + epsilon)
    normed = (source * scale_inv * extra_ref[EXPERTS : EXPERTS + 1, :]).astype(bf16)
    normed_ref[...] = normed
    cosine, sine = cos_ref[...], sin_ref[...]
    low = lanes_of(cosine.shape) < HEAD_SIZE
    for j in range(MODEL_WIDTH // TILE):
        block = dot_nn(normed, wq_ref[:, j * TILE : (j + 1) * TILE])
        for i in range(TILE // LANES):
            at = j * TILE + i * LANES
            tile = block[:, i * LANES : (i + 1) * LANES]
            q_ref[:, at : at + LANES] = rotate_tile(tile, cosine, sine).astype(bf16)
    for j in range(MODEL_WIDTH // TILE):
        block = dot_nn(normed, wkv_ref[:, j * TILE : (j + 1) * TILE])
        for i in range(TILE // LANES):
            at = j * TILE + i * LANES
            tile = block[:, i * LANES : (i + 1) * LANES]
            kv_ref[:, at : at + LANES] = jnp.where(low, rotate_tile(tile, cosine, sine), tile).astype(bf16)


def causal_scores(pair, keys, k):
    scores = dot_nt(pair, keys)
    if k == 0:
        rows = keys.shape[0]
        place = lax.broadcasted_iota(jnp.int32, scores.shape, 0) % rows
        scores = jnp.where(place >= lanes_of(scores.shape), scores, -jnp.inf)
    return scores


def query_pair(tile):
    low = lanes_of(tile.shape) < HEAD_SIZE
    tile = tile.astype(f32) * att_scale
    even = jnp.where(low, tile, 0.0)
    odd = jnp.where(low, pltpu.roll(tile, HEAD_SIZE, 1), 0.0)
    return jnp.concatenate([even, odd], axis=0).astype(bf16)


def attend_body(count, pieces, meta, q_ref, x_ref, wo_ref, extra_ref, *refs):
    blocks = refs[: len(pieces)]
    a_ref, lse_ref, h_ref, normed_ref = refs[len(pieces) :]
    rows = q_ref.shape[0]
    place = meta[0]

    def variant(seen):
        def group(g, carry):
            lanes = aligned(g * LANES, LANES)
            pair = query_pair(q_ref[:, lanes])
            keys = [block_lanes(pieces, blocks, k, lanes) for k in range(seen)]
            scores = [causal_scores(pair, keys[k], k) for k in range(seen)]
            top = functools.reduce(jnp.maximum, [jnp.max(s, axis=-1, keepdims=True) for s in scores])
            weights = [jnp.exp(s - top) for s in scores]
            total = functools.reduce(jnp.add, [jnp.sum(w, axis=-1, keepdims=True) for w in weights])
            summed = functools.reduce(jnp.add, [dot_nn(w.astype(bf16), t) for w, t in zip(weights, keys)])
            summed = summed * (1.0 / total)
            logsum = top + jnp.log(total)
            low = lanes_of((rows, LANES)) < HEAD_SIZE
            a_ref[:, lanes] = jnp.where(low, pltpu.roll(summed[:rows], HEAD_SIZE, 1), summed[rows:]).astype(bf16)
            lse_ref[:, lanes] = jnp.where(low, logsum[:rows], logsum[rows:])
            return carry

        lax.fori_loop(0, KEY_VALUE_HEADS, group, 0)

    for seen in range(1, count + 1):
        pl.when(place == seen - 1)(functools.partial(variant, seen))
    resid = x_ref[...].astype(f32) + res_scale * dot_nn(a_ref[...], wo_ref[...])
    h_ref[...] = resid
    scale_inv = lax.rsqrt(jnp.mean(resid * resid, axis=-1, keepdims=True) + epsilon)
    normed_ref[...] = (resid * scale_inv * extra_ref[EXPERTS + 1 : EXPERTS + 2, :]).astype(bf16)


def softmax_over(picked, logits, axis):
    top = jnp.max(jnp.where(picked, logits, -jnp.inf), axis=axis, keepdims=True)
    raised = jnp.where(picked, jnp.exp(jnp.minimum(logits - top, 0.0)), 0.0)
    return raised / jnp.sum(raised, axis=axis, keepdims=True)


def experts_body(count, shards, pieces, chunk, last, meta, routes_ref, c_ref, extra_ref, *refs):
    refs = list(refs)

    def take(number):
        taken = refs[:number]
        del refs[:number]
        return taken

    weights, blocks = take(len(pieces[0])), take(len(pieces[1]))
    if chunk > 0:
        (part_g, part_m) = take(2)
    send_ref, keep_ref = take(2)
    (mix_ref,) = take(1)
    ring_refs = take(len(ring_shapes(count, TILE, WIDE)) if last else 1)
    up_s, down_s, x_s, c_s, ge_s, a_s, gu_s, d_s, eg_s, gs_s, gup_s, gdown_s, gate_s, rank_s, gg_s = refs
    step = pl.program_id(0)
    local = EXPERTS // count
    members = local // CHUNKS
    up_rows, down_rows = MODEL_WIDTH // shards, FF // shards
    slots = count * CAP
    place = meta[shards]
    expert = place * local + chunk * members + step

    def absolute(k):
        return lax.rem(place - k + count, count)

    @pl.when(step == 0)
    def routing():
        router = extra_ref[:EXPERTS, :].astype(bf16)
        later = (
            lax.broadcasted_iota(jnp.int32, (TILE, TILE), 0) < lax.broadcasted_iota(jnp.int32, (TILE, TILE), 1)
        )
        later = jnp.where(later, 1.0, 0.0).astype(bf16)
        names = lax.broadcasted_iota(jnp.int32, (EXPERTS, TILE), 0)
        for k in range(count):
            named = routes_ref[absolute(k)]
            picked = names == named[0:1, :]
            for j in range(1, TOP):
                picked = jnp.logical_or(picked, names == named[j : j + 1, :])
            logits = dot_nt(router, block_value(pieces[1], blocks, k))
            gate_s[k] = softmax_over(picked, logits, 0)
            before = dot_nn(jnp.where(picked, 1.0, 0.0).astype(bf16), later)
            rank_s[k] = jnp.where(picked, before, -1.0)
        gg_s[...] = jnp.zeros_like(gg_s)

    for (r, row, value), ref in zip(pieces[0], weights):
        rows = value.shape[1]
        low, high = row, min(row + rows, up_rows)
        if high > low:
            to = pl.ds(pl.multiple_of(meta[r] * up_rows + low, 32), high - low)
            up_s[to, :] = ref[0, low - row : high - row, :]
        low, high = max(row, up_rows), row + rows
        if high > low:
            to = pl.ds(pl.multiple_of(meta[r] * down_rows + low - up_rows, 32), high - low)
            down_s[to, :] = ref[0, low - row : high - row, :]

    wanted = lax.broadcasted_iota(jnp.int32, (CAP, TILE), 0).astype(f32)
    held = aligned(step * CAP, CAP)
    gates = []
    for k in range(count):
        rank = rank_s[k, pl.ds(expert, 1), :]
        gate = gate_s[k, pl.ds(expert, 1), :]
        hit = wanted == rank
        chosen = jnp.where(hit, 1.0, 0.0).astype(bf16)
        d_s[k, held, :] = chosen
        here = slice(k * CAP, (k + 1) * CAP)
        x_s[here, :] = dot_nn(chosen, block_value(pieces[1], blocks, k)).astype(bf16)
        upstream = dot_nn(chosen, c_ref[aligned(absolute(k) * TILE, TILE), :])
        own_gate = jnp.sum(jnp.where(hit, gate, 0.0), axis=1, keepdims=True)
        gates.append(own_gate)
        c_s[here, :] = upstream.astype(bf16)
        ge_s[here, :] = (own_gate * (res_scale * upstream)).astype(bf16)

    for j in range(FF // TILE):
        left, right = slice(j * TILE, (j + 1) * TILE), slice(FF + j * TILE, FF + (j + 1) * TILE)
        gate_part = dot_nn(x_s[...], up_s[:, left])
        up_part = dot_nn(x_s[...], up_s[:, right])
        hidden_grad = dot_nt(ge_s[...], down_s[left, :])
        sigmoid_gate = jax.nn.sigmoid(gate_part)
        swish = gate_part * sigmoid_gate
        a_s[:, left] = (swish * up_part).astype(bf16)
        slope = sigmoid_gate * (1.0 + gate_part * (1.0 - sigmoid_gate))
        gu_s[:, left] = (hidden_grad * up_part * slope).astype(bf16)
        gu_s[:, right] = (hidden_grad * swish).astype(bf16)

    gate_grad = jnp.zeros((slots, 1), f32)
    for j in range(MODEL_WIDTH // TILE):
        columns = slice(j * TILE, (j + 1) * TILE)
        produced = dot_nn(a_s[...], down_s[:, columns]).astype(bf16).astype(f32)
        gate_grad += jnp.sum(res_scale * c_s[:, columns].astype(f32) * produced, axis=1, keepdims=True)
        input_grad = dot_nt(gu_s[...], up_s[columns, :]).astype(bf16)
        for k in range(count):
            here = slice(k * CAP, (k + 1) * CAP)
            eg_s[k, held, columns] = (gates[k] * produced[here]).astype(bf16)
            gs_s[k, held, columns] = input_grad[here]
    for k in range(count):
        hit = wanted == rank_s[k, pl.ds(expert, 1), :]
        spread = jnp.where(hit, gate_grad[k * CAP : (k + 1) * CAP], 0.0)
        gg_s[k, pl.ds(expert, 1), :] = jnp.sum(spread, axis=0, keepdims=True)

    for j in range(FF // TILE):
        rows = slice(j * TILE, (j + 1) * TILE)
        gdown_s[rows, :] = dot_tn(a_s[:, rows], ge_s[...]).astype(bf16)
    for j in range(MODEL_WIDTH // TILE):
        rows = slice(j * TILE, (j + 1) * TILE)
        gup_s[rows, :] = dot_tn(x_s[:, rows], gu_s[...]).astype(bf16)
    for r in range(shards):
        ref = send_ref if r % 2 else keep_ref
        ref[r // 2, 0, :up_rows, :] = gup_s[aligned(meta[r] * up_rows, up_rows), :]
        ref[r // 2, 0, up_rows:, :] = gdown_s[aligned(meta[r] * down_rows, down_rows), :]

    @pl.when(step == members - 1)
    def combine():
        for k in range(count):
            spread = d_s[k]
            mixed = dot_tn(spread, eg_s[k])
            summed = dot_tn(spread, gs_s[k])
            exact = gg_s[k]
            rounded = exact.astype(bf16).astype(f32)
            rest = jnp.zeros((LANES - 2 * EXPERTS, TILE), f32)
            tail = jnp.concatenate([rounded, exact - rounded, rest], axis=0).T
            at = absolute(k)
            if chunk > 0:
                mixed += part_m[at].astype(f32)
                summed += part_g[k, :, :MODEL_WIDTH].astype(f32)
                tail += part_g[k, :, MODEL_WIDTH:].astype(f32)
            mix_ref[at] = mixed.astype(bf16)
            if last:
                ring_put(count, ring_refs, k, TILE, summed)
                ring_put_tail(count, ring_refs, k, TILE, tail)
            else:
                ring_refs[0][k, :, :MODEL_WIDTH] = summed.astype(bf16)
                ring_refs[0][k, :, MODEL_WIDTH:] = tail.astype(bf16)


def backward_body(count, pieces, summed, meta, routes_ref, normed_ref, extra_ref, h_ref, c_ref, a_ref, wo_ref, q_ref, lse_ref, cos_ref, sin_ref, *refs):
    sums = refs[:summed]
    blocks = refs[summed : summed + len(pieces)]
    outs = refs[summed + len(pieces) :]
    gh_ref, go_ref, gpq_ref, gex_ref, gain_ref = outs[:5]
    ring_refs, ga_s = outs[5:-1], outs[-1]
    rows = q_ref.shape[0]
    place = meta[0]
    total = ring_total(sums)
    normed_grad, tail = total[:, :MODEL_WIDTH], total[:, MODEL_WIDTH:]
    names = lanes_of((rows, LANES))
    named = routes_ref[...]
    picked = names == named[:, 0:1]
    for j in range(1, TOP):
        picked = jnp.logical_or(picked, names == named[:, j : j + 1])
    row_names = lax.broadcasted_iota(jnp.int32, (LANES, MODEL_WIDTH), 0)
    router = jnp.where(row_names < EXPERTS, extra_ref[...], 0.0).astype(bf16)
    gate = softmax_over(picked, dot_nt(normed_ref[...], router), 1)
    gate_grad = jnp.where(picked, tail + pltpu.roll(tail, LANES - EXPERTS, 1), 0.0)
    inner = jnp.sum(gate * gate_grad, axis=1, keepdims=True)
    logit_grad = (gate * (gate_grad - inner)).astype(bf16)
    gex_ref[...] = dot_tn(normed_ref[...], logit_grad)
    normed_grad += dot_nn(logit_grad, router)
    resid = h_ref[...]
    scale_inv = lax.rsqrt(jnp.mean(resid * resid, axis=-1, keepdims=True) + epsilon)
    hat = resid * scale_inv
    gain_ref[...] = jnp.broadcast_to(jnp.sum(normed_grad * hat, axis=0, keepdims=True), gain_ref.shape)
    scaled = normed_grad * extra_ref[EXPERTS + 1 : EXPERTS + 2, :]
    part = scale_inv * (scaled - hat * jnp.mean(scaled * hat, axis=-1, keepdims=True))
    resid_grad = c_ref[...].astype(f32) + part
    gh_ref[...] = resid_grad
    go = (res_scale * resid_grad).astype(bf16)
    go_ref[...] = go
    ga_s[...] = dot_nt(go, wo_ref[...]).astype(bf16)
    cosine, sine = cos_ref[...], sin_ref[...]
    low = lanes_of((rows, LANES)) < HEAD_SIZE

    def variant(seen):
        def group(g, carry):
            lanes = aligned(g * LANES, LANES)
            pair = query_pair(q_ref[:, lanes])
            upstream = ga_s[:, lanes].astype(f32)
            product = upstream * a_ref[:, lanes].astype(f32)
            inner_low = jnp.sum(jnp.where(low, product, 0.0), axis=1, keepdims=True)
            inner_high = jnp.sum(jnp.where(low, 0.0, product), axis=1, keepdims=True)
            delta = jnp.concatenate([inner_low, inner_high], axis=0)
            logs = lse_ref[:, lanes]
            logsum = jnp.concatenate([logs[:, 0:1], logs[:, HEAD_SIZE : HEAD_SIZE + 1]], axis=0)
            high_pair = jnp.concatenate(
                [jnp.where(low, 0.0, pltpu.roll(upstream, HEAD_SIZE, 1)), jnp.where(low, 0.0, upstream)], axis=0
            ).astype(bf16)
            query_grad = jnp.zeros((2 * rows, LANES), f32)
            for k in range(seen):
                keys = block_lanes(pieces, blocks, k, lanes)
                weights = jnp.exp(causal_scores(pair, keys, k) - logsum)
                score_grad = (weights * (dot_nt(high_pair, keys) - delta)).astype(bf16)
                query_grad += dot_nn(score_grad, keys)
                back = dot_tn(score_grad, pair) + dot_tn(weights.astype(bf16), high_pair)
                put_lanes(k, lanes, back)
            query_grad = query_grad * att_scale
            tile = jnp.where(low, query_grad[:rows], pltpu.roll(query_grad[rows:], HEAD_SIZE, 1))
            tile = tile.astype(bf16).astype(f32)
            gpq_ref[:, lanes] = rotate_tile_back(tile, cosine, sine).astype(bf16)
            return carry

        lax.fori_loop(0, KEY_VALUE_HEADS, group, 0)
        for k in range(seen, count):
            ring_put(count, ring_refs, k, rows, jnp.zeros((rows, MODEL_WIDTH), f32))

    def put_lanes(k, lanes, value):
        views = [r.at[..., lanes] for r in ring_refs]
        ring_put(count, views, k, rows, value)

    for seen in range(1, count + 1):
        pl.when(place == seen - 1)(functools.partial(variant, seen))


def store_sets(shards, meta, source, send_ref, keep_ref, columns):
    rows = MODEL_WIDTH // shards
    for r in range(shards):
        ref = send_ref if r % 2 else keep_ref
        ref[r // 2, :, columns] = source[aligned(meta[r] * rows, rows), :].astype(bf16)


def query_weights_body(shards, meta, a_ref, go_ref, normed_ref, gpq_ref, wq_ref, send_ref, keep_ref, part_ref, full_s):
    full_s[...] = dot_tn(normed_ref[...], gpq_ref[...]).astype(bf16)
    store_sets(shards, meta, full_s, send_ref, keep_ref, slice(0, MODEL_WIDTH))
    full_s[...] = dot_tn(a_ref[...], go_ref[...]).astype(bf16)
    store_sets(shards, meta, full_s, send_ref, keep_ref, slice(MODEL_WIDTH, 2 * MODEL_WIDTH))
    part_ref[...] = dot_nt(gpq_ref[...], wq_ref[...])


def final_body(shards, summed, meta, x_ref, normed_ref, wkv_ref, extra_ref, part_ref, gh_ref, gex_ref, gain_ref, cos_ref, sin_ref, *refs):
    sums = refs[:summed]
    grad_ref, send_ref, keep_ref, gpkv_s, full_s, extra_s = refs[summed:]
    total = ring_total(sums).astype(bf16).astype(f32)
    cosine, sine = cos_ref[...], sin_ref[...]
    low = lanes_of(cosine.shape) < HEAD_SIZE
    for j in range(MODEL_WIDTH // LANES):
        lanes = slice(j * LANES, (j + 1) * LANES)
        tile = total[:, lanes]
        gpkv_s[:, lanes] = jnp.where(low, rotate_tile_back(tile, cosine, sine), tile).astype(bf16)
    normed_grad = part_ref[...] + dot_nt(gpkv_s[...], wkv_ref[...])
    source = x_ref[...].astype(f32)
    scale_inv = lax.rsqrt(jnp.mean(source * source, axis=-1, keepdims=True) + epsilon)
    hat = source * scale_inv
    gain_grad = jnp.sum(normed_grad * hat, axis=0, keepdims=True)
    scaled = normed_grad * extra_ref[EXPERTS : EXPERTS + 1, :]
    part = scale_inv * (scaled - hat * jnp.mean(scaled * hat, axis=-1, keepdims=True))
    grad_ref[...] = gh_ref[...] + part
    full_s[...] = dot_tn(normed_ref[...], gpkv_s[...]).astype(bf16)
    store_sets(shards, meta, full_s, send_ref, keep_ref, slice(0, MODEL_WIDTH))
    row_names = lax.broadcasted_iota(jnp.int32, (LANES, MODEL_WIDTH), 0)
    gains = jnp.where(row_names == EXPERTS, gain_grad, jnp.where(row_names == EXPERTS + 1, gain_ref[0:1, :], 0.0))
    extra_s[...] = gex_ref[...] + gains.T
    store_sets(shards, meta, extra_s, send_ref, keep_ref, slice(MODEL_WIDTH, WIDE))


def angle_tables(rows, offset):
    position = (offset + jnp.arange(rows)).astype(f32)
    frequency = 10000.0 ** (-(jnp.arange(HEAD_SIZE // 2).astype(f32) * 2.0 / HEAD_SIZE))
    angles = position[:, None] * frequency[None, :]
    cosine, sine = jnp.cos(angles), jnp.sin(angles)
    return (jnp.concatenate([cosine] * 4, axis=1), jnp.concatenate([-sine, sine] * 2, axis=1))


def shards_step(
    tokens,
    routes,
    cotangent,
    norm_gains,
    qkv_weight,
    out_weight,
    router_weight,
    expert_up,
    expert_down,
    mean_gains,
    square_gains,
    mean_qkv,
    square_qkv,
    mean_out,
    square_out,
    mean_router,
    square_router,
    mean_up,
    square_up,
    mean_down,
    square_down,
):
    rows = tokens.shape[1]
    count = lax.axis_size("seq")
    shards = lax.axis_size("fsdp")
    shard_rows = MODEL_WIDTH // shards
    local = EXPERTS // count
    members = local // CHUNKS
    place = lax.axis_index("seq").astype(jnp.int32)
    owners = (lax.axis_index("fsdp") ^ jnp.arange(shards)).astype(jnp.int32)
    owner_meta = jnp.concatenate([owners, place[None]])
    place_meta = place[None]
    x, c, own_routes = tokens[0], cotangent[0], routes[0]

    blank = jnp.zeros((shard_rows, LANES - EXPERTS - 2), f32)
    dense = jnp.concatenate([qkv_weight, out_weight, router_weight, norm_gains.T, blank], axis=1).astype(bf16)
    dense_pieces = gather_shards(dense)
    expert_pieces = []
    for i in range(CHUNKS):
        mine = slice(i * members, (i + 1) * members)
        packed = jnp.concatenate([expert_up[mine], expert_down[mine]], axis=1).astype(bf16)
        expert_pieces.append(gather_shards(packed))
    all_c = lax.all_gather(c, "seq", axis=0, tiled=True)
    all_routes = lax.all_gather(own_routes.T, "seq", axis=0)
    cosine, sine = angle_tables(rows, place * rows)

    square = shape_of((MODEL_WIDTH, MODEL_WIDTH))
    wide = shape_of((rows, MODEL_WIDTH))
    wide_f = shape_of((rows, MODEL_WIDTH), f32)
    extra_shape = shape_of((LANES, MODEL_WIDTH), f32)
    unit = 2 * rows * MODEL_WIDTH * MODEL_WIDTH
    wq, wkv, wo, extra, normed_one, q, kv = kernel_call(
        functools.partial(qkv_body, dense_pieces),
        [square, square, square, extra_shape, wide, wide, wide],
        [x, cosine, sine] + [a for _, _, a in dense_pieces],
        owner_meta,
        scratch=[pltpu.VMEM((MODEL_WIDTH, LANES), f32)],
        flops=2 * unit,
    )
    kv_pieces = ring_gather(kv)
    attended, logsum, resid, normed_two = kernel_call(
        functools.partial(attend_body, count, kv_pieces),
        [wide, wide_f, wide_f, wide],
        [q, x, wo, extra] + [a for _, _, a in kv_pieces],
        place_meta,
        flops=4 * unit,
    )
    two_pieces = ring_gather(normed_two)

    slots = count * CAP
    packed_rows = (MODEL_WIDTH + FF) // shards
    part_g = part_m = None
    sets = []
    for i in range(CHUNKS):
        last = i == CHUNKS - 1
        pieces = (expert_pieces[i], two_pieces)
        ins = [all_routes, all_c, extra] + [a for _, _, a in pieces[0]] + [a for _, _, a in pieces[1]]

        def still(a):
            return pl.BlockSpec(a.shape, functools.partial(lambda n, e, m: (0,) * n, a.ndim), pipeline_mode=pl.Buffered(1))

        in_specs = [still(a) for a in ins[:3]]
        in_specs += [pl.BlockSpec((1,) + a.shape[1:], lambda e, m: (e, 0, 0)) for _, _, a in pieces[0]]
        in_specs += [still(a) for _, _, a in pieces[1]]
        if i > 0:
            ins += [part_g, part_m]
            in_specs += [still(part_g), still(part_m)]
        set_shape = shape_of((shards // 2, members, packed_rows, MODEL_WIDTH))
        set_spec = pl.BlockSpec((shards // 2, 1, packed_rows, MODEL_WIDTH), lambda e, m: (0, e, 0, 0))
        ring = ring_shapes(count, rows, WIDE) if last else [shape_of((count, rows, WIDE))]
        outs = [set_shape, set_shape, shape_of((count, rows, MODEL_WIDTH))] + ring
        out_specs = [set_spec, set_spec] + [still(a) for a in outs[2:]]
        scratch = [
            pltpu.VMEM((MODEL_WIDTH, 2 * FF), bf16),
            pltpu.VMEM((FF, MODEL_WIDTH), bf16),
            pltpu.VMEM((slots, MODEL_WIDTH), bf16),
            pltpu.VMEM((slots, MODEL_WIDTH), bf16),
            pltpu.VMEM((slots, MODEL_WIDTH), bf16),
            pltpu.VMEM((slots, FF), bf16),
            pltpu.VMEM((slots, 2 * FF), bf16),
            pltpu.VMEM((count, members * CAP, rows), bf16),
            pltpu.VMEM((count, members * CAP, MODEL_WIDTH), bf16),
            pltpu.VMEM((count, members * CAP, MODEL_WIDTH), bf16),
            pltpu.VMEM((MODEL_WIDTH, 2 * FF), bf16),
            pltpu.VMEM((FF, MODEL_WIDTH), bf16),
            pltpu.VMEM((count, EXPERTS, rows), f32),
            pltpu.VMEM((count, EXPERTS, rows), f32),
            pltpu.VMEM((count, EXPERTS, rows), f32),
        ]
        results = kernel_call(
            functools.partial(experts_body, count, shards, pieces, i, last),
            outs,
            ins,
            owner_meta,
            scratch=scratch,
            grid=(members,),
            in_specs=in_specs,
            out_specs=out_specs,
            flops=members * slots * MODEL_WIDTH * FF * 18,
            limit=60,
        )
        sets.append(scatter_sets(results[0], results[1]))
        part_m = results[2]
        part_g = results[3]
        ring_parts = results[3:]

    mixture = lax.psum_scatter(part_m, "seq", scatter_dimension=0).astype(f32)
    output = (resid + res_scale * mixture).astype(bf16)[None]

    two_sums = ring_reduce(ring_parts)
    ring = ring_shapes(count, rows, MODEL_WIDTH)
    results = kernel_call(
        functools.partial(backward_body, count, kv_pieces, len(two_sums)),
        [wide_f, wide, wide, shape_of((MODEL_WIDTH, LANES), f32), shape_of((8, MODEL_WIDTH), f32)] + ring,
        [own_routes, normed_two, extra, resid, c, attended, wo, q, logsum, cosine, sine]
        + list(two_sums)
        + [a for _, _, a in kv_pieces],
        place_meta,
        scratch=[pltpu.VMEM((rows, MODEL_WIDTH), bf16)],
        flops=8 * unit,
    )
    resid_grad, go, gpq, router_grad, gain_grad = results[:5]
    kv_sums = ring_reduce(results[5:])
    dense_sets = shape_of((shards // 2, shard_rows, 2 * MODEL_WIDTH))
    send_q, keep_q, normed_part = kernel_call(
        functools.partial(query_weights_body, shards),
        [dense_sets, dense_sets, wide_f],
        [attended, go, normed_one, gpq, wq],
        owner_meta,
        scratch=[pltpu.VMEM((MODEL_WIDTH, MODEL_WIDTH), bf16)],
        flops=3 * unit,
    )
    rest_sets = shape_of((shards // 2, shard_rows, WIDE))
    tokens_grad, send_kv, keep_kv = kernel_call(
        functools.partial(final_body, shards, len(kv_sums)),
        [wide_f, rest_sets, rest_sets],
        [x, normed_one, wkv, extra, normed_part, resid_grad, router_grad, gain_grad, cosine, sine] + list(kv_sums),
        owner_meta,
        scratch=[
            pltpu.VMEM((rows, MODEL_WIDTH), bf16),
            pltpu.VMEM((MODEL_WIDTH, MODEL_WIDTH), bf16),
            pltpu.VMEM((MODEL_WIDTH, LANES), f32),
        ],
        flops=2 * unit,
    )
    tokens_grad = tokens_grad[None]

    def dense_total(send, keep):
        whole = jnp.concatenate(scatter_sets(send, keep), axis=0)
        return lax.psum(whole.astype(bf16), "seq").astype(f32)

    first = dense_total(send_q, keep_q)
    second = dense_total(send_kv, keep_kv)
    shard_qkv = jnp.concatenate([first[:, :MODEL_WIDTH], second[:, :MODEL_WIDTH]], axis=1)
    shard_out = first[:, MODEL_WIDTH:]
    shard_router = second[:, MODEL_WIDTH : MODEL_WIDTH + EXPERTS]
    shard_gains = second[:, MODEL_WIDTH + EXPERTS : MODEL_WIDTH + EXPERTS + 2].T
    packed_grad = jnp.concatenate([jnp.concatenate(s, axis=1) for s in sets], axis=0)
    shard_up = packed_grad[:, :shard_rows]
    shard_down = packed_grad[:, shard_rows:]
    fresh_gains, momentum_gains, variance_gains = adam_update(
        norm_gains, shard_gains, mean_gains, square_gains, learn_rates[0]
    )
    fresh_qkv, momentum_qkv, variance_qkv = adam_update(
        qkv_weight, shard_qkv, mean_qkv, square_qkv, learn_rates[1]
    )
    fresh_out, momentum_out, variance_out = adam_update(
        out_weight, shard_out, mean_out, square_out, learn_rates[2]
    )
    fresh_router, momentum_router, variance_router = adam_update(
        router_weight, shard_router, mean_router, square_router, learn_rates[3]
    )
    fresh_up, momentum_up, variance_up = adam_update(
        expert_up, shard_up, mean_up, square_up, learn_rates[4]
    )
    fresh_down, momentum_down, variance_down = adam_update(
        expert_down, shard_down, mean_down, square_down, learn_rates[5]
    )
    return (
        output,
        tokens_grad,
        shard_gains,
        shard_qkv,
        shard_out,
        shard_router,
        shard_up,
        shard_down,
        fresh_gains,
        fresh_qkv,
        fresh_out,
        fresh_router,
        fresh_up,
        fresh_down,
        momentum_gains,
        momentum_qkv,
        momentum_out,
        momentum_router,
        momentum_up,
        momentum_down,
        variance_gains,
        variance_qkv,
        variance_out,
        variance_router,
        variance_up,
        variance_down,
    )


def solution(mesh):
    block = P("fsdp", "seq", None)
    gains, dense, experts = P(None, "fsdp"), P("fsdp", None), P("seq", "fsdp", None)
    weights = (gains, dense, dense, dense, experts, experts)
    moments = tuple(s for spec in weights for s in (spec, spec))
    return jax.shard_map(
        shards_step,
        mesh=mesh,
        in_specs=(block, block, block) + weights + moments,
        out_specs=(block, block) + weights * 4,
        check_vma=False,
    )
```

time: 1350 us -> 621 us (0.46)
  the two profiles are of different devices: /device:TPU:12 before, /device:TPU:0 now
where the time goes in v1:
time: 621 us; the launch traced here: 611 us
  waiting for transfers between devices  272 us (44%)
  Pallas kernels  107 us (17%)
  starting transfers between devices  92.4 us (15%)
  other arithmetic  69.8 us (11%)
  local copies, waits for them, and re-layouts  36.9 us (6%)
  blocking collectives  17.7 us (3%)
  between operations  15.2 us (2%)
    ppermute x47, waiting for transfers between devices, xor_permute(): lax.ppermute(value, axis, [(i, i ^ mask) for i in range(lax.axis_size(axi...  121 us
    pallas_call x7, Pallas kernels, kernel_call(): pl.pallas_call(body, out_shape=outs, grid_spec=pltpu.PrefetchScalarGridSp...  107 us
    ppermute x16, waiting for transfers between devices, shift_permute(): lax.ppermute(value, axis, [(i, (i + step) % size) for i in range(size)])  101 us
    ppermute x16, starting transfers between devices, shift_permute(): lax.ppermute(value, axis, [(i, (i + step) % size) for i in range(size)])  55 us
    psum x1, waiting for transfers between devices, dense_total(): return lax.psum(whole.astype(bf16), 'seq').astype(f32)  46.2 us
    ppermute x47, starting transfers between devices, xor_permute(): lax.ppermute(value, axis, [(i, i ^ mask) for i in range(lax.axis_size(axi...  37.1 us
    unnamed x159, local copies, waits for them, and re-layouts  23.6 us
    sub x6, other arithmetic, adam_update(): weight - rate * (first_hat / (jnp.sqrt(second_hat) + adam_eps) + weight_d...  18.1 us
  transfers between devices with their start and end apart: 66, of which 35 were waited for; matrix products, arithmetic and copies ran while one was open for 12% of the time, Pallas kernels for 9%

profile of v1, /device:TPU:0, one launch (start us, length us, event | category | flops | bytes accessed | tf_op | source)
XLA Modules:
  0.0 611.5 jit_solution(8588849942571909092)
XLA Ops:
  16.3 14.2 %collective-permute-done.refs_1_ = bf16[128,3200]{1,0:T(8,128)(2,1)S(1)} collective-permute-done((bf16[128,3200]{1,0:T(8,128)(2,1)S(1)}, bf16[128,3200]{1,0:T(8,128)(2,1)S(1)}, u32[]{:S(2)}, u32[]{:S(2)}) %collective-permute-start) | collective-permute-done | bytes 819232 | tf_op jit(solution)/shard_map/ppermute | solution.py:90
  54.9 7.1 %shard_map.404 = (bf16[1024,1024]{1,0:T(8,128)(2,1)}, bf16[1024,1024]{1,0:T(8,128)(2,1)}, bf16[1024,1024]{1,0:T(8,128)(2,1)}, f32[128,1024]{1,0:T(8,128)S(1)}, b...) custom-call(s32[9]{0:T(128)S(1)} %pad_add_fusion.meta, ...), custom_call_target="tpu_custom_call" | custom-call | flops 1073741824 | bytes 15728640 | tf_op jit(solution)/shard_map/pallas_call | solution.py:70
  62.0 18.2 %collective-permute-done.26.refs_1_ = bf16[4,192,1024]{2,1,0:T(8,128)(2,1)} collective-permute-done((bf16[4,192,1024]{2,1,0:T(8,128)(2,1)}, bf16[4,192,1024]{2,1,0:T(8,128)(2,1)}, u32[]{:S(2)}, u32[]{:S(2)}) %collective-permute-start.26) | collective-permute-done | bytes 1572896 | tf_op jit(solution)/shard_map/ppermute | solution.py:90
  86.4 18.5 %collective-permute-done.9.refs_1_.refs_6_ = bf16[256,1024]{1,0:T(8,128)(2,1)S(1)} collective-permute-done((bf16[256,1024]{1,0:T(8,128)(2,1)S(1)}, bf16[256,1024]{1,0:T(8,128)(2,1)S(1)}, u32[]{:S(2)}, u32[]{:S(2)}) %collective-permute-start.9) | collective-permute-done | bytes 524320 | tf_op jit(solution)/shard_map/ppermute | solution.py:95
  107.6 6.2 %collective-permute-done.10.refs_2_.refs_7_ = bf16[256,1024]{1,0:T(8,128)(2,1)S(1)} collective-permute-done((bf16[256,1024]{1,0:T(8,128)(2,1)S(1)}, bf16[256,1024]{1,0:T(8,128)(2,1)S(1)}, u32[]{:S(2)}, u32[]{:S(2)}) %collective-permute-start.10) | collective-permute-done | bytes 524320 | tf_op jit(solution)/shard_map/ppermute | solution.py:95
  130.7 7.7 %shard_map.405 = (bf16[256,1024]{1,0:T(8,128)(2,1)S(1)}, f32[256,1024]{1,0:T(8,128)S(1)}, f32[256,1024]{1,0:T(8,128)}, bf16[256,1024]{1,0:T(8,128)(2,1)S(1)}) custom-call(s32[1]{0:T(128)} %bitcast.meta, bf16[256,1024]{1,0:T(8,128)(2,1)S(1)} %get-tuple-element.65.q_ref, bf16[256,1024]{1,0:T(8,128)(2,1)S(1)} %bitcast.67, ...), custom_call_target="tpu_custom_call" | custom-call | flops 2147483648 | bytes 8912896 | tf_op jit(solution)/shard_map/pallas_call | solution.py:70
  149.7 10.9 %collective-permute-done.22.refs_11_ = bf16[256,1024]{1,0:T(8,128)(2,1)S(1)} collective-permute-done((bf16[256,1024]{1,0:T(8,128)(2,1)S(1)}, bf16[256,1024]{1,0:T(8,128)(2,1)S(1)}, u32[]{:S(2)}, u32[]{:S(2)}) %collective-permute-start.22) | collective-permute-done | bytes 524320 | tf_op jit(solution)/shard_map/ppermute | solution.py:95
  160.7 7.5 %collective-permute-done.23.refs_12_ = bf16[256,1024]{1,0:T(8,128)(2,1)S(1)} collective-permute-done((bf16[256,1024]{1,0:T(8,128)(2,1)S(1)}, bf16[256,1024]{1,0:T(8,128)(2,1)S(1)}, u32[]{:S(2)}, u32[]{:S(2)}) %collective-permute-start.23) | collective-permute-done | bytes 524320 | tf_op jit(solution)/shard_map/ppermute | solution.py:95
  176.4 17.7 %all-gather = s32[32,256]{1,0:T(8,128)} all-gather(s32[8,256]{1,0:T(8,128)S(1)} %bitcast.76), channel_id=2, replica_groups=mesh['seq'=4,'fsdp'=8] {'seq'}, dimensions={0}, use_global_device_ids=true | all-gather | bytes 40960 | tf_op jit(solution)/shard_map/all_gather | solution.py:638
  195.5 32.1 %shard_map.406 = (bf16[4,4,192,1024]{3,2,1,0:T(8,128)(2,1)}, bf16[4,4,192,1024]{3,2,1,0:T(8,128)(2,1)}, bf16[4,256,1024]{2,1,0:T(8,128)(2,1)}, bf16[4,256,1152]{2,1,0:T(8,128)(2,1)}) custom-call(s32[9]{0:T(128)} %copy-done.13, s32[4,8,256]{2,1,0:T(8,128)} %bitcast.77, bf16[1024,1024]{1,0:T(8,128)(2,1)} %bitcast.79, f32[128,1024]{1,0:T(8,128)} %copy-done.1, ...), custom_call_target="tpu_custom_call" | custom-call | flops 14495514624 | bytes 34373632 | tf_op jit(solution)/shard_map/pallas_call | solution.py:70
  227.6 33.9 %shard_map.407 = (bf16[4,4,192,1024]{3,2,1,0:T(8,128)(2,1)}, bf16[4,4,192,1024]{3,2,1,0:T(8,128)(2,1)}, bf16[4,256,1024]{2,1,0:T(8,128)(2,1)}, bf16[256,1152]{1,...) custom-call(s32[9]{0:T(128)} %copy-done.13, ...), custom_call_target="tpu_custom_call" | custom-call | flops 14495514624 | bytes 38830080 | tf_op jit(solution)/shard_map/pallas_call | solution.py:70
  265.3 14.4 %collective-permute-done.36.refs_2_ = bf16[256,1152]{1,0:T(8,128)(2,1)S(1)} collective-permute-done((bf16[256,1152]{1,0:T(8,128)(2,1)}, bf16[256,1152]{1,0:T(8,128)(2,1)S(1)}, u32[]{:S(2)}, u32[]{:S(2)}) %collective-permute-start.36) | collective-permute-done | bytes 589856 | tf_op jit(solution)/shard_map/ppermute | solution.py:95
  281.7 8.1 %collective-permute-done.35.refs_1_ = bf16[256,1152]{1,0:T(8,128)(2,1)S(1)} collective-permute-done((bf16[256,1152]{1,0:T(8,128)(2,1)}, bf16[256,1152]{1,0:T(8,128)(2,1)S(1)}, u32[]{:S(2)}, u32[]{:S(2)}) %collective-permute-start.35) | collective-permute-done | bytes 589856 | tf_op jit(solution)/shard_map/ppermute | solution.py:95
  308.7 14.9 %shard_map.408 = (f32[256,1024]{1,0:T(8,128)}, bf16[256,1024]{1,0:T(8,128)(2,1)S(1)}, bf16[256,1024]{1,0:T(8,128)(2,1)S(1)}, f32[1024,128]{1,0:T(8,128)S(1)}, f3...) custom-call(s32[1]{0:T(128)} %bitcast.meta, ...), custom_call_target="tpu_custom_call" | custom-call | flops 4294967296 | bytes 16293888 | tf_op jit(solution)/shard_map/pallas_call | solution.py:70
  327.1 9.1 %collective-permute-start.39 = (bf16[256,1024]{1,0:T(8,128)(2,1)S(1)}, bf16[256,1024]{1,0:T(8,128)(2,1)S(1)}, u32[]{:S(2)}, u32[]{:S(2)}) collective-permute-start(bf16[256,1024]{1,0:T(8,128)(2,1)S(1)} %get-tuple-element.91), channel_id=1, source_target_pairs={{0,24},{8,0},{16,8},{24,16},{1,25},{9,1},{17,9},{25,17},{2,26},{10... | collective-permute-start | bytes 1572872 | tf_op jit(solution)/shard_map/ppermute | solution.py:95
  336.3 12.8 %collective-permute-done.40.refs_2_ = bf16[256,1024]{1,0:T(8,128)(2,1)S(1)} collective-permute-done((bf16[256,1024]{1,0:T(8,128)(2,1)S(1)}, bf16[256,1024]{1,0:T(8,128)(2,1)S(1)}, u32[]{:S(2)}, u32[]{:S(2)}) %collective-permute-start.40) | collective-permute-done | bytes 524320 | tf_op jit(solution)/shard_map/ppermute | solution.py:95
  352.9 7.4 %collective-permute-start.41 = (bf16[128,1024]{1,0:T(8,128)(2,1)S(1)}, bf16[128,1024]{1,0:T(8,128)(2,1)S(1)}, u32[]{:S(2)}, u32[]{:S(2)}) collective-permute-start(bf16[128,1024]{1,0:T(8,128)(2,1)S(1)} %add_convert_fusion.21), channel_id=1, source_target_pairs={{0,24},{8,0},{16,8},{24,16},{1,25},{9,1},{17,9},{25,17},{2,26},{10... | collective-permute-start | bytes 786440 | tf_op jit(solution)/shard_map/ppermute | solution.py:95
  393.5 8.0 %collective-permute-done.51 = bf16[2,64,2048]{2,1,0:T(8,128)(2,1)S(1)} collective-permute-done((bf16[2,64,2048]{2,1,0:T(8,128)(2,1)S(1)}, bf16[2,64,2048]{2,1,0:T(8,128)(2,1)S(1)}, u32[]{:S(2)}, u32[]{:S(2)}) %collective-permute-start.51) | collective-permute-done | bytes 524320 | tf_op jit(solution)/shard_map/ppermute | solution.py:90
  421.4 46.2 %all-reduce.3.cloned.1.call-done = (bf16[128,2048]{1,0:T(8,128)(2,1)}, bf16[128,1152]{1,0:T(8,128)(2,1)}) async-done(((bf16[128,2048]{1,0:T(8,128)(2,1)}, bf16[128,1152]{1,0:T(8,128)(2,1)}), (bf16[128,2048]{1,0:T(8,128)(2,1)}, bf16[128,1152]{1,0:T(8,128)(2,1)})) %all-reduce.3.cloned.1.call-update) | async-done | bytes 819216 | tf_op jit(solution)/shard_map/psum | solution.py:764
  502.8 12.6 %collective-permute-done.56 = bf16[2,4,96,1024]{3,2,1,0:T(8,128)(2,1)} collective-permute-done((bf16[2,4,96,1024]{3,2,1,0:T(8,128)(2,1)}, bf16[2,4,96,1024]{3,2,1,0:T(8,128)(2,1)}, u32[]{:S(2)}, u32[]{:S(2)}) %collective-permute-start.56) | collective-permute-done | bytes 1572896 | tf_op jit(solution)/shard_map/ppermute | solution.py:90
  523.7 25.4 %collective-permute-done.61 = bf16[2,4,96,1024]{3,2,1,0:T(8,128)(2,1)} collective-permute-done((bf16[2,4,96,1024]{3,2,1,0:T(8,128)(2,1)}, bf16[2,4,96,1024]{3,2,1,0:T(8,128)(2,1)}, u32[]{:S(2)}, u32[]{:S(2)}) %collective-permute-start.61) | collective-permute-done | bytes 1572896 | tf_op jit(solution)/shard_map/ppermute | solution.py:90
  559.3 6.5 %collective-permute-done.55 = bf16[4,96,1024]{2,1,0:T(8,128)(2,1)S(1)} collective-permute-done((bf16[4,96,1024]{2,1,0:T(8,128)(2,1)S(1)}, bf16[4,96,1024]{2,1,0:T(8,128)(2,1)S(1)}, u32[]{:S(2)}, u32[]{:S(2)}) %collective-permute-start.55) | collective-permute-done | bytes 786464 | tf_op jit(solution)/shard_map/ppermute | solution.py:90
  572.6 9.1 %collective-permute-done.60 = bf16[4,96,1024]{2,1,0:T(8,128)(2,1)S(1)} collective-permute-done((bf16[4,96,1024]{2,1,0:T(8,128)(2,1)S(1)}, bf16[4,96,1024]{2,1,0:T(8,128)(2,1)S(1)}, u32[]{:S(2)}, u32[]{:S(2)}) %collective-permute-start.60) | collective-permute-done | bytes 786464 | tf_op jit(solution)/shard_map/ppermute | solution.py:90
  597.8 6.7 %multiply_subtract_fusion = (f32[8,128,1024]{2,1,0:T(8,128)}, f32[8,128,1024]{2,1,0:T(8,128)}, f32[8,128,1024]{2,1,0:T(8,128)}, f32[8,128,1024]{2,1,0:T(8,128)}) fusion(f32[8,128,1024]{2,1,0:T(8,128)S(1)} %copy-done.30, f32[8,128,1024]{2,1,0:T(8,128)S(1)} %copy-done.34, f32[8,128,1024]{2,1,0:T(8,128)S(1)} %copy-done.35, ...), kind=kLoop, calls=%fused_computation.3 | loop fusion | flops 15728640 | bytes 33554432 | tf_op jit(solution)/shard_map/sub | solution.py:42
  (357 shorter events, 241.0 us)
Async XLA Ops:
  7.2 188.2 %all-gather.4.cloned.1.call-start = ((), (), s32[]{:S(2)}) async-start(), calls=%async_computation.2 | async-start | bytes 2621440 | tf_op jit(solution)/shard_map/all_gather | solution.py:637
  42.7 37.5 %collective-permute-start.26 = (bf16[4,192,1024]{2,1,0:T(8,128)(2,1)}, bf16[4,192,1024]{2,1,0:T(8,128)(2,1)}, u32[]{:S(2)}, u32[]{:S(2)}) collective-permute-start(bf16[4,192,1024]{2,1,0:T(8,128)(2,1)} %pad_maximum_fusion.1.refs_0_), channel_id=1, source_target_pairs={{0,2},{1,3},{2,0},{3,1},{4,6},{5,7},{6,4},{7,5},{8,10},{9,11},{10,... | collective-permute-start | bytes 4718600 | tf_op jit(solution)/shard_map/ppermute | solution.py:90
  44.1 37.6 %collective-permute-start.27 = (bf16[4,192,1024]{2,1,0:T(8,128)(2,1)}, bf16[4,192,1024]{2,1,0:T(8,128)(2,1)}, u32[]{:S(2)}, u32[]{:S(2)}) collective-permute-start(bf16[4,192,1024]{2,1,0:T(8,128)(2,1)} %pad_maximum_fusion.1.refs_0_), channel_id=1, source_target_pairs={{0,4},{1,5},{2,6},{3,7},{4,0},{5,1},{6,2},{7,3},{8,12},{9,13},{10,... | collective-permute-start | bytes 4718600 | tf_op jit(solution)/shard_map/ppermute | solution.py:90
  46.9 372.4 %reduce-scatter.2.cloned.1.call-start = ((), (), s32[]{:S(2)}) async-start(), calls=%async_computation.1 | async-start | bytes 2621440 | tf_op jit(solution)/shard_map/reduce_scatter | solution.py:721
  49.8 65.5 %collective-permute-start.30 = (bf16[4,192,1024]{2,1,0:T(8,128)(2,1)}, bf16[4,192,1024]{2,1,0:T(8,128)(2,1)S(1)}, u32[]{:S(2)}, u32[]{:S(2)}) collective-permute-start(bf16[4,192,1024]{2,1,0:T(8,128)(2,1)} %pad_maximum_fusion.1.refs_0_), channel_id=1, source_target_pairs={{0,1},{1,0},{2,3},{3,2},{4,5},{5,4},{6,7},{7,6},{8,9},{9,8},{10,11... | collective-permute-start | bytes 4718600 | tf_op jit(solution)/shard_map/ppermute | solution.py:90
  50.0 67.3 %collective-permute-start.13 = (bf16[4,192,1024]{2,1,0:T(8,128)(2,1)}, bf16[4,192,1024]{2,1,0:T(8,128)(2,1)}, u32[]{:S(2)}, u32[]{:S(2)}) collective-permute-start(bf16[4,192,1024]{2,1,0:T(8,128)(2,1)} %pad_maximum_fusion.refs_0_), channel_id=1, source_target_pairs={{0,2},{1,3},{2,0},{3,1},{4,6},{5,7},{6,4},{7,5},{8,10},{9,11},{10,... | collective-permute-start | bytes 4718600 | tf_op jit(solution)/shard_map/ppermute | solution.py:90
  50.8 69.6 %collective-permute-start.14 = (bf16[4,192,1024]{2,1,0:T(8,128)(2,1)}, bf16[4,192,1024]{2,1,0:T(8,128)(2,1)}, u32[]{:S(2)}, u32[]{:S(2)}) collective-permute-start(bf16[4,192,1024]{2,1,0:T(8,128)(2,1)} %pad_maximum_fusion.refs_0_), channel_id=1, source_target_pairs={{0,4},{1,5},{2,6},{3,7},{4,0},{5,1},{6,2},{7,3},{8,12},{9,13},{10,... | collective-permute-start | bytes 4718600 | tf_op jit(solution)/shard_map/ppermute | solution.py:90
  104.9 34.3 %collective-permute-start.28 = (bf16[4,96,1024]{2,1,0:T(8,128)(2,1)S(1)}, bf16[4,96,1024]{2,1,0:T(8,128)(2,1)S(1)}, u32[]{:S(2)}, u32[]{:S(2)}) collective-permute-start(bf16[4,96,1024]{2,1,0:T(8,128)(2,1)S(1)} %slice.436), channel_id=1, source_target_pairs={{0,4},{1,5},{2,6},{3,7},{4,0},{5,1},{6,2},{7,3},{8,12},{9,13},{10,... | collective-permute-start | bytes 2359304 | tf_op jit(solution)/shard_map/ppermute | solution.py:90
  126.4 49.4 %collective-permute-start.31 = (bf16[4,192,1024]{2,1,0:T(8,128)(2,1)}, bf16[4,192,1024]{2,1,0:T(8,128)(2,1)S(1)}, u32[]{:S(2)}, u32[]{:S(2)}) collective-permute-start(bf16[4,192,1024]{2,1,0:T(8,128)(2,1)} %collective-permute-done.26.refs_1_), channel_id=1, source_target_pairs={{0,1},{1,0},{2,3},{3,2},{4,5},{5,4},{6,7},{7,6},{8,9},{9,8},{10,11... | collective-permute-start | bytes 4718600 | tf_op jit(solution)/shard_map/ppermute | solution.py:90
  130.6 45.7 %collective-permute-start.32 = (bf16[4,192,1024]{2,1,0:T(8,128)(2,1)}, bf16[4,192,1024]{2,1,0:T(8,128)(2,1)S(1)}, u32[]{:S(2)}, u32[]{:S(2)}) collective-permute-start(bf16[4,192,1024]{2,1,0:T(8,128)(2,1)} %collective-permute-done.27.refs_2_), channel_id=1, source_target_pairs={{0,1},{1,0},{2,3},{3,2},{4,5},{5,4},{6,7},{7,6},{8,9},{9,8},{10,11... | collective-permute-start | bytes 4718600 | tf_op jit(solution)/shard_map/ppermute | solution.py:90
  175.8 51.7 %collective-permute-start.17 = (bf16[4,192,1024]{2,1,0:T(8,128)(2,1)}, bf16[4,192,1024]{2,1,0:T(8,128)(2,1)}, u32[]{:S(2)}, u32[]{:S(2)}) collective-permute-start(bf16[4,192,1024]{2,1,0:T(8,128)(2,1)} %pad_maximum_fusion.refs_0_), channel_id=1, source_target_pairs={{0,1},{1,0},{2,3},{3,2},{4,5},{5,4},{6,7},{7,6},{8,9},{9,8},{10,11... | collective-permute-start | bytes 4718600 | tf_op jit(solution)/shard_map/ppermute | solution.py:90
  175.8 51.7 %collective-permute-start.18 = (bf16[4,192,1024]{2,1,0:T(8,128)(2,1)}, bf16[4,192,1024]{2,1,0:T(8,128)(2,1)}, u32[]{:S(2)}, u32[]{:S(2)}) collective-permute-start(bf16[4,192,1024]{2,1,0:T(8,128)(2,1)} %collective-permute-done.13.refs_1_), channel_id=1, source_target_pairs={{0,1},{1,0},{2,3},{3,2},{4,5},{5,4},{6,7},{7,6},{8,9},{9,8},{10,11... | collective-permute-start | bytes 4718600 | tf_op jit(solution)/shard_map/ppermute | solution.py:90
  176.3 51.2 %collective-permute-start.19 = (bf16[4,192,1024]{2,1,0:T(8,128)(2,1)}, bf16[4,192,1024]{2,1,0:T(8,128)(2,1)}, u32[]{:S(2)}, u32[]{:S(2)}) collective-permute-start(bf16[4,192,1024]{2,1,0:T(8,128)(2,1)} %collective-permute-done.14.refs_2_), channel_id=1, source_target_pairs={{0,1},{1,0},{2,3},{3,2},{4,5},{5,4},{6,7},{7,6},{8,9},{9,8},{10,11... | collective-permute-start | bytes 4718600 | tf_op jit(solution)/shard_map/ppermute | solution.py:90
  194.1 33.4 %collective-permute-start.20 = (bf16[4,96,1024]{2,1,0:T(8,128)(2,1)}, bf16[4,96,1024]{2,1,0:T(8,128)(2,1)}, u32[]{:S(2)}, u32[]{:S(2)}) collective-permute-start(bf16[4,96,1024]{2,1,0:T(8,128)(2,1)} %collective-permute-done.15.refs_3_), channel_id=1, source_target_pairs={{0,1},{1,0},{2,3},{3,2},{4,5},{5,4},{6,7},{7,6},{8,9},{9,8},{10,11... | collective-permute-start | bytes 2359304 | tf_op jit(solution)/shard_map/ppermute | solution.py:90
  195.0 32.6 %collective-permute-start.21 = (bf16[4,96,1024]{2,1,0:T(8,128)(2,1)}, bf16[4,96,1024]{2,1,0:T(8,128)(2,1)}, u32[]{:S(2)}, u32[]{:S(2)}) collective-permute-start(bf16[4,96,1024]{2,1,0:T(8,128)(2,1)} %collective-permute-done.16.refs_4_), channel_id=1, source_target_pairs={{0,1},{1,0},{2,3},{3,2},{4,5},{5,4},{6,7},{7,6},{8,9},{9,8},{10,11... | collective-permute-start | bytes 2359304 | tf_op jit(solution)/shard_map/ppermute | solution.py:90
  376.4 95.6 %collective-permute-start.53 = (bf16[4,4,192,1024]{3,2,1,0:T(8,128)(2,1)}, bf16[4,4,192,1024]{3,2,1,0:T(8,128)(2,1)}, u32[]{:S(2)}, u32[]{:S(2)}) collective-permute-start(bf16[4,4,192,1024]{3,2,1,0:T(8,128)(2,1)} %get-tuple-element.101), channel_id=1, source_target_pairs={{0,1},{1,0},{2,3},{3,2},{4,5},{5,4},{6,7},{7,6},{8,9},{9,8},{10,11... | collective-permute-start | bytes 18874376 | tf_op jit(solution)/shard_map/ppermute | solution.py:90
  376.4 105.6 %collective-permute-start.58 = (bf16[4,4,192,1024]{3,2,1,0:T(8,128)(2,1)}, bf16[4,4,192,1024]{3,2,1,0:T(8,128)(2,1)}, u32[]{:S(2)}, u32[]{:S(2)}) collective-permute-start(bf16[4,4,192,1024]{3,2,1,0:T(8,128)(2,1)} %get-tuple-element.103), channel_id=1, source_target_pairs={{0,1},{1,0},{2,3},{3,2},{4,5},{5,4},{6,7},{7,6},{8,9},{9,8},{10,11... | collective-permute-start | bytes 18874376 | tf_op jit(solution)/shard_map/ppermute | solution.py:90
  376.9 90.6 %all-reduce.3.cloned.1.call-start = ((), (), s32[]{:S(2)}) async-start(), calls=%async_computation.3 | async-start | bytes 1638400 | tf_op jit(solution)/shard_map/psum | solution.py:764
  477.8 37.6 %collective-permute-start.56 = (bf16[2,4,96,1024]{3,2,1,0:T(8,128)(2,1)}, bf16[2,4,96,1024]{3,2,1,0:T(8,128)(2,1)}, u32[]{:S(2)}, u32[]{:S(2)}) collective-permute-start(bf16[2,4,96,1024]{3,2,1,0:T(8,128)(2,1)} %pad_maximum_fusion.3), channel_id=1, source_target_pairs={{0,4},{1,5},{2,6},{3,7},{4,0},{5,1},{6,2},{7,3},{8,12},{9,13},{10,... | collective-permute-start | bytes 4718600 | tf_op jit(solution)/shard_map/ppermute | solution.py:90
  480.5 37.6 %collective-permute-start.54 = (bf16[2,4,96,1024]{3,2,1,0:T(8,128)(2,1)}, bf16[2,4,96,1024]{3,2,1,0:T(8,128)(2,1)}, u32[]{:S(2)}, u32[]{:S(2)}) collective-permute-start(bf16[2,4,96,1024]{3,2,1,0:T(8,128)(2,1)} %pad_maximum_fusion.2), channel_id=1, source_target_pairs={{0,2},{1,3},{2,0},{3,1},{4,6},{5,7},{6,4},{7,5},{8,10},{9,11},{10,... | collective-permute-start | bytes 4718600 | tf_op jit(solution)/shard_map/ppermute | solution.py:90
  486.7 62.3 %collective-permute-start.61 = (bf16[2,4,96,1024]{3,2,1,0:T(8,128)(2,1)}, bf16[2,4,96,1024]{3,2,1,0:T(8,128)(2,1)}, u32[]{:S(2)}, u32[]{:S(2)}) collective-permute-start(bf16[2,4,96,1024]{3,2,1,0:T(8,128)(2,1)} %pad_maximum_fusion.5), channel_id=1, source_target_pairs={{0,4},{1,5},{2,6},{3,7},{4,0},{5,1},{6,2},{7,3},{8,12},{9,13},{10,... | collective-permute-start | bytes 4718600 | tf_op jit(solution)/shard_map/ppermute | solution.py:90
  488.6 63.3 %collective-permute-start.59 = (bf16[2,4,96,1024]{3,2,1,0:T(8,128)(2,1)}, bf16[2,4,96,1024]{3,2,1,0:T(8,128)(2,1)}, u32[]{:S(2)}, u32[]{:S(2)}) collective-permute-start(bf16[2,4,96,1024]{3,2,1,0:T(8,128)(2,1)} %pad_maximum_fusion.4), channel_id=1, source_target_pairs={{0,2},{1,3},{2,0},{3,1},{4,6},{5,7},{6,4},{7,5},{8,10},{9,11},{10,... | collective-permute-start | bytes 4718600 | tf_op jit(solution)/shard_map/ppermute | solution.py:90
  521.5 44.3 %collective-permute-start.55 = (bf16[4,96,1024]{2,1,0:T(8,128)(2,1)S(1)}, bf16[4,96,1024]{2,1,0:T(8,128)(2,1)S(1)}, u32[]{:S(2)}, u32[]{:S(2)}) collective-permute-start(bf16[4,96,1024]{2,1,0:T(8,128)(2,1)S(1)} %get-tuple-element.235), channel_id=1, source_target_pairs={{0,4},{1,5},{2,6},{3,7},{4,0},{5,1},{6,2},{7,3},{8,12},{9,13},{10,... | collective-permute-start | bytes 2359304 | tf_op jit(solution)/shard_map/ppermute | solution.py:90
  522.2 46.5 %collective-permute-start.57 = (bf16[4,96,1024]{2,1,0:T(8,128)(2,1)S(1)}, bf16[4,96,1024]{2,1,0:T(8,128)(2,1)S(1)}, u32[]{:S(2)}, u32[]{:S(2)}) collective-permute-start(bf16[4,96,1024]{2,1,0:T(8,128)(2,1)S(1)} %get-tuple-element.236), channel_id=1, source_target_pairs={{0,2},{1,3},{2,0},{3,1},{4,6},{5,7},{6,4},{7,5},{8,10},{9,11},{10,... | collective-permute-start | bytes 2359304 | tf_op jit(solution)/shard_map/ppermute | solution.py:90
  (115 other events, 1896.7 us)
Sparse Core Ops, SparseCore 0:
  47.0 61.5 all-gather.3
  377.0 42.2 reduce-scatter.1
  423.1 44.3 all-reduce.2

commit v2 on v1

v2 whole, which is shorter than its diff:
```python
import functools

import jax
import jax.numpy as jnp
from jax import lax
from jax.experimental import pallas as pl
from jax.experimental.pallas import tpu as pltpu
from jax.sharding import PartitionSpec as P

MODEL_WIDTH = 1024
QUERY_HEADS = 16
KEY_VALUE_HEADS = 8
HEAD_SIZE = 64
EXPERTS = 32
FF = 512
TOP = 8
STEP = 3
CAP = 96
LANES = 128
TILE = 256

epsilon = 1e-06
res_scale = 0.22
att_scale = 0.015625
beta_one = 0.9
beta_two = 0.95
adam_eps = 1e-08
weight_decay = 0.1
learn_rates = (0.4, 0.04, 0.2, 0.01, 0.01, 0.05)

bf16 = jnp.bfloat16
f32 = jnp.float32
WIDE = MODEL_WIDTH + LANES


def adam_update(weight, gradient, first, second, rate):
    first_new = beta_one * first + (1.0 - beta_one) * gradient
    second_new = beta_two * second + (1.0 - beta_two) * gradient * gradient
    first_hat = first_new / (1.0 - beta_one**STEP)
    second_hat = second_new / (1.0 - beta_two**STEP)
    fresh = weight - rate * (first_hat / (jnp.sqrt(second_hat) + adam_eps) + weight_decay * weight)
    return (fresh, first_new, second_new)


def dot_nn(a, b):
    return lax.dot_general(a, b, (((1,), (0,)), ((), ())), preferred_element_type=f32)


def dot_nt(a, b):
    return lax.dot_general(a, b, (((1,), (1,)), ((), ())), preferred_element_type=f32)


def dot_tn(a, b):
    return lax.dot_general(a, b, (((0,), (0,)), ((), ())), preferred_element_type=f32)


def lanes_of(shape):
    return lax.broadcasted_iota(jnp.int32, shape, len(shape) - 1)


def aligned(index, size):
    if isinstance(index, int):
        return slice(index, index + size)
    return pl.ds(pl.multiple_of(index, size), size)


def kernel_call(body, outs, ins, scalars, scratch=(), grid=None, in_specs=None, out_specs=None, limit=60, after=(), micros=10, aliases=None):
    in_specs = in_specs or [pl.BlockSpec(memory_space=pltpu.VMEM)] * len(ins)
    out_specs = out_specs or [pl.BlockSpec(memory_space=pltpu.VMEM)] * len(outs)
    in_specs = [pl.BlockSpec(memory_space=pl.ANY)] * len(after) + in_specs

    def ordered_body(meta, *refs):
        body(meta, *refs[len(after) :])

    return pl.pallas_call(
        ordered_body,
        out_shape=outs,
        grid_spec=pltpu.PrefetchScalarGridSpec(
            num_scalar_prefetch=1,
            grid=grid or (1,),
            in_specs=in_specs,
            out_specs=out_specs,
            scratch_shapes=list(scratch),
        ),
        compiler_params=pltpu.CompilerParams(vmem_limit_bytes=limit * 1024 * 1024),
        input_output_aliases=aliases or {},
        cost_estimate=pl.CostEstimate(flops=micros * 10**9, bytes_accessed=micros * 10**6, transcendentals=0),
    )(scalars, *after, *ins)


def tie(value, *earlier):
    anywhere = pl.BlockSpec(memory_space=pl.ANY)
    return pl.pallas_call(
        lambda *refs: None,
        out_shape=shape_of(value.shape, value.dtype),
        in_specs=[anywhere] * (1 + len(earlier)),
        out_specs=anywhere,
        input_output_aliases={0: 0},
    )(value, *earlier)


def shape_of(shape, kind=bf16):
    return jax.ShapeDtypeStruct(shape, kind)


def xor_permute(value, axis, mask):
    return lax.ppermute(value, axis, [(i, i ^ mask) for i in range(lax.axis_size(axis))])


def shift_permute(value, axis, step):
    size = lax.axis_size(axis)
    return lax.ppermute(value, axis, [(i, (i + step) % size) for i in range(size)])


class Gathered:
    def __init__(self, value):
        self.plain = lax.axis_size("fsdp") != 8
        self.value = value
        self.half = value.shape[0] // 2
        if not self.plain:
            self.over_x = xor_permute(value, "fsdp", 2)
            self.over_y = xor_permute(value, "fsdp", 4)
            self.core = xor_permute(value, "fsdp", 1)

    def forward(self, *earlier):
        if self.plain:
            return
        self.over_x = tie(self.over_x, self.core, *earlier)
        self.over_y = tie(self.over_y, self.core, *earlier)
        self.far_first = xor_permute(self.over_x[: self.half], "fsdp", 4)
        self.far_second = xor_permute(self.over_y[self.half :], "fsdp", 2)

    def arrived(self):
        return () if self.plain else (self.far_first, self.far_second)

    def pieces(self, *earlier):
        count, half = lax.axis_size("fsdp"), self.half
        if self.plain:
            whole = lax.all_gather(self.value, "fsdp", axis=0)
            whole = jnp.take(whole, lax.axis_index("fsdp") ^ jnp.arange(count), axis=0)
            return [(r, 0, whole[r]) for r in range(count)]
        if earlier:
            self.far_first = tie(self.far_first, *earlier)
            self.far_second = tie(self.far_second, *earlier)
        mine = [(2, 0, self.over_x), (4, 0, self.over_y), (6, 0, self.far_first), (6, half, self.far_second)]
        pieces = [(0, 0, self.value), (1, 0, self.core)] + mine
        return pieces + [(r + 1, row, xor_permute(a, "fsdp", 1)) for r, row, a in mine]


def pairs_body(groups, meta, *refs):
    sent_x, sent_y, rest = refs[2 * groups :]
    left = 0
    for keep, got in zip(refs[:groups], refs[groups : 2 * groups]):
        half, columns = keep.shape[1] // 2, keep.shape[2]
        lanes = slice(left, left + columns)
        left += columns

        def pair(i, part):
            piece = slice(part * half, (part + 1) * half)
            return (keep[i, piece, :].astype(f32) + got[i, piece, :].astype(f32)).astype(bf16)

        for ref, place, value in (
            (sent_x, 0, pair(3, 0)),
            (sent_x, 1, pair(1, 0)),
            (sent_y, 0, pair(3, 1)),
            (sent_y, 1, pair(2, 1)),
            (rest, 0, pair(0, 0)),
            (rest, 1, pair(0, 1)),
            (rest, 2, pair(1, 1)),
            (rest, 3, pair(2, 0)),
        ):
            ref[place, :, lanes] = value


def passed_body(meta, rest, over_x, over_y, then_x, then_y):
    then_x[...] = (rest[2].astype(f32) + over_y[0].astype(f32)).astype(bf16)
    then_y[...] = (rest[3].astype(f32) + over_x[0].astype(f32)).astype(bf16)


def summed_body(meta, rest, over_x, over_y, then_x, then_y, total):
    half = rest.shape[1]
    total[:half, :] = (rest[0].astype(f32) + over_x[1].astype(f32) + then_y[...].astype(f32)).astype(bf16)
    total[half:, :] = (rest[1].astype(f32) + over_y[1].astype(f32) + then_x[...].astype(f32)).astype(bf16)


class Scattered:
    def __init__(self, scalars):
        self.plain = lax.axis_size("fsdp") != 8
        self.scalars = scalars
        self.send, self.keep, self.got = [], [], []

    def add(self, send, keep, *earlier):
        self.send.append(send)
        self.keep.append(keep)
        if not self.plain:
            self.got.append(xor_permute(tie(send, *earlier) if earlier else send, "fsdp", 1))

    def first(self, *earlier):
        if self.plain:
            return ()
        rows, columns = self.keep[0].shape[1], sum(a.shape[2] for a in self.keep)
        two, four = shape_of((2, rows // 2, columns)), shape_of((4, rows // 2, columns))
        body = functools.partial(pairs_body, len(self.keep))
        sent_x, sent_y, self.rest = kernel_call(
            body, [two, two, four], self.keep + self.got, self.scalars, after=earlier, micros=3
        )
        self.over_x = xor_permute(sent_x, "fsdp", 2)
        self.over_y = xor_permute(sent_y, "fsdp", 4)
        return (sent_x, sent_y)

    def second(self, *earlier):
        if self.plain:
            return ()
        one = shape_of(self.rest.shape[1:])
        ins = [self.rest, self.over_x, self.over_y]
        sent_x, sent_y = kernel_call(passed_body, [one, one], ins, self.scalars, after=earlier, micros=2)
        self.then_x = xor_permute(sent_x, "fsdp", 2)
        self.then_y = xor_permute(sent_y, "fsdp", 4)
        return (sent_x, sent_y)

    def total(self, *earlier):
        if self.plain:
            count = lax.axis_size("fsdp")
            keep, send = jnp.concatenate(self.keep, axis=2), jnp.concatenate(self.send, axis=2)
            both = jnp.stack([keep, send], axis=1).reshape((count,) + keep.shape[1:])
            both = jnp.take(both, lax.axis_index("fsdp") ^ jnp.arange(count), axis=0)
            return lax.psum_scatter(both, "fsdp", scatter_dimension=0)
        ins = [self.rest, self.over_x, self.over_y, self.then_x, self.then_y]
        outs = [shape_of((2 * self.rest.shape[1], self.rest.shape[2]))]
        return kernel_call(summed_body, outs, ins, self.scalars, after=earlier, micros=2)[0]


def expert_pairs_body(meta, keep, got, sent_x, sent_y, rest):
    half = keep.shape[2] // 2

    def pair(i, part):
        piece = slice(part * half, (part + 1) * half)
        return (keep[i, 0, piece, :].astype(f32) + got[i, 0, piece, :].astype(f32)).astype(bf16)

    sent_x[0, 0], sent_x[1, 0] = pair(3, 0), pair(1, 0)
    sent_y[0, 0], sent_y[1, 0] = pair(3, 1), pair(2, 1)
    rest[0, 0], rest[1, 0], rest[2, 0], rest[3, 0] = pair(0, 0), pair(0, 1), pair(1, 1), pair(2, 0)


def expert_passed_body(meta, rest, over_x, over_y, then_x, then_y):
    then_x[0] = (rest[0, 0].astype(f32) + over_y[0, 0].astype(f32)).astype(bf16)
    then_y[0] = (rest[1, 0].astype(f32) + over_x[0, 0].astype(f32)).astype(bf16)


class ScatteredExperts:
    def __init__(self, send, keep, scalars):
        self.plain = lax.axis_size("fsdp") != 8
        self.send, self.keep, self.scalars = send, keep, scalars
        if not self.plain:
            self.got = xor_permute(send, "fsdp", 1)

    def first(self, *earlier):
        if self.plain:
            return ()
        sets, self.members, rows, columns = self.keep.shape
        half = rows // 2

        def group(n, start=0):
            return pl.BlockSpec((n, 1, half, columns), lambda e, m: (start, e, 0, 0))

        self.group = group
        self.single = pl.BlockSpec((1, half, columns), lambda e, m: (e, 0, 0))
        whole = pl.BlockSpec((sets, 1, rows, columns), lambda e, m: (0, e, 0, 0))
        shapes = [shape_of((n, self.members, half, columns)) for n in (2, 2, 4)]
        sent_x, sent_y, self.rest = kernel_call(
            expert_pairs_body,
            shapes,
            [self.keep, self.got],
            self.scalars,
            grid=(self.members,),
            in_specs=[whole, whole],
            out_specs=[group(2), group(2), group(4)],
            after=earlier,
            micros=6,
        )
        self.over_x = xor_permute(sent_x, "fsdp", 2)
        self.over_y = xor_permute(sent_y, "fsdp", 4)
        return (sent_x, sent_y)

    def arrived(self):
        return () if self.plain else (self.over_x, self.over_y)

    def second(self, *earlier):
        if self.plain:
            return ()
        one = shape_of(self.rest.shape[1:])
        sent_x, sent_y = kernel_call(
            expert_passed_body,
            [one, one],
            [self.rest, self.over_x, self.over_y],
            self.scalars,
            grid=(self.members,),
            in_specs=[self.group(2, 1), self.group(1), self.group(1)],
            out_specs=[self.single, self.single],
            after=earlier,
            micros=4,
        )
        self.then_x = xor_permute(sent_x, "fsdp", 2)
        self.then_y = xor_permute(sent_y, "fsdp", 4)
        return (sent_x, sent_y)

    def total(self):
        if self.plain:
            count = lax.axis_size("fsdp")
            both = jnp.stack([self.keep, self.send], axis=1).reshape((count,) + self.keep.shape[1:])
            both = jnp.take(both, lax.axis_index("fsdp") ^ jnp.arange(count), axis=0)
            share = lax.psum_scatter(both, "fsdp", scatter_dimension=0)
            spec = pl.BlockSpec((1,) + share.shape[1:], lambda e, m: (e, 0, 0))
            return ([share], [spec], lambda refs: refs[0][0].astype(f32))
        arrays = [self.rest, self.over_x, self.over_y, self.then_x, self.then_y]
        specs = [self.group(2), self.group(1, 1), self.group(1, 1), self.single, self.single]

        def rows_of(refs):
            rest, over_x, over_y, then_x, then_y = refs
            first = rest[0, 0].astype(f32) + over_x[0, 0].astype(f32) + then_y[0].astype(f32)
            second = rest[1, 0].astype(f32) + over_y[0, 0].astype(f32) + then_x[0].astype(f32)
            return jnp.concatenate([first, second], axis=0)

        return (arrays, specs, rows_of)


class Ringed:
    def __init__(self, block):
        self.plain = lax.axis_size("seq") != 4
        self.block = block
        self.half = block.shape[0] // 2
        if not self.plain:
            self.below = shift_permute(block, "seq", 1)
            self.above = shift_permute(block, "seq", -1)

    def near(self):
        return () if self.plain else (self.below, self.above)

    def forward(self):
        if self.plain:
            return ()
        self.far_first = shift_permute(self.below[: self.half], "seq", 1)
        self.far_second = shift_permute(self.above[self.half :], "seq", -1)
        return (self.far_first, self.far_second)

    def pieces(self):
        count = lax.axis_size("seq")
        if self.plain:
            whole = lax.all_gather(self.block, "seq", axis=0)
            whole = jnp.take(whole, (lax.axis_index("seq") - jnp.arange(count)) % count, axis=0)
            return [(k, 0, whole[k]) for k in range(count)]
        pieces = [(0, 0, self.block), (1, 0, self.below), (3, 0, self.above)]
        return pieces + [(2, 0, self.far_first), (2, self.half, self.far_second)]


def ring_gather(block):
    ring = Ringed(block)
    ring.forward()
    return ring.pieces()


def ring_shapes(count, rows, columns):
    if count != 4:
        return [shape_of((count, rows, columns))]
    half = rows // 2
    return [shape_of((r, columns)) for r in (rows, rows, rows, half, half)]


def ring_put(count, refs, k, rows, value):
    half = rows // 2
    width = value.shape[1]
    value = value.astype(bf16)
    if count != 4:
        refs[0][k, :, :width] = value
        return
    own, down, up, keep_down, keep_up = refs
    places = {
        0: ((own, 0), (own, half)),
        1: ((keep_down, 0), (down, half)),
        2: ((down, 0), (up, 0)),
        3: ((up, half), (keep_up, 0)),
    }
    for part, (ref, row) in enumerate(places[k]):
        ref[row : row + half, :width] = value[part * half : (part + 1) * half]


def ring_put_tail(count, refs, k, rows, value):
    half = rows // 2
    value = value.astype(bf16)
    if count != 4:
        refs[0][k, :, MODEL_WIDTH:] = value
        return
    own, down, up, keep_down, keep_up = refs
    places = {
        0: ((own, 0), (own, half)),
        1: ((keep_down, 0), (down, half)),
        2: ((down, 0), (up, 0)),
        3: ((up, half), (keep_up, 0)),
    }
    for part, (ref, row) in enumerate(places[k]):
        ref[row : row + half, MODEL_WIDTH:] = value[part * half : (part + 1) * half]


def ring_get(count, refs, k, rows):
    if count != 4:
        return refs[0][k]
    half = rows // 2
    own, down, up, keep_down, keep_up = refs
    if k == 0:
        return own[...]
    first, second = {
        1: ((keep_down, 0), (down, half)),
        2: ((down, 0), (up, 0)),
        3: ((up, half), (keep_up, 0)),
    }[k]
    return jnp.concatenate([ref[row : row + half, :] for ref, row in (first, second)], axis=0)


class RingSum:
    def __init__(self, arrays, *earlier):
        self.plain = lax.axis_size("seq") != 4
        self.arrays = list(arrays)
        self.sent = ()
        if not self.plain:
            own, down, up, keep_down, keep_up = self.arrays
            if earlier:
                down, up = tie(down, *earlier), tie(up, *earlier)
            self.from_above = shift_permute(down, "seq", -1)
            self.from_below = shift_permute(up, "seq", 1)

    def near(self):
        return () if self.plain else (self.from_above, self.from_below)

    def parts(self, *earlier):
        if self.plain:
            count = lax.axis_size("seq")
            whole = jnp.take(self.arrays[0], (lax.axis_index("seq") - jnp.arange(count)) % count, axis=0)
            return [lax.psum_scatter(whole, "seq", scatter_dimension=0)]
        own, down, up, keep_down, keep_up = self.arrays
        half = keep_down.shape[0]
        if earlier:
            self.from_above = tie(self.from_above, *earlier)
            self.from_below = tie(self.from_below, *earlier)
        then_down = (keep_down.astype(f32) + self.from_above[:half].astype(f32)).astype(bf16)
        then_up = (keep_up.astype(f32) + self.from_below[:half].astype(f32)).astype(bf16)
        self.sent = (then_down, then_up)
        last_above = shift_permute(then_down, "seq", -1)
        last_below = shift_permute(then_up, "seq", 1)
        return [own, self.from_above, self.from_below, last_above, last_below]


def ring_total(refs):
    if len(refs) == 1:
        return refs[0][...].astype(f32)
    own, above, below, last_above, last_below = [r[...].astype(f32) for r in refs]
    half = own.shape[0] // 2
    first = own[:half] + below[half:] + last_above
    second = own[half:] + above[half:] + last_below
    return jnp.concatenate([first, second], axis=0)


def block_value(pieces, refs, k):
    found = [(row, ref) for (kk, row, _), ref in zip(pieces, refs) if kk == k]
    found.sort(key=lambda entry: entry[0])
    if len(found) == 1:
        return found[0][1][...]
    return jnp.concatenate([ref[...] for _, ref in found], axis=0)


def block_lanes(pieces, refs, k, lanes):
    found = [(row, ref) for (kk, row, _), ref in zip(pieces, refs) if kk == k]
    found.sort(key=lambda entry: entry[0])
    if len(found) == 1:
        return found[0][1][:, lanes]
    return jnp.concatenate([ref[:, lanes] for _, ref in found], axis=0)


def rotate_tile(tile, cosine, sine):
    first = lanes_of(tile.shape) % HEAD_SIZE < HEAD_SIZE // 2
    turned = jnp.where(first, pltpu.roll(tile, LANES - HEAD_SIZE // 2, 1), pltpu.roll(tile, HEAD_SIZE // 2, 1))
    return tile * cosine + turned * sine


def rotate_tile_back(tile, cosine, sine):
    return rotate_tile(tile, cosine, -sine)


def qkv_body(pieces, meta, x_ref, cos_ref, sin_ref, *refs):
    shards = refs[: len(pieces)]
    wq_ref, wkv_ref, wo_ref, extra_ref, normed_ref, q_ref, kv_ref, columns = refs[len(pieces) :]
    shard_rows = MODEL_WIDTH // max(r + 1 for r, _, _ in pieces)
    for (r, row, value), ref in zip(pieces, shards):
        rows = value.shape[0]
        place = pl.ds(pl.multiple_of(meta[r] * shard_rows + row, rows), rows)
        wq_ref[place, :] = ref[:, :MODEL_WIDTH]
        wkv_ref[place, :] = ref[:, MODEL_WIDTH : 2 * MODEL_WIDTH]
        wo_ref[place, :] = ref[:, 2 * MODEL_WIDTH : 3 * MODEL_WIDTH]
        columns[place, :] = ref[:, 3 * MODEL_WIDTH :].astype(f32)
    extra_ref[...] = columns[...].T
    source = x_ref[...].astype(f32)
    scale_inv = lax.rsqrt(jnp.mean(source * source, axis=-1, keepdims=True) + epsilon)
    normed = (source * scale_inv * extra_ref[EXPERTS : EXPERTS + 1, :]).astype(bf16)
    normed_ref[...] = normed
    cosine, sine = cos_ref[...], sin_ref[...]
    low = lanes_of(cosine.shape) < HEAD_SIZE
    for j in range(MODEL_WIDTH // TILE):
        block = dot_nn(normed, wq_ref[:, j * TILE : (j + 1) * TILE])
        for i in range(TILE // LANES):
            at = j * TILE + i * LANES
            tile = block[:, i * LANES : (i + 1) * LANES]
            q_ref[:, at : at + LANES] = rotate_tile(tile, cosine, sine).astype(bf16)
    for j in range(MODEL_WIDTH // TILE):
        block = dot_nn(normed, wkv_ref[:, j * TILE : (j + 1) * TILE])
        for i in range(TILE // LANES):
            at = j * TILE + i * LANES
            tile = block[:, i * LANES : (i + 1) * LANES]
            tile = jnp.where(low, rotate_tile(tile, cosine, sine), tile).astype(bf16)
            kv_ref[:, at : at + LANES] = tile


def causal_scores(keys, pair, k):
    scores = dot_nt(keys, pair)
    if k == 0:
        rows = keys.shape[0]
        query = lanes_of(scores.shape) % rows
        scores = jnp.where(query >= lax.broadcasted_iota(jnp.int32, scores.shape, 0), scores, -jnp.inf)
    return scores


def query_pair(tile):
    low = lanes_of(tile.shape) < HEAD_SIZE
    tile = tile.astype(f32) * att_scale
    even = jnp.where(low, tile, 0.0)
    odd = jnp.where(low, pltpu.roll(tile, HEAD_SIZE, 1), 0.0)
    return jnp.concatenate([even, odd], axis=0).astype(bf16)


def attend_body(count, pieces, meta, q_ref, x_ref, wo_ref, extra_ref, *refs):
    blocks = refs[: len(pieces)]
    a_ref, lse_ref, h_ref, normed_ref = refs[len(pieces) :]
    rows = q_ref.shape[0]
    place = meta[0]

    def variant(seen):
        def group(g, carry):
            lanes = aligned(g * LANES, LANES)
            pair = query_pair(q_ref[:, lanes])
            keys = [block_lanes(pieces, blocks, k, lanes) for k in range(seen)]
            scores = [causal_scores(keys[k], pair, k) for k in range(seen)]
            top = functools.reduce(jnp.maximum, [jnp.max(s, axis=0, keepdims=True) for s in scores])
            weights = [jnp.exp(s - top) for s in scores]
            total = functools.reduce(jnp.add, [jnp.sum(w, axis=0, keepdims=True) for w in weights])
            summed = functools.reduce(jnp.add, [dot_tn(t, w.astype(bf16)) for w, t in zip(weights, keys)])
            summed = summed[HEAD_SIZE:] * (1.0 / total)
            both = jnp.concatenate([summed[:, :rows], summed[:, rows:]], axis=0)
            a_ref[:, lanes] = both.T.astype(bf16)
            lse_ref[pl.ds(g, 1), :] = top + jnp.log(total)
            return carry

        lax.fori_loop(0, KEY_VALUE_HEADS, group, 0)

    for seen in range(1, count + 1):
        pl.when(place == seen - 1)(functools.partial(variant, seen))
    resid = x_ref[...].astype(f32) + res_scale * dot_nn(a_ref[...], wo_ref[...])
    h_ref[...] = resid
    scale_inv = lax.rsqrt(jnp.mean(resid * resid, axis=-1, keepdims=True) + epsilon)
    normed_ref[...] = (resid * scale_inv * extra_ref[EXPERTS + 1 : EXPERTS + 2, :]).astype(bf16)


def softmax_over(picked, logits, axis):
    top = jnp.max(jnp.where(picked, logits, -jnp.inf), axis=axis, keepdims=True)
    raised = jnp.where(picked, jnp.exp(jnp.minimum(logits - top, 0.0)), 0.0)
    return raised / jnp.sum(raised, axis=axis, keepdims=True)


def experts_body(count, shards, pieces, start, members, last, meta, extra_ref, *refs):
    refs = list(refs)

    def take(number):
        taken = refs[:number]
        del refs[:number]
        return taken

    (weights,) = take(1)
    blocks, (told,) = take(len(pieces)), take(1)
    if start > 0:
        (part_g, part_m) = take(2)
    keep_ref, send_ref = take(2) if last else (take(1) + [None])
    ring_count = len(ring_shapes(count, TILE, WIDE)) if last else 1
    mix_refs, ring_refs = take(ring_count), take(ring_count)
    up_s, down_s, x_s, c_s, ge_s, a_s, gu_s, d_s, eg_s, gs_s, gup_s, gdown_s, gate_s, rank_s, gg_s = refs
    step = pl.program_id(0)
    local = EXPERTS // count
    up_rows, down_rows = MODEL_WIDTH // shards, FF // shards
    slots = count * CAP
    place = meta[shards]
    expert = place * local + start + step

    def absolute(k):
        return lax.rem(place - k + count, count)

    @pl.when(step == 0)
    def routing():
        router = extra_ref[:EXPERTS, :].astype(bf16)
        later = (
            lax.broadcasted_iota(jnp.int32, (TILE, TILE), 0) < lax.broadcasted_iota(jnp.int32, (TILE, TILE), 1)
        )
        later = jnp.where(later, 1.0, 0.0).astype(bf16)
        names = lax.broadcasted_iota(jnp.int32, (EXPERTS, TILE), 0).astype(f32)
        for k in range(count):
            named = told[absolute(k), :, MODEL_WIDTH:].astype(f32).T
            picked = names == named[0:1, :]
            for j in range(1, TOP):
                picked = jnp.logical_or(picked, names == named[j : j + 1, :])
            logits = dot_nt(router, block_value(pieces, blocks, k))
            gate_s[k] = softmax_over(picked, logits, 0)
            before = dot_nn(jnp.where(picked, 1.0, 0.0).astype(bf16), later)
            rank_s[k] = jnp.where(picked, before, -1.0)
        gg_s[...] = jnp.zeros_like(gg_s)

    for r in range(shards):
        up_s[r * up_rows : (r + 1) * up_rows, :] = weights[r, 0, :up_rows, :]
        down_s[r * down_rows : (r + 1) * down_rows, :] = weights[r, 0, up_rows:, :]

    wanted = lax.broadcasted_iota(jnp.int32, (CAP, TILE), 0).astype(f32)
    held = aligned(step * CAP, CAP)
    gates = []
    for k in range(count):
        rank = rank_s[k, pl.ds(expert, 1), :]
        gate = gate_s[k, pl.ds(expert, 1), :]
        hit = wanted == rank
        chosen = jnp.where(hit, 1.0, 0.0).astype(bf16)
        d_s[k, held, :] = chosen
        here = slice(k * CAP, (k + 1) * CAP)
        x_s[here, :] = dot_nn(chosen, block_value(pieces, blocks, k)).astype(bf16)
        upstream = dot_nn(chosen, told[absolute(k), :, :MODEL_WIDTH])
        own_gate = jnp.sum(jnp.where(hit, gate, 0.0), axis=1, keepdims=True)
        gates.append(own_gate)
        c_s[here, :] = upstream.astype(bf16)
        ge_s[here, :] = (own_gate * (res_scale * upstream)).astype(bf16)

    for j in range(FF // TILE):
        left, right = slice(j * TILE, (j + 1) * TILE), slice(FF + j * TILE, FF + (j + 1) * TILE)
        gate_part = dot_nn(x_s[...], up_s[:, left])
        up_part = dot_nn(x_s[...], up_s[:, right])
        hidden_grad = dot_nt(ge_s[...], down_s[left, :])
        sigmoid_gate = jax.nn.sigmoid(gate_part)
        swish = gate_part * sigmoid_gate
        a_s[:, left] = (swish * up_part).astype(bf16)
        slope = sigmoid_gate * (1.0 + gate_part * (1.0 - sigmoid_gate))
        gu_s[:, left] = (hidden_grad * up_part * slope).astype(bf16)
        gu_s[:, right] = (hidden_grad * swish).astype(bf16)

    gate_grad = jnp.zeros((slots, 1), f32)
    for j in range(MODEL_WIDTH // TILE):
        columns = slice(j * TILE, (j + 1) * TILE)
        produced = dot_nn(a_s[...], down_s[:, columns]).astype(bf16).astype(f32)
        gate_grad += jnp.sum(res_scale * c_s[:, columns].astype(f32) * produced, axis=1, keepdims=True)
        input_grad = dot_nt(gu_s[...], up_s[columns, :]).astype(bf16)
        for k in range(count):
            here = slice(k * CAP, (k + 1) * CAP)
            eg_s[k, held, columns] = (gates[k] * produced[here]).astype(bf16)
            gs_s[k, held, columns] = input_grad[here]
    for k in range(count):
        hit = wanted == rank_s[k, pl.ds(expert, 1), :]
        spread = jnp.where(hit, gate_grad[k * CAP : (k + 1) * CAP], 0.0)
        gg_s[k, pl.ds(expert, 1), :] = jnp.sum(spread, axis=0, keepdims=True)

    for j in range(FF // TILE):
        rows = slice(j * TILE, (j + 1) * TILE)
        gdown_s[rows, :] = dot_tn(a_s[:, rows], ge_s[...]).astype(bf16)
    for j in range(MODEL_WIDTH // TILE):
        rows = slice(j * TILE, (j + 1) * TILE)
        gup_s[rows, :] = dot_tn(x_s[:, rows], gu_s[...]).astype(bf16)
    for r in range(shards):
        if last:
            ref, at, owner = (send_ref if r % 2 else keep_ref), r // 2, meta[r]
        else:
            ref, at, owner = keep_ref, r, r
        ref[at, 0, :up_rows, :] = gup_s[aligned(owner * up_rows, up_rows), :]
        ref[at, 0, up_rows:, :] = gdown_s[aligned(owner * down_rows, down_rows), :]

    @pl.when(step == members - 1)
    def combine():
        for k in range(count):
            spread = d_s[k]
            mixed = dot_tn(spread, eg_s[k])
            summed = dot_tn(spread, gs_s[k])
            exact = gg_s[k]
            rounded = exact.astype(bf16).astype(f32)
            rest = jnp.zeros((LANES - 2 * EXPERTS, TILE), f32)
            tail = jnp.concatenate([rounded, exact - rounded, rest], axis=0).T
            if start > 0:
                mixed += part_m[k].astype(f32)
                summed += part_g[k, :, :MODEL_WIDTH].astype(f32)
                tail += part_g[k, :, MODEL_WIDTH:].astype(f32)
            if last:
                ring_put(count, mix_refs, k, TILE, mixed)
                ring_put(count, ring_refs, k, TILE, summed)
                ring_put_tail(count, ring_refs, k, TILE, tail)
            else:
                mix_refs[0][k] = mixed.astype(bf16)
                ring_refs[0][k, :, :MODEL_WIDTH] = summed.astype(bf16)
                ring_refs[0][k, :, MODEL_WIDTH:] = tail.astype(bf16)


def backward_body(count, pieces, summed, meta, routes_ref, normed_ref, extra_ref, h_ref, c_ref, a_ref, wo_ref, q_ref, lse_ref, cos_ref, sin_ref, *refs):
    sums = refs[:summed]
    blocks = refs[summed : summed + len(pieces)]
    outs = refs[summed + len(pieces) :]
    gh_ref, go_ref, gpq_ref, gex_ref, gain_ref = outs[:5]
    ring_refs, ga_s = outs[5:-1], outs[-1]
    rows = q_ref.shape[0]
    place = meta[0]
    normed = normed_ref[...]
    total = ring_total(sums)
    normed_grad, tail = total[:, :MODEL_WIDTH], total[:, MODEL_WIDTH:]
    names = lanes_of((rows, LANES))
    named = routes_ref[...]
    picked = names == named[:, 0:1]
    for j in range(1, TOP):
        picked = jnp.logical_or(picked, names == named[:, j : j + 1])
    row_names = lax.broadcasted_iota(jnp.int32, (LANES, MODEL_WIDTH), 0)
    router = jnp.where(row_names < EXPERTS, extra_ref[...], 0.0).astype(bf16)
    gate = softmax_over(picked, dot_nt(normed, router), 1)
    gate_grad = jnp.where(picked, tail + pltpu.roll(tail, LANES - EXPERTS, 1), 0.0)
    inner = jnp.sum(gate * gate_grad, axis=1, keepdims=True)
    logit_grad = (gate * (gate_grad - inner)).astype(bf16)
    gex_ref[...] = dot_tn(normed, logit_grad)
    normed_grad += dot_nn(logit_grad, router)
    resid = h_ref[...]
    scale_inv = lax.rsqrt(jnp.mean(resid * resid, axis=-1, keepdims=True) + epsilon)
    hat = resid * scale_inv
    gain_ref[...] = jnp.broadcast_to(jnp.sum(normed_grad * hat, axis=0, keepdims=True), gain_ref.shape)
    scaled = normed_grad * extra_ref[EXPERTS + 1 : EXPERTS + 2, :]
    part = scale_inv * (scaled - hat * jnp.mean(scaled * hat, axis=-1, keepdims=True))
    resid_grad = c_ref[...].astype(f32) + part
    gh_ref[...] = resid_grad
    go = (res_scale * resid_grad).astype(bf16)
    go_ref[...] = go
    ga_s[...] = dot_nt(go, wo_ref[...]).astype(bf16)
    cosine, sine = cos_ref[...], sin_ref[...]
    low = lanes_of((rows, LANES)) < HEAD_SIZE

    def variant(seen):
        def group(g, carry):
            lanes = aligned(g * LANES, LANES)
            pair = query_pair(q_ref[:, lanes])
            upstream = ga_s[:, lanes].astype(f32)
            product = (upstream * a_ref[:, lanes].astype(f32)).T
            delta = jnp.concatenate(
                [
                    jnp.sum(product[:HEAD_SIZE], axis=0, keepdims=True),
                    jnp.sum(product[HEAD_SIZE:], axis=0, keepdims=True),
                ],
                axis=1,
            )
            logsum = lse_ref[pl.ds(g, 1), :]
            high_pair = jnp.concatenate(
                [jnp.where(low, 0.0, pltpu.roll(upstream, HEAD_SIZE, 1)), jnp.where(low, 0.0, upstream)], axis=0
            ).astype(bf16)
            query_grad = jnp.zeros((LANES, 2 * rows), f32)
            for k in range(seen):
                keys = block_lanes(pieces, blocks, k, lanes)
                weights = jnp.exp(causal_scores(keys, pair, k) - logsum)
                score_grad = (weights * (dot_nt(keys, high_pair) - delta)).astype(bf16)
                query_grad += dot_tn(keys, score_grad)
                back = dot_nn(score_grad, pair) + dot_nn(weights.astype(bf16), high_pair)
                put_lanes(k, lanes, back)
            query_grad = query_grad[:HEAD_SIZE] * att_scale
            tile = jnp.concatenate([query_grad[:, :rows], query_grad[:, rows:]], axis=0).T
            tile = tile.astype(bf16).astype(f32)
            gpq_ref[:, lanes] = rotate_tile_back(tile, cosine, sine).astype(bf16)
            return carry

        lax.fori_loop(0, KEY_VALUE_HEADS, group, 0)
        for k in range(seen, count):
            ring_put(count, ring_refs, k, rows, jnp.zeros((rows, MODEL_WIDTH), f32))

    def put_lanes(k, lanes, value):
        views = [r.at[..., lanes] for r in ring_refs]
        ring_put(count, views, k, rows, value)

    for seen in range(1, count + 1):
        pl.when(place == seen - 1)(functools.partial(variant, seen))


def store_sets(shards, meta, source, sets, columns):
    rows = MODEL_WIDTH // shards
    for r in range(shards):
        sets[r % 2][r // 2, :, columns] = source[aligned(meta[r] * rows, rows), :].astype(bf16)


def weights_body(count, shards, pieces, meta, a_ref, go_ref, gpq_ref, gex_ref, gain_ref, wq_ref, wkv_ref, extra_ref, cos_ref, sin_ref, *refs):
    blocks, parts = refs[: len(pieces)], refs[len(pieces) : -6]
    *sets, gp_s, normed_s, full_s, extra_s = refs[-6:]
    rows = gpq_ref.shape[0]
    low = lanes_of((rows, LANES)) < HEAD_SIZE
    for k in range(count):
        here = slice(k * rows, (k + 1) * rows)
        normed_s[here, :] = block_value(pieces, blocks, k)
        cosine, sine = cos_ref[k], sin_ref[k]
        part = ring_get(count, parts, k, rows).astype(f32)
        for j in range(MODEL_WIDTH // LANES):
            lanes = slice(j * LANES, (j + 1) * LANES)
            tile = part[:, lanes]
            gp_s[here, lanes] = jnp.where(low, rotate_tile_back(tile, cosine, sine), tile).astype(bf16)
    full_s[...] = dot_tn(normed_s[:rows, :], gpq_ref[...]).astype(bf16)
    store_sets(shards, meta, full_s, sets, slice(0, MODEL_WIDTH))
    full_s[...] = dot_tn(normed_s[...], gp_s[...]).astype(bf16)
    store_sets(shards, meta, full_s, sets, slice(MODEL_WIDTH, 2 * MODEL_WIDTH))
    full_s[...] = dot_tn(a_ref[...], go_ref[...]).astype(bf16)
    store_sets(shards, meta, full_s, sets, slice(2 * MODEL_WIDTH, 3 * MODEL_WIDTH))
    gain_grad = jnp.sum(dot_nt(gpq_ref[...], wq_ref[...]) * normed_s[:rows, :].astype(f32), axis=0, keepdims=True)
    for k in range(count):
        here = slice(k * rows, (k + 1) * rows)
        product = dot_nt(gp_s[here, :], wkv_ref[...]) * normed_s[here, :].astype(f32)
        gain_grad += jnp.sum(product, axis=0, keepdims=True)
    gain_grad = gain_grad / extra_ref[EXPERTS : EXPERTS + 1, :]
    row_names = lax.broadcasted_iota(jnp.int32, (LANES, MODEL_WIDTH), 0)
    gains = jnp.where(row_names == EXPERTS, gain_grad, jnp.where(row_names == EXPERTS + 1, gain_ref[0:1, :], 0.0))
    extra_s[...] = gex_ref[...] + gains.T
    store_sets(shards, meta, extra_s, sets, slice(3 * MODEL_WIDTH, 3 * MODEL_WIDTH + LANES))


def tokens_body(meta, x_ref, gpq_ref, wq_ref, wkv_ref, extra_ref, gh_ref, cos_ref, sin_ref, *refs):
    *sums, grad_ref, gpkv_s = refs
    total = ring_total(sums).astype(bf16).astype(f32)
    cosine, sine = cos_ref[...], sin_ref[...]
    low = lanes_of(cosine.shape) < HEAD_SIZE
    for j in range(MODEL_WIDTH // LANES):
        lanes = slice(j * LANES, (j + 1) * LANES)
        tile = total[:, lanes]
        gpkv_s[:, lanes] = jnp.where(low, rotate_tile_back(tile, cosine, sine), tile).astype(bf16)
    normed_grad = dot_nt(gpq_ref[...], wq_ref[...]) + dot_nt(gpkv_s[...], wkv_ref[...])
    source = x_ref[...].astype(f32)
    scale_inv = lax.rsqrt(jnp.mean(source * source, axis=-1, keepdims=True) + epsilon)
    hat = source * scale_inv
    scaled = normed_grad * extra_ref[EXPERTS : EXPERTS + 1, :]
    part = scale_inv * (scaled - hat * jnp.mean(scaled * hat, axis=-1, keepdims=True))
    grad_ref[...] = gh_ref[...] + part


def dense_update_body(count, rates, meta, *refs):
    quarters, refs = refs[:count], refs[count:]
    ins, outs, total_s = refs[:12], refs[12:28], refs[28]
    rows = quarters[0].shape[0]
    for k in range(count):
        at = lax.rem(meta[0] - k + count, count) * rows
        total_s[pl.ds(pl.multiple_of(at, rows), rows), :] = quarters[k][...].astype(f32)
    rest = total_s[:, 3 * MODEL_WIDTH :].T
    out = total_s[:, 2 * MODEL_WIDTH : 3 * MODEL_WIDTH]
    gradients = (rest[EXPERTS : EXPERTS + 2], total_s[:, : 2 * MODEL_WIDTH], out, rest[:EXPERTS])
    for i, (gradient, rate) in enumerate(zip(gradients, rates)):
        weight, first, second = [r[...] for r in ins[3 * i : 3 * i + 3]]
        for ref, value in zip(outs[4 * i : 4 * i + 4], (gradient, *adam_update(weight, gradient, first, second, rate))):
            ref[...] = value


def output_body(meta, h_ref, *refs):
    refs[-1][...] = (h_ref[...] + res_scale * ring_total(refs[:-1])).astype(bf16)


def experts_update_body(rates, rows, parts, rows_of, meta, *refs):
    gradient = rows_of(refs[:parts])
    ins, outs = refs[parts : parts + 6], refs[-8:]
    for i, rate in enumerate(rates):
        own = gradient[: rows[0]] if i == 0 else gradient[rows[0] :]
        weight, first, second = [r[0] for r in ins[3 * i : 3 * i + 3]]
        fresh, first, second = adam_update(weight, own, first, second, rate)
        for ref, value in zip(outs[4 * i : 4 * i + 4], (own, fresh, first, second)):
            ref[0] = value


def experts_update(start, share, arrays, rates, earlier, scalars, after=()):
    shares, share_specs, rows_of = share
    members = shares[0].shape[-3]
    rows = (arrays[0].shape[1], arrays[3].shape[1])

    def spec(a):
        return pl.BlockSpec((1,) + a.shape[1:], lambda e, m: (start + e, 0, 0))

    outs = [shape_of(a.shape, f32) for a in (arrays[0],) * 4 + (arrays[3],) * 4]
    in_specs = share_specs + [spec(a) for a in arrays]
    ins = shares + list(arrays)
    aliases = {}
    if earlier is not None:
        aliases = {1 + len(after) + len(ins) + i: i for i in range(8)}
        in_specs += [pl.BlockSpec(memory_space=pl.ANY)] * 8
        ins += list(earlier)
    return kernel_call(
        functools.partial(experts_update_body, rates, rows, len(shares), rows_of),
        outs,
        ins,
        scalars,
        grid=(members,),
        in_specs=in_specs,
        out_specs=[spec(a) for a in outs],
        micros=8,
        after=after,
        aliases=aliases,
    )


def angle_tables(rows, offsets):
    position = (offsets[:, None] + jnp.arange(rows)[None, :]).reshape(-1).astype(f32)
    frequency = 10000.0 ** (-(jnp.arange(HEAD_SIZE // 2).astype(f32) * 2.0 / HEAD_SIZE))
    angles = position[:, None] * frequency[None, :]
    cosine, sine = jnp.cos(angles), jnp.sin(angles)
    shape = (offsets.shape[0], rows, LANES)
    cosine = jnp.concatenate([cosine] * 4, axis=1).reshape(shape)
    return (cosine, jnp.concatenate([-sine, sine] * 2, axis=1).reshape(shape))


def shards_step(
    tokens,
    routes,
    cotangent,
    norm_gains,
    qkv_weight,
    out_weight,
    router_weight,
    expert_up,
    expert_down,
    mean_gains,
    square_gains,
    mean_qkv,
    square_qkv,
    mean_out,
    square_out,
    mean_router,
    square_router,
    mean_up,
    square_up,
    mean_down,
    square_down,
):
    rows = tokens.shape[1]
    count = lax.axis_size("seq")
    shards = lax.axis_size("fsdp")
    shard_rows = MODEL_WIDTH // shards
    local = EXPERTS // count
    early_experts = (5 * local + 4) // 8
    chunks = [(0, early_experts), (early_experts, local - early_experts)]
    place = lax.axis_index("seq").astype(jnp.int32)
    owners = (lax.axis_index("fsdp") ^ jnp.arange(shards)).astype(jnp.int32)
    owner_meta = jnp.concatenate([owners, place[None]])
    place_meta = place[None]
    x, c, own_routes = tokens[0], cotangent[0], routes[0]

    blank = jnp.zeros((shard_rows, LANES - EXPERTS - 2), f32)
    dense = jnp.concatenate([qkv_weight, out_weight, router_weight, norm_gains.T, blank], axis=1).astype(bf16)
    listed = jnp.zeros((rows, LANES), f32).at[:, :TOP].set(own_routes.astype(f32))
    dense_shards = Gathered(dense)
    told = lax.all_gather(jnp.concatenate([c, listed.astype(bf16)], axis=1), "seq", axis=0)
    dense_shards.forward()
    early = dense_shards.arrived()
    dense_pieces = dense_shards.pieces()
    expert_weights = []
    for start, members in chunks:
        mine = slice(start, start + members)
        packed = jnp.concatenate([expert_up[mine], expert_down[mine]], axis=1).astype(bf16)
        expert_weights.append(lax.all_gather(tie(packed, *early), "fsdp", axis=0))
    cosines, sines = angle_tables(rows, jnp.maximum(place - jnp.arange(count), 0) * rows)
    cosine, sine = cosines[0], sines[0]

    square = shape_of((MODEL_WIDTH, MODEL_WIDTH))
    wide = shape_of((rows, MODEL_WIDTH))
    wide_f = shape_of((rows, MODEL_WIDTH), f32)
    extra_shape = shape_of((LANES, MODEL_WIDTH), f32)
    unit = 2 * rows * MODEL_WIDTH * MODEL_WIDTH
    wq, wkv, wo, extra, normed_one, q, kv = kernel_call(
        functools.partial(qkv_body, dense_pieces),
        [square, square, square, extra_shape, wide, wide, wide],
        [x, cosine, sine] + [a for _, _, a in dense_pieces],
        owner_meta,
        scratch=[pltpu.VMEM((MODEL_WIDTH, LANES), f32)],
        micros=8,
    )
    kv_pieces = ring_gather(kv)
    attended, logsum, resid, normed_two = kernel_call(
        functools.partial(attend_body, count, kv_pieces),
        [wide, shape_of((KEY_VALUE_HEADS, 2 * rows), f32), wide_f, wide],
        [q, x, wo, extra] + [a for _, _, a in kv_pieces],
        place_meta,
        micros=12,
    )
    two_pieces = ring_gather(normed_two)

    slots = count * CAP
    packed_rows = (MODEL_WIDTH + FF) // shards
    part_g = part_m = None
    waited = (cosines, sines)
    normed_ring = Ringed(tie(normed_one, *[a for _, _, a in two_pieces[1:]]))
    for i, (start, members) in enumerate(chunks):
        last = i == len(chunks) - 1
        ins = [extra, expert_weights[i]] + [a for _, _, a in two_pieces] + [told]

        def still(a):
            return pl.BlockSpec(a.shape, functools.partial(lambda n, e, m: (0,) * n, a.ndim), pipeline_mode=pl.Buffered(1))

        all_spec = pl.BlockSpec((shards, 1, packed_rows, MODEL_WIDTH), lambda e, m: (0, e, 0, 0))
        set_spec = pl.BlockSpec((shards // 2, 1, packed_rows, MODEL_WIDTH), lambda e, m: (0, e, 0, 0))
        sets = [shape_of((shards // 2, members, packed_rows, MODEL_WIDTH))] * 2
        set_specs = [set_spec] * 2
        if not last:
            sets, set_specs = [shape_of((shards, members, packed_rows, MODEL_WIDTH))], [all_spec]
        in_specs = [still(extra), all_spec] + [still(a) for a in ins[2:]]
        if i > 0:
            ins += [part_g, part_m]
            in_specs += [still(part_g), still(part_m)]
        ring = ring_shapes if last else lambda n, r, w: [shape_of((n, r, w))]
        ring_count = len(ring(count, rows, WIDE))
        outs = sets + ring(count, rows, MODEL_WIDTH) + ring(count, rows, WIDE)
        out_specs = set_specs + [still(a) for a in outs[len(sets) :]]
        scratch = [
            pltpu.VMEM((MODEL_WIDTH, 2 * FF), bf16),
            pltpu.VMEM((FF, MODEL_WIDTH), bf16),
            pltpu.VMEM((slots, MODEL_WIDTH), bf16),
            pltpu.VMEM((slots, MODEL_WIDTH), bf16),
            pltpu.VMEM((slots, MODEL_WIDTH), bf16),
            pltpu.VMEM((slots, FF), bf16),
            pltpu.VMEM((slots, 2 * FF), bf16),
            pltpu.VMEM((count, members * CAP, rows), bf16),
            pltpu.VMEM((count, members * CAP, MODEL_WIDTH), bf16),
            pltpu.VMEM((count, members * CAP, MODEL_WIDTH), bf16),
            pltpu.VMEM((MODEL_WIDTH, 2 * FF), bf16),
            pltpu.VMEM((FF, MODEL_WIDTH), bf16),
            pltpu.VMEM((count, EXPERTS, rows), f32),
            pltpu.VMEM((count, EXPERTS, rows), f32),
            pltpu.VMEM((count, EXPERTS, rows), f32),
        ]
        results = kernel_call(
            functools.partial(experts_body, count, shards, two_pieces, start, members, last),
            outs,
            ins,
            owner_meta,
            scratch=scratch,
            grid=(members,),
            in_specs=in_specs,
            out_specs=out_specs,
            micros=8 * members,
            after=waited,
        )
        beside = normed_ring.forward() if last else normed_ring.near()
        results = list(results)
        first_part = len(sets)
        part_m, part_g = results[first_part], results[first_part + ring_count]
        mix_parts, ring_parts = results[first_part : first_part + ring_count], results[first_part + ring_count :]
        if not last:
            share = tie(results[0], *beside) if beside else results[0]
            share = lax.psum_scatter(share, "fsdp", scatter_dimension=0)

    two_ring = RingSum(ring_parts, *beside)
    late_sum = ScatteredExperts(tie(results[1], *beside, *two_ring.near()), results[0], place_meta)
    two_sums = two_ring.parts()
    sent = late_sum.first(*two_ring.sent)
    mixing = RingSum(mix_parts, *two_sums[3:], *sent)
    ring = ring_shapes(count, rows, MODEL_WIDTH)
    results = kernel_call(
        functools.partial(backward_body, count, kv_pieces, len(two_sums)),
        [wide_f, wide, wide, shape_of((MODEL_WIDTH, LANES), f32), shape_of((8, MODEL_WIDTH), f32)] + ring,
        [own_routes, normed_two, extra, resid, c, attended, wo, q, logsum, cosine, sine]
        + list(two_sums)
        + [a for _, _, a in kv_pieces],
        place_meta,
        scratch=[pltpu.VMEM((rows, MODEL_WIDTH), bf16)],
        micros=22,
    )
    resid_grad, go, gpq, router_grad, gain_grad = results[:5]
    mix_sums = mixing.parts()
    normed_pieces = normed_ring.pieces()
    dense_set = shape_of((shards // 2, shard_rows, 3 * MODEL_WIDTH + LANES))
    keep, send = kernel_call(
        functools.partial(weights_body, count, shards, normed_pieces),
        [dense_set] * 2,
        [attended, go, gpq, router_grad, gain_grad, wq, wkv, extra, cosines, sines]
        + [a for _, _, a in normed_pieces]
        + list(results[5:]),
        owner_meta,
        scratch=[
            pltpu.VMEM((count * rows, MODEL_WIDTH), bf16),
            pltpu.VMEM((count * rows, MODEL_WIDTH), bf16),
            pltpu.VMEM((MODEL_WIDTH, MODEL_WIDTH), bf16),
            pltpu.VMEM((MODEL_WIDTH, LANES), f32),
        ],
        after=mixing.near() + late_sum.arrived(),
        micros=12,
    )
    dense_sum = Scattered(place_meta)
    dense_sum.add(send, keep, *mix_sums[3:])
    rates = (learn_rates[4], learn_rates[5])
    experts = (expert_up, mean_up, square_up, expert_down, mean_down, square_down)
    sent = dense_sum.first()
    kv_ring = RingSum(results[5:], *mix_sums[3:])
    kv_sums = kv_ring.parts(*sent)
    spec = pl.BlockSpec((1,) + share.shape[1:], lambda e, m: (e, 0, 0))
    total = ([share], [spec], lambda refs: refs[0][0].astype(f32))
    dense_sum.second()
    own = dense_sum.total(*kv_sums[3:])
    updated = experts_update(chunks[0][0], total, experts, rates, None, place_meta, (own,))
    late_sum.second(own)
    quarters = own.reshape((count, shard_rows // count, own.shape[1]))
    quarters = lax.all_to_all(quarters, "seq", split_axis=0, concat_axis=0, tiled=True)
    (tokens_grad,) = kernel_call(
        tokens_body,
        [wide_f],
        [x, gpq, wq, wkv, extra, resid_grad, cosine, sine] + list(kv_sums),
        place_meta,
        scratch=[pltpu.VMEM((rows, MODEL_WIDTH), bf16)],
        after=(own,),
        micros=6,
    )
    (output,) = kernel_call(output_body, [wide], [resid] + mix_sums, place_meta, after=(own,), micros=3)
    quarter = jnp.sum(tie(quarters, tokens_grad, output, updated[0]).astype(f32), axis=0).astype(bf16)
    tokens_grad, output = tokens_grad[None], output[None]
    quarters = [quarter] + [shift_permute(quarter, "seq", k) for k in range(1, count)]
    updated = experts_update(chunks[1][0], late_sum.total(), experts, rates, updated, place_meta, (quarter,))
    dense_ins = [norm_gains, mean_gains, square_gains, qkv_weight, mean_qkv, square_qkv]
    dense_ins += [out_weight, mean_out, square_out, router_weight.T, mean_router.T, square_router.T]
    dense_outs = kernel_call(
        functools.partial(dense_update_body, count, learn_rates[:4]),
        [shape_of(a.shape, f32) for a in dense_ins[::3] for _ in range(4)],
        quarters + dense_ins,
        place_meta,
        scratch=[pltpu.VMEM((shard_rows, 3 * MODEL_WIDTH + LANES), f32)],
        after=(updated[0],),
        micros=5,
    )
    shard_gains, fresh_gains, momentum_gains, variance_gains = dense_outs[:4]
    shard_qkv, fresh_qkv, momentum_qkv, variance_qkv = dense_outs[4:8]
    shard_out, fresh_out, momentum_out, variance_out = dense_outs[8:12]
    shard_router, fresh_router, momentum_router, variance_router = [a.T for a in dense_outs[12:]]
    shard_up, fresh_up, momentum_up, variance_up = updated[:4]
    shard_down, fresh_down, momentum_down, variance_down = updated[4:]
    return (
        output,
        tokens_grad,
        shard_gains,
        shard_qkv,
        shard_out,
        shard_router,
        shard_up,
        shard_down,
        fresh_gains,
        fresh_qkv,
        fresh_out,
        fresh_router,
        fresh_up,
        fresh_down,
        momentum_gains,
        momentum_qkv,
        momentum_out,
        momentum_router,
        momentum_up,
        momentum_down,
        variance_gains,
        variance_qkv,
        variance_out,
        variance_router,
        variance_up,
        variance_down,
    )


def solution(mesh):
    block = P("fsdp", "seq", None)
    gains, dense, experts = P(None, "fsdp"), P("fsdp", None), P("seq", "fsdp", None)
    weights = (gains, dense, dense, dense, experts, experts)
    moments = tuple(s for spec in weights for s in (spec, spec))
    return jax.shard_map(
        shards_step,
        mesh=mesh,
        in_specs=(block, block, block) + weights + moments,
        out_specs=(block, block) + weights * 4,
        check_vma=False,
    )
```

time: 621 us -> 484 us (0.78)
  the two profiles are of different devices: /device:TPU:0 before, /device:TPU:12 now
where the time goes in v2:
time: 484 us; the launch traced here: 475 us
  waiting for transfers between devices  182 us (38%)
  Pallas kernels  173 us (36%)
  starting transfers between devices  54.1 us (11%)
  local copies, waits for them, and re-layouts  28 us (6%)
  other arithmetic  22.4 us (5%)
  between operations  14.9 us (3%)
    pallas_call x16, Pallas kernels, kernel_call(): pl.pallas_call(ordered_body, out_shape=outs, grid_spec=pltpu.PrefetchScal...  173 us
    ppermute x27, waiting for transfers between devices, shift_permute(): lax.ppermute(value, axis, [(i, (i + step) % size) for i in range(size)])  127 us
    ppermute x19, waiting for transfers between devices, xor_permute(): lax.ppermute(value, axis, [(i, i ^ mask) for i in range(lax.axis_size(axi...  45.6 us
    ppermute x27, starting transfers between devices, shift_permute(): lax.ppermute(value, axis, [(i, (i + step) % size) for i in range(size)])  36.3 us
    unnamed x128, local copies, waits for them, and re-layouts  23.5 us
    ppermute x19, starting transfers between devices, xor_permute(): lax.ppermute(value, axis, [(i, i ^ mask) for i in range(lax.axis_size(axi...  13.8 us
  transfers between devices with their start and end apart: 51, of which 28 were waited for; matrix products, arithmetic and copies ran while one was open for 5% of the time, Pallas kernels for 35%

profile of v2, /device:TPU:12, one launch (start us, length us, event | category | flops | bytes accessed | tf_op | source)
XLA Modules:
  0.0 474.6 jit_solution(9726467361504310795)
XLA Ops:
  15.5 18.3 %collective-permute-done.1.refs_0_ = bf16[128,3200]{1,0:T(8,128)(2,1)S(1)} collective-permute-done((bf16[128,3200]{1,0:T(8,128)(2,1)}, bf16[128,3200]{1,0:T(8,128)(2,1)S(1)}, u32[]{:S(2)}, u32[]{:S(2)}) %collective-permute-start.1) | collective-permute-done | bytes 819232 | tf_op jit(solution)/shard_map/ppermute | solution.py:107
  58.5 8.3 %shard_map.406 = (bf16[1024,1024]{1,0:T(8,128)(2,1)}, bf16[1024,1024]{1,0:T(8,128)(2,1)}, bf16[1024,1024]{1,0:T(8,128)(2,1)}, f32[128,1024]{1,0:T(8,128)}, bf16[...) custom-call(s32[9]{0:T(128)} %pad_add_fusion.meta, bf16[256,1024]{1,0:T(8,128)(2,1)} %bitcast.36, ...), custom_call_target="tpu_custom_call" | custom-call | flops 8000000000 | bytes 8000000 | tf_op jit(solution)/shard_map/pallas_call | solution.py:75
  68.9 13.0 %collective-permute-done.9.refs_5_.refs_17_ = bf16[256,1024]{1,0:T(8,128)(2,1)S(1)} collective-permute-done((bf16[256,1024]{1,0:T(8,128)(2,1)}, bf16[256,1024]{1,0:T(8,128)(2,1)S(1)}, u32[]{:S(2)}, u32[]{:S(2)}) %collective-permute-start.9) | collective-permute-done | bytes 524320 | tf_op jit(solution)/shard_map/ppermute | solution.py:112
  83.4 10.4 %collective-permute-done.10.refs_6_.refs_18_ = bf16[256,1024]{1,0:T(8,128)(2,1)S(1)} collective-permute-done((bf16[256,1024]{1,0:T(8,128)(2,1)}, bf16[256,1024]{1,0:T(8,128)(2,1)S(1)}, u32[]{:S(2)}, u32[]{:S(2)}) %collective-permute-start.10) | collective-permute-done | bytes 524320 | tf_op jit(solution)/shard_map/ppermute | solution.py:112
  98.8 5.9 %collective-permute-done.12.refs_8_.refs_20_ = bf16[128,1024]{1,0:T(8,128)(2,1)S(1)} collective-permute-done((bf16[128,1024]{1,0:T(8,128)(2,1)S(1)}, bf16[128,1024]{1,0:T(8,128)(2,1)S(1)}, u32[]{:S(2)}, u32[]{:S(2)}) %collective-permute-start.12) | collective-permute-done | bytes 262176 | tf_op jit(solution)/shard_map/ppermute | solution.py:112
  105.4 10.6 %shard_map.407 = (bf16[256,1024]{1,0:T(8,128)(2,1)}, f32[8,512]{1,0:T(8,128)}, f32[256,1024]{1,0:T(8,128)}, bf16[256,1024]{1,0:T(8,128)(2,1)}) custom-call(s32[1]{0:T(128)} %bitcast.meta, bf16[256,1024]{1,0:T(8,128)(2,1)} %get-tuple-element.118.refs_0_.refs_7_, bf16[256,1024]{1,0:T(8,128)(2,1)} %bitcast.37, ...), custom_call_target="tpu_custom_call" | custom-call | flops 12000000000 | bytes 12000000 | tf_op jit(solution)/shard_map/pallas_call | solution.py:75
  119.0 21.9 %collective-permute-done.13.refs_5_.refs_1_ = bf16[256,1024]{1,0:T(8,128)(2,1)S(1)} collective-permute-done((bf16[256,1024]{1,0:T(8,128)(2,1)}, bf16[256,1024]{1,0:T(8,128)(2,1)S(1)}, u32[]{:S(2)}, u32[]{:S(2)}) %collective-permute-start.13) | collective-permute-done | bytes 524320 | tf_op jit(solution)/shard_map/ppermute | solution.py:112
  160.0 36.0 %shard_map.410 = (bf16[8,5,192,1024]{3,2,1,0:T(8,128)(2,1)}, bf16[4,256,1024]{2,1,0:T(8,128)(2,1)}, bf16[4,256,1152]{2,1,0:T(8,128)(2,1)}) custom-call(s32[9]{0:T(128)} %pad_add_fusion.meta, f32[4,256,128]{2,1,0:T(8,128)} %get-tuple-element.208.refs_0_.refs_12_, f32[4,256,128]{2,1,0:T(8,128)} %get-tuple-element.209.refs_1_.refs_13_, ...), custom_call_target="tpu_custom_call" | custom-call | flops 40000000000 | bytes 40000000 | tf_op jit(solution)/shard_map/pallas_call | solution.py:75
  201.3 9.5 %all-gather.7.cloned.1.call-done = bf16[24,192,1024]{2,1,0:T(8,128)(2,1)} async-done(((bf16[3,192,1024]{2,1,0:T(8,128)(2,1)}), bf16[24,192,1024]{2,1,0:T(8,128)(2,1)}) %all-gather.7.cloned.1.call-update) | async-done | bytes 9437200 | tf_op jit(solution)/shard_map/all_gather | solution.py:963
  210.8 27.3 %shard_map.411 = (bf16[4,3,192,1024]{3,2,1,0:T(8,128)(2,1)}, bf16[4,3,192,1024]{3,2,1,0:T(8,128)(2,1)}, bf16[256,1024]{1,0:T(8,128)(2,1)}, bf16[256,1024]{1,0:T(...) custom-call(s32[9]{0:T(128)} %pad_add_fusion.meta, ...), custom_call_target="tpu_custom_call" | custom-call | flops 24000000000 | bytes 24000000 | tf_op jit(solution)/shard_map/pallas_call | solution.py:75
  240.9 14.3 %collective-permute-done.22.refs_13_.refs_4_ = bf16[256,1152]{1,0:T(8,128)(2,1)S(1)} collective-permute-done((bf16[256,1152]{1,0:T(8,128)(2,1)}, bf16[256,1152]{1,0:T(8,128)(2,1)S(1)}, u32[]{:S(2)}, u32[]{:S(2)}) %collective-permute-start.22) | collective-permute-done | bytes 589856 | tf_op jit(solution)/shard_map/ppermute | solution.py:112
  255.2 12.8 %collective-permute-done.21.refs_12_.refs_3_ = bf16[256,1152]{1,0:T(8,128)(2,1)S(1)} collective-permute-done((bf16[256,1152]{1,0:T(8,128)(2,1)}, bf16[256,1152]{1,0:T(8,128)(2,1)S(1)}, u32[]{:S(2)}, u32[]{:S(2)}) %collective-permute-start.21) | collective-permute-done | bytes 589856 | tf_op jit(solution)/shard_map/ppermute | solution.py:112
  277.2 7.0 %shard_map.417 = (bf16[2,3,96,1024]{3,2,1,0:T(8,128)(2,1)}, bf16[2,3,96,1024]{3,2,1,0:T(8,128)(2,1)}, bf16[4,3,96,1024]{3,2,1,0:T(8,128)(2,1)}) custom-call(s32[1]{0:T(128)} %bitcast.meta, bf16[128,1152]{1,0:T(8,128)(2,1)} %copy-done.37, bf16[128,1152]{1,0:T(8,128)(2,1)} %copy-done.36, bf16[4,3,192,1024]{3,2,1,0:T(8,128)(2,1)} %get-tuple-element.138.refs_2_, ...), custom_call_target="tpu_custom_call" | custom-call | flops 6000000000 | bytes 6000000 | tf_op jit(solution)/shard_map/pallas_call | solution.py:75
  289.7 17.0 %shard_map.415 = (f32[256,1024]{1,0:T(8,128)}, bf16[256,1024]{1,0:T(8,128)(2,1)}, bf16[256,1024]{1,0:T(8,128)(2,1)}, f32[1024,128]{1,0:T(8,128)}, f32[8,1024]{1,...) custom-call(s32[1]{0:T(128)} %bitcast.meta, ...), custom_call_target="tpu_custom_call" | custom-call | flops 22000001024 | bytes 22000000 | tf_op jit(solution)/shard_map/pallas_call | solution.py:75
  316.0 11.7 %collective-permute-done.31.refs_2_ = bf16[2,3,96,1024]{3,2,1,0:T(8,128)(2,1)S(1)} collective-permute-done((bf16[2,3,96,1024]{3,2,1,0:T(8,128)(2,1)}, bf16[2,3,96,1024]{3,2,1,0:T(8,128)(2,1)S(1)}, u32[]{:S(2)}, u32[]{:S(2)}) %collective-permute-start.31) | collective-permute-done | bytes 1179680 | tf_op jit(solution)/shard_map/ppermute | solution.py:107
  329.2 15.1 %shard_map.421 = (bf16[4,128,3200]{2,1,0:T(8,128)(2,1)}, bf16[4,128,3200]{2,1,0:T(8,128)(2,1)}) custom-call(s32[9]{0:T(128)} %pad_add_fusion.meta, bf16[256,1024]{1,0:T(8,128)(2,1)} %collective-permute-done.26.refs_0_.refs_3_, bf16[256,1024]{1,0:T(8,128)(2,1)} %collective-permute-done.28.refs_1_.refs_4_, bf16[2,3,96,1024]{3,2,1,0:T(8,128)(2,1)} %copy-done.19, ...), custom_call_target="tpu_custom_call" | custom-call | flops 12000000000 | bytes 12000000 | tf_op jit(solution)/shard_map/pallas_call | solution.py:75
  345.0 6.1 %collective-permute-done.33.refs_1_ = bf16[4,128,3200]{2,1,0:T(8,128)(2,1)S(1)} collective-permute-done((bf16[4,128,3200]{2,1,0:T(8,128)(2,1)}, bf16[4,128,3200]{2,1,0:T(8,128)(2,1)S(1)}, u32[]{:S(2)}, u32[]{:S(2)}) %collective-permute-start.33) | collective-permute-done | bytes 3276832 | tf_op jit(solution)/shard_map/ppermute | solution.py:107
  361.4 13.0 %collective-permute-done.35.refs_0_ = bf16[256,1024]{1,0:T(8,128)(2,1)S(1)} collective-permute-done((bf16[256,1024]{1,0:T(8,128)(2,1)}, bf16[256,1024]{1,0:T(8,128)(2,1)S(1)}, u32[]{:S(2)}, u32[]{:S(2)}) %collective-permute-start.35) | collective-permute-done | bytes 524320 | tf_op jit(solution)/shard_map/ppermute | solution.py:112
  377.8 8.7 %collective-permute-done.30.refs_0_ = bf16[256,1024]{1,0:T(8,128)(2,1)S(1)} collective-permute-done((bf16[256,1024]{1,0:T(8,128)(2,1)}, bf16[256,1024]{1,0:T(8,128)(2,1)S(1)}, u32[]{:S(2)}, u32[]{:S(2)}) %collective-permute-start.30) | collective-permute-done | bytes 524320 | tf_op jit(solution)/shard_map/ppermute | solution.py:112
  394.1 7.4 %collective-permute-done.34.refs_0_.refs_12_ = bf16[128,1024]{1,0:T(8,128)(2,1)S(1)} collective-permute-done((bf16[128,1024]{1,0:T(8,128)(2,1)S(1)}, bf16[128,1024]{1,0:T(8,128)(2,1)S(1)}, u32[]{:S(2)}, u32[]{:S(2)}) %collective-permute-start.34) | collective-permute-done | bytes 262176 | tf_op jit(solution)/shard_map/ppermute | solution.py:112
  420.2 6.3 %shard_map.430.refs_1_ = f32[256,1024]{1,0:T(8,128)} custom-call(s32[1]{0:T(128)} %bitcast.meta, bf16[128,3200]{1,0:T(8,128)(2,1)} %shard_map.428.refs_0_, bf16[256,1024]{1,0:T(8,128)(2,1)} %bitcast.38, bf16[256,1024]{1,0:T(8,128)(2,1)} %get-tuple-element.145.refs_6_.refs_2_, bf16[1024,1024]{1,0:T(8,128)(2,1)} %get-tuple-element.148.refs_9_.refs_3_, ...), custom_call_target="tpu_custom_call" | custom-call | flops 6000000000 | bytes 6000000 | tf_op jit(solution)/shard_map/pallas_call | solution.py:75
  426.5 12.9 %shard_map.432 = (f32[8,128,1024]{2,1,0:T(8,128)}, f32[8,128,1024]{2,1,0:T(8,128)}, f32[8,128,1024]{2,1,0:T(8,128)}, f32[8,128,1024]{2,1,0:T(8,128)}, f32[8,64,1...) custom-call(s32[1]{0:T(128)} %bitcast.meta, ...), custom_call_target="tpu_custom_call" | custom-call | flops 8000000000 | bytes 8000000 | tf_op jit(solution)/shard_map/pallas_call | solution.py:75
  446.8 9.1 %shard_map.435 = (f32[8,128,1024]{2,1,0:T(8,128)}, f32[8,128,1024]{2,1,0:T(8,128)}, f32[8,128,1024]{2,1,0:T(8,128)}, f32[8,128,1024]{2,1,0:T(8,128)}, f32[8,64,1...) custom-call(s32[1]{0:T(128)} %bitcast.meta, ...), custom_call_target="tpu_custom_call", output_to_operand_aliasing={{0}: (13, {}), {1}: (14, {}), {2}: (15, {}), {3}: (16, {}),... | custom-call | flops 8000000000 | bytes 8000000 | tf_op jit(solution)/shard_map/pallas_call | solution.py:75
  461.0 6.7 %shard_map.436 = (f32[2,128]{1,0:T(2,128)}, f32[2,128]{1,0:T(2,128)}, f32[2,128]{1,0:T(2,128)}, f32[2,128]{1,0:T(2,128)}, f32[128,2048]{1,0:T(8,128)}, /*index=5...) custom-call(s32[1]{0:T(128)} %bitcast.meta, ...), custom_call_target="tpu_custom_call" | custom-call | flops 5000000000 | bytes 5000000 | tf_op jit(solution)/shard_map/pallas_call | solution.py:75
  (286 shorter events, 150.7 us)
Async XLA Ops:
  7.2 152.8 %all-gather.9.cloned.1.call-start = ((), (), s32[]{:S(2)}) async-start(), calls=%async_computation.4 | async-start | bytes 2949120 | tf_op jit(solution)/shard_map/all_gather | solution.py:955
  11.4 148.6 %all-gather.11.cloned.1.call-start = ((), (), s32[]{:S(2)}) async-start(), calls=%async_computation.5 | async-start | bytes 17694720 | tf_op jit(solution)/shard_map/all_gather | solution.py:963
  14.4 22.6 %collective-permute-start.2 = (bf16[128,3200]{1,0:T(8,128)(2,1)}, bf16[128,3200]{1,0:T(8,128)(2,1)S(1)}, u32[]{:S(2)}, u32[]{:S(2)}) collective-permute-start(bf16[128,3200]{1,0:T(8,128)(2,1)} %concatenate.35.refs_3_), channel_id=1, source_target_pairs={{0,4},{1,5},{2,6},{3,7},{4,0},{5,1},{6,2},{7,3},{8,12},{9,13},{10,... | collective-permute-start | bytes 2457608 | tf_op jit(solution)/shard_map/ppermute | solution.py:107
  50.1 160.8 %all-gather.7.cloned.1.call-start = ((), (), s32[]{:S(2)}) async-start(), calls=%async_computation.3 | async-start | bytes 10616832 | tf_op jit(solution)/shard_map/all_gather | solution.py:963
  51.3 375.2 %reduce-scatter.2.cloned.1.call-start = ((), (), s32[]{:S(2)}) async-start(), calls=%async_computation.2 | async-start | bytes 17694720 | tf_op jit(solution)/shard_map/reduce_scatter | solution.py:1052
  68.3 25.4 %collective-permute-start.10 = (bf16[256,1024]{1,0:T(8,128)(2,1)}, bf16[256,1024]{1,0:T(8,128)(2,1)S(1)}, u32[]{:S(2)}, u32[]{:S(2)}) collective-permute-start(bf16[256,1024]{1,0:T(8,128)(2,1)} %get-tuple-element.121.refs_4_.refs_16_), channel_id=1, source_target_pairs={{0,24},{8,0},{16,8},{24,16},{1,25},{9,1},{17,9},{25,17},{2,26},{10... | collective-permute-start | bytes 1572872 | tf_op jit(solution)/shard_map/ppermute | solution.py:112
  116.0 24.9 %collective-permute-start.13 = (bf16[256,1024]{1,0:T(8,128)(2,1)}, bf16[256,1024]{1,0:T(8,128)(2,1)S(1)}, u32[]{:S(2)}, u32[]{:S(2)}) collective-permute-start(bf16[256,1024]{1,0:T(8,128)(2,1)} %get-tuple-element.122.refs_4_.refs_1_), channel_id=1, source_target_pairs={{0,8},{8,16},{16,24},{24,0},{1,9},{9,17},{17,25},{25,1},{2,10},{10... | collective-permute-start | bytes 1572872 | tf_op jit(solution)/shard_map/ppermute | solution.py:112
  119.0 25.4 %collective-permute-start.14 = (bf16[256,1024]{1,0:T(8,128)(2,1)}, bf16[256,1024]{1,0:T(8,128)(2,1)S(1)}, u32[]{:S(2)}, u32[]{:S(2)}) collective-permute-start(bf16[256,1024]{1,0:T(8,128)(2,1)} %get-tuple-element.122.refs_4_.refs_1_), channel_id=1, source_target_pairs={{0,24},{8,0},{16,8},{24,16},{1,25},{9,1},{17,9},{25,17},{2,26},{10... | collective-permute-start | bytes 1572872 | tf_op jit(solution)/shard_map/ppermute | solution.py:112
  158.0 38.1 %collective-permute-start.17 = (bf16[256,1024]{1,0:T(8,128)(2,1)}, bf16[256,1024]{1,0:T(8,128)(2,1)S(1)}, u32[]{:S(2)}, u32[]{:S(2)}) collective-permute-start(bf16[256,1024]{1,0:T(8,128)(2,1)} %shard_map.412.refs_14_), channel_id=1, source_target_pairs={{0,8},{8,16},{16,24},{24,0},{1,9},{9,17},{17,25},{25,1},{2,10},{10... | collective-permute-start | bytes 1572872 | tf_op jit(solution)/shard_map/ppermute | solution.py:112
  158.6 37.5 %collective-permute-start.19 = (bf16[256,1024]{1,0:T(8,128)(2,1)}, bf16[256,1024]{1,0:T(8,128)(2,1)S(1)}, u32[]{:S(2)}, u32[]{:S(2)}) collective-permute-start(bf16[256,1024]{1,0:T(8,128)(2,1)} %shard_map.412.refs_14_), channel_id=1, source_target_pairs={{0,24},{8,0},{16,8},{24,16},{1,25},{9,1},{17,9},{25,17},{2,26},{10... | collective-permute-start | bytes 1572872 | tf_op jit(solution)/shard_map/ppermute | solution.py:112
  198.1 40.0 %collective-permute-start.18 = (bf16[128,1024]{1,0:T(8,128)(2,1)S(1)}, bf16[128,1024]{1,0:T(8,128)(2,1)S(1)}, u32[]{:S(2)}, u32[]{:S(2)}) collective-permute-start(bf16[128,1024]{1,0:T(8,128)(2,1)S(1)} %slice.112), channel_id=1, source_target_pairs={{0,8},{8,16},{16,24},{24,0},{1,9},{9,17},{17,25},{25,1},{2,10},{10... | collective-permute-start | bytes 786440 | tf_op jit(solution)/shard_map/ppermute | solution.py:112
  199.0 39.1 %collective-permute-start.20 = (bf16[128,1024]{1,0:T(8,128)(2,1)S(1)}, bf16[128,1024]{1,0:T(8,128)(2,1)S(1)}, u32[]{:S(2)}, u32[]{:S(2)}) collective-permute-start(bf16[128,1024]{1,0:T(8,128)(2,1)S(1)} %slice.113), channel_id=1, source_target_pairs={{0,24},{8,0},{16,8},{24,16},{1,25},{9,1},{17,9},{25,17},{2,26},{10... | collective-permute-start | bytes 786440 | tf_op jit(solution)/shard_map/ppermute | solution.py:112
  240.4 27.7 %collective-permute-start.21 = (bf16[256,1152]{1,0:T(8,128)(2,1)}, bf16[256,1152]{1,0:T(8,128)(2,1)S(1)}, u32[]{:S(2)}, u32[]{:S(2)}) collective-permute-start(bf16[256,1152]{1,0:T(8,128)(2,1)} %shard_map.413), channel_id=1, source_target_pairs={{0,24},{8,0},{16,8},{24,16},{1,25},{9,1},{17,9},{25,17},{2,26},{10... | collective-permute-start | bytes 1769480 | tf_op jit(solution)/shard_map/ppermute | solution.py:112
  284.1 43.6 %collective-permute-start.31 = (bf16[2,3,96,1024]{3,2,1,0:T(8,128)(2,1)}, bf16[2,3,96,1024]{3,2,1,0:T(8,128)(2,1)S(1)}, u32[]{:S(2)}, u32[]{:S(2)}) collective-permute-start(bf16[2,3,96,1024]{3,2,1,0:T(8,128)(2,1)} %get-tuple-element.140.refs_3_), channel_id=1, source_target_pairs={{0,2},{1,3},{2,0},{3,1},{4,6},{5,7},{6,4},{7,5},{8,10},{9,11},{10,... | collective-permute-start | bytes 3538952 | tf_op jit(solution)/shard_map/ppermute | solution.py:107
  285.3 42.4 %collective-permute-start.32 = (bf16[2,3,96,1024]{3,2,1,0:T(8,128)(2,1)}, bf16[2,3,96,1024]{3,2,1,0:T(8,128)(2,1)S(1)}, u32[]{:S(2)}, u32[]{:S(2)}) collective-permute-start(bf16[2,3,96,1024]{3,2,1,0:T(8,128)(2,1)} %get-tuple-element.141.refs_4_), channel_id=1, source_target_pairs={{0,4},{1,5},{2,6},{3,7},{4,0},{5,1},{6,2},{7,3},{8,12},{9,13},{10,... | collective-permute-start | bytes 3538952 | tf_op jit(solution)/shard_map/ppermute | solution.py:107
  288.3 24.9 %collective-permute-start.26 = (bf16[256,1024]{1,0:T(8,128)(2,1)}, bf16[256,1024]{1,0:T(8,128)(2,1)}, u32[]{:S(2)}, u32[]{:S(2)}) collective-permute-start(bf16[256,1024]{1,0:T(8,128)(2,1)} %shard_map.418), channel_id=1, source_target_pairs={{0,24},{8,0},{16,8},{24,16},{1,25},{9,1},{17,9},{25,17},{2,26},{10... | collective-permute-start | bytes 1572872 | tf_op jit(solution)/shard_map/ppermute | solution.py:112
  307.7 36.5 %collective-permute-start.29 = (bf16[128,1024]{1,0:T(8,128)(2,1)S(1)}, bf16[128,1024]{1,0:T(8,128)(2,1)S(1)}, u32[]{:S(2)}, u32[]{:S(2)}) collective-permute-start(bf16[128,1024]{1,0:T(8,128)(2,1)S(1)} %add_convert_fusion.4), channel_id=1, source_target_pairs={{0,8},{8,16},{16,24},{24,0},{1,9},{9,17},{17,25},{25,1},{2,10},{10... | collective-permute-start | bytes 786440 | tf_op jit(solution)/shard_map/ppermute | solution.py:112
  314.2 30.0 %collective-permute-start.27 = (bf16[128,1024]{1,0:T(8,128)(2,1)S(1)}, bf16[128,1024]{1,0:T(8,128)(2,1)S(1)}, u32[]{:S(2)}, u32[]{:S(2)}) collective-permute-start(bf16[128,1024]{1,0:T(8,128)(2,1)S(1)} %add_convert_fusion.5), channel_id=1, source_target_pairs={{0,24},{8,0},{16,8},{24,16},{1,25},{9,1},{17,9},{25,17},{2,26},{10... | collective-permute-start | bytes 786440 | tf_op jit(solution)/shard_map/ppermute | solution.py:112
  357.6 29.7 %collective-permute-start.37 = (bf16[2,64,3200]{2,1,0:T(8,128)(2,1)}, bf16[2,64,3200]{2,1,0:T(8,128)(2,1)S(1)}, u32[]{:S(2)}, u32[]{:S(2)}) collective-permute-start(bf16[2,64,3200]{2,1,0:T(8,128)(2,1)} %get-tuple-element.155.refs_1_), channel_id=1, source_target_pairs={{0,2},{1,3},{2,0},{3,1},{4,6},{5,7},{6,4},{7,5},{8,10},{9,11},{10,... | collective-permute-start | bytes 2457608 | tf_op jit(solution)/shard_map/ppermute | solution.py:107
  358.2 29.1 %collective-permute-start.38 = (bf16[2,64,3200]{2,1,0:T(8,128)(2,1)}, bf16[2,64,3200]{2,1,0:T(8,128)(2,1)S(1)}, u32[]{:S(2)}, u32[]{:S(2)}) collective-permute-start(bf16[2,64,3200]{2,1,0:T(8,128)(2,1)} %get-tuple-element.156.refs_2_), channel_id=1, source_target_pairs={{0,4},{1,5},{2,6},{3,7},{4,0},{5,1},{6,2},{7,3},{8,12},{9,13},{10,... | collective-permute-start | bytes 2457608 | tf_op jit(solution)/shard_map/ppermute | solution.py:107
  360.9 25.6 %collective-permute-start.30 = (bf16[256,1024]{1,0:T(8,128)(2,1)}, bf16[256,1024]{1,0:T(8,128)(2,1)S(1)}, u32[]{:S(2)}, u32[]{:S(2)}) collective-permute-start(bf16[256,1024]{1,0:T(8,128)(2,1)} %shard_map.420), channel_id=1, source_target_pairs={{0,24},{8,0},{16,8},{24,16},{1,25},{9,1},{17,9},{25,17},{2,26},{10... | collective-permute-start | bytes 1572872 | tf_op jit(solution)/shard_map/ppermute | solution.py:112
  411.2 34.6 %collective-permute-start.41 = (bf16[3,96,1024]{2,1,0:T(8,128)(2,1)}, bf16[3,96,1024]{2,1,0:T(8,128)(2,1)S(1)}, u32[]{:S(2)}, u32[]{:S(2)}) collective-permute-start(bf16[3,96,1024]{2,1,0:T(8,128)(2,1)} %get-tuple-element.165), channel_id=1, source_target_pairs={{0,2},{1,3},{2,0},{3,1},{4,6},{5,7},{6,4},{7,5},{8,10},{9,11},{10,... | collective-permute-start | bytes 1769480 | tf_op jit(solution)/shard_map/ppermute | solution.py:107
  412.2 33.6 %collective-permute-start.42 = (bf16[3,96,1024]{2,1,0:T(8,128)(2,1)}, bf16[3,96,1024]{2,1,0:T(8,128)(2,1)S(1)}, u32[]{:S(2)}, u32[]{:S(2)}) collective-permute-start(bf16[3,96,1024]{2,1,0:T(8,128)(2,1)} %get-tuple-element.166), channel_id=1, source_target_pairs={{0,4},{1,5},{2,6},{3,7},{4,0},{5,1},{6,2},{7,3},{8,12},{9,13},{10,... | collective-permute-start | bytes 1769480 | tf_op jit(solution)/shard_map/ppermute | solution.py:107
  413.6 25.8 %all-to-all-start = ((bf16[4,32,3200]{2,1,0:T(8,128)(2,1)}), bf16[4,32,3200]{2,1,0:T(8,128)(2,1)S(1)}, u32[]{:S(2)}, u32[]{:S(2)}) async-start(bf16[4,32,3200]{2,1,0:T(8,128)(2,1)} %bitcast.10), calls=%async_computation | async-start | bytes 1638400 | tf_op jit(solution)/shard_map/all_to_all | solution.py:1104
  (90 other events, 555.4 us)
Sparse Core Ops, SparseCore 0:
  11.5 49.9 all-gather.8
  64.0 85.1 all-gather.10
  151.7 59.1 all-gather.6
  214.2 125.1 reduce-scatter.1

commit v3 on v2

--- a/solution.py
+++ b/solution.py
@@ -64,8 +64,11 @@
     return pl.ds(pl.multiple_of(index, size), size)
 
 
-def kernel_call(body, outs, ins, scalars, scratch=(), grid=None, in_specs=None, out_specs=None, limit=60, after=(), micros=10, aliases=None):
+def kernel_call(body, outs, ins, scalars, scratch=(), grid=None, in_specs=None, out_specs=None, limit=60, after=(), micros=10, aliases=None, tables=()):
     in_specs = in_specs or [pl.BlockSpec(memory_space=pltpu.VMEM)] * len(ins)
+    for a in tables:
+        ins = list(ins) + [a]
+        in_specs = in_specs + [pl.BlockSpec((1,) + a.shape[1:], lambda i, m: (0, 0, 0))]
     out_specs = out_specs or [pl.BlockSpec(memory_space=pltpu.VMEM)] * len(outs)
     in_specs = [pl.BlockSpec(memory_space=pl.ANY)] * len(after) + in_specs
 
@@ -113,38 +116,36 @@
 
 
 class Gathered:
-    def __init__(self, value):
+    def __init__(self, first, second):
         self.plain = lax.axis_size("fsdp") != 8
-        self.value = value
-        self.half = value.shape[0] // 2
+        self.first, self.second = first, second
+        self.half = first.shape[0]
         if not self.plain:
-            self.over_x = xor_permute(value, "fsdp", 2)
-            self.over_y = xor_permute(value, "fsdp", 4)
-            self.core = xor_permute(value, "fsdp", 1)
+            self.x_first = xor_permute(first, "fsdp", 2)
+            self.y_second = xor_permute(second, "fsdp", 4)
+            self.x_second = xor_permute(second, "fsdp", 2)
+            self.y_first = xor_permute(first, "fsdp", 4)
 
     def forward(self, *earlier):
         if self.plain:
             return
-        self.over_x = tie(self.over_x, self.core, *earlier)
-        self.over_y = tie(self.over_y, self.core, *earlier)
-        self.far_first = xor_permute(self.over_x[: self.half], "fsdp", 4)
-        self.far_second = xor_permute(self.over_y[self.half :], "fsdp", 2)
+        self.x_first = tie(self.x_first, *earlier)
+        self.y_second = tie(self.y_second, *earlier)
+        self.far_first = xor_permute(self.x_first, "fsdp", 4)
+        self.far_second = xor_permute(self.y_second, "fsdp", 2)
 
     def arrived(self):
         return () if self.plain else (self.far_first, self.far_second)
 
-    def pieces(self, *earlier):
+    def pieces(self):
         count, half = lax.axis_size("fsdp"), self.half
         if self.plain:
-            whole = lax.all_gather(self.value, "fsdp", axis=0)
+            whole = lax.all_gather(jnp.concatenate([self.first, self.second]), "fsdp", axis=0)
             whole = jnp.take(whole, lax.axis_index("fsdp") ^ jnp.arange(count), axis=0)
             return [(r, 0, whole[r]) for r in range(count)]
-        if earlier:
-            self.far_first = tie(self.far_first, *earlier)
-            self.far_second = tie(self.far_second, *earlier)
-        mine = [(2, 0, self.over_x), (4, 0, self.over_y), (6, 0, self.far_first), (6, half, self.far_second)]
-        pieces = [(0, 0, self.value), (1, 0, self.core)] + mine
-        return pieces + [(r + 1, row, xor_permute(a, "fsdp", 1)) for r, row, a in mine]
+        mine = [(0, 0, self.first), (0, half, self.second), (2, 0, self.x_first), (2, half, self.x_second)]
+        mine += [(4, 0, self.y_first), (4, half, self.y_second), (6, 0, self.far_first), (6, half, self.far_second)]
+        return mine + [(r + 1, row, xor_permute(a, "fsdp", 1)) for r, row, a in mine]
 
 
 def pairs_body(groups, meta, *refs):
@@ -179,8 +180,12 @@
 
 def summed_body(meta, rest, over_x, over_y, then_x, then_y, total):
     half = rest.shape[1]
-    total[:half, :] = (rest[0].astype(f32) + over_x[1].astype(f32) + then_y[...].astype(f32)).astype(bf16)
-    total[half:, :] = (rest[1].astype(f32) + over_y[1].astype(f32) + then_x[...].astype(f32)).astype(bf16)
+    first = (rest[0].astype(f32) + over_x[1].astype(f32) + then_y[...].astype(f32)).astype(bf16)
+    second = (rest[1].astype(f32) + over_y[1].astype(f32) + then_x[...].astype(f32)).astype(bf16)
+    places, rows = total.shape[:2]
+    for k in range(places):
+        source, row = (first, k * rows) if k * rows < half else (second, k * rows - half)
+        total[k] = source[row : row + rows]
 
 
 class Scattered:
@@ -202,7 +207,7 @@
         two, four = shape_of((2, rows // 2, columns)), shape_of((4, rows // 2, columns))
         body = functools.partial(pairs_body, len(self.keep))
         sent_x, sent_y, self.rest = kernel_call(
-            body, [two, two, four], self.keep + self.got, self.scalars, after=earlier, micros=3
+            body, [two, two, four], self.keep + self.got, self.scalars, after=earlier, limit=24, micros=3
         )
         self.over_x = xor_permute(sent_x, "fsdp", 2)
         self.over_y = xor_permute(sent_y, "fsdp", 4)
@@ -213,21 +218,22 @@
             return ()
         one = shape_of(self.rest.shape[1:])
         ins = [self.rest, self.over_x, self.over_y]
-        sent_x, sent_y = kernel_call(passed_body, [one, one], ins, self.scalars, after=earlier, micros=2)
+        sent_x, sent_y = kernel_call(passed_body, [one, one], ins, self.scalars, after=earlier, limit=60, micros=2)
         self.then_x = xor_permute(sent_x, "fsdp", 2)
         self.then_y = xor_permute(sent_y, "fsdp", 4)
         return (sent_x, sent_y)
 
-    def total(self, *earlier):
+    def total(self, places, *earlier):
         if self.plain:
             count = lax.axis_size("fsdp")
             keep, send = jnp.concatenate(self.keep, axis=2), jnp.concatenate(self.send, axis=2)
             both = jnp.stack([keep, send], axis=1).reshape((count,) + keep.shape[1:])
             both = jnp.take(both, lax.axis_index("fsdp") ^ jnp.arange(count), axis=0)
-            return lax.psum_scatter(both, "fsdp", scatter_dimension=0)
+            total = lax.psum_scatter(both, "fsdp", scatter_dimension=0)
+            return total.reshape((places, -1, total.shape[1]))
         ins = [self.rest, self.over_x, self.over_y, self.then_x, self.then_y]
-        outs = [shape_of((2 * self.rest.shape[1], self.rest.shape[2]))]
-        return kernel_call(summed_body, outs, ins, self.scalars, after=earlier, micros=2)[0]
+        outs = [shape_of((places, 2 * self.rest.shape[1] // places, self.rest.shape[2]))]
+        return kernel_call(summed_body, outs, ins, self.scalars, after=earlier, limit=60, micros=2)[0]
 
 
 def expert_pairs_body(meta, keep, got, sent_x, sent_y, rest):
@@ -276,11 +282,16 @@
             in_specs=[whole, whole],
             out_specs=[group(2), group(2), group(4)],
             after=earlier,
-            micros=6,
+            limit=60, micros=6,
         )
-        self.over_x = xor_permute(sent_x, "fsdp", 2)
-        self.over_y = xor_permute(sent_y, "fsdp", 4)
-        return (sent_x, sent_y)
+        self.sent = (sent_x, sent_y)
+        return self.sent
+
+    def depart(self, *earlier):
+        if self.plain:
+            return
+        self.over_x = xor_permute(tie(self.sent[0], *earlier), "fsdp", 2)
+        self.over_y = xor_permute(tie(self.sent[1], *earlier), "fsdp", 4)
 
     def arrived(self):
         return () if self.plain else (self.over_x, self.over_y)
@@ -298,7 +309,7 @@
             in_specs=[self.group(2, 1), self.group(1), self.group(1)],
             out_specs=[self.single, self.single],
             after=earlier,
-            micros=4,
+            limit=60, micros=4,
         )
         self.then_x = xor_permute(sent_x, "fsdp", 2)
         self.then_y = xor_permute(sent_y, "fsdp", 4)
@@ -485,9 +496,10 @@
     return rotate_tile(tile, cosine, -sine)
 
 
-def qkv_body(pieces, meta, x_ref, cos_ref, sin_ref, *refs):
+def qkv_body(pieces, meta, x_ref, *refs):
     shards = refs[: len(pieces)]
-    wq_ref, wkv_ref, wo_ref, extra_ref, normed_ref, q_ref, kv_ref, columns = refs[len(pieces) :]
+    cos_ref, sin_ref, *refs = refs[len(pieces) :]
+    wq_ref, wkv_ref, wo_ref, extra_ref, normed_ref, q_ref, kv_ref, columns = refs
     shard_rows = MODEL_WIDTH // max(r + 1 for r, _, _ in pieces)
     for (r, row, value), ref in zip(pieces, shards):
         rows = value.shape[0]
@@ -501,7 +513,7 @@
     scale_inv = lax.rsqrt(jnp.mean(source * source, axis=-1, keepdims=True) + epsilon)
     normed = (source * scale_inv * extra_ref[EXPERTS : EXPERTS + 1, :]).astype(bf16)
     normed_ref[...] = normed
-    cosine, sine = cos_ref[...], sin_ref[...]
+    cosine, sine = cos_ref[0], sin_ref[0]
     low = lanes_of(cosine.shape) < HEAD_SIZE
     for j in range(MODEL_WIDTH // TILE):
         block = dot_nn(normed, wq_ref[:, j * TILE : (j + 1) * TILE])
@@ -581,14 +593,14 @@
         del refs[:number]
         return taken
 
-    (weights,) = take(1)
-    blocks, (told,) = take(len(pieces)), take(1)
+    up_w, down_w = take(2)
+    blocks, (told,), listed = take(len(pieces)), take(1), take(count)
     if start > 0:
         (part_g, part_m) = take(2)
     keep_ref, send_ref = take(2) if last else (take(1) + [None])
     ring_count = len(ring_shapes(count, TILE, WIDE)) if last else 1
     mix_refs, ring_refs = take(ring_count), take(ring_count)
-    up_s, down_s, x_s, c_s, ge_s, a_s, gu_s, d_s, eg_s, gs_s, gup_s, gdown_s, gate_s, rank_s, gg_s = refs
+    x_s, c_s, ge_s, a_s, gu_s, d_s, eg_s, gs_s, gup_s, gdown_s, gate_s, rank_s, gg_s = refs
     step = pl.program_id(0)
     local = EXPERTS // count
     up_rows, down_rows = MODEL_WIDTH // shards, FF // shards
@@ -608,7 +620,7 @@
         later = jnp.where(later, 1.0, 0.0).astype(bf16)
         names = lax.broadcasted_iota(jnp.int32, (EXPERTS, TILE), 0).astype(f32)
         for k in range(count):
-            named = told[absolute(k), :, MODEL_WIDTH:].astype(f32).T
+            named = listed[k][...].astype(f32)
             picked = names == named[0:1, :]
             for j in range(1, TOP):
                 picked = jnp.logical_or(picked, names == named[j : j + 1, :])
@@ -618,9 +630,19 @@
             rank_s[k] = jnp.where(picked, before, -1.0)
         gg_s[...] = jnp.zeros_like(gg_s)
 
-    for r in range(shards):
-        up_s[r * up_rows : (r + 1) * up_rows, :] = weights[r, 0, :up_rows, :]
-        down_s[r * down_rows : (r + 1) * down_rows, :] = weights[r, 0, up_rows:, :]
+    def up_columns(columns):
+        return up_w[:, 0, :, columns].reshape(MODEL_WIDTH, TILE)
+
+    def up_tile(j):
+        here = slice(j * TILE // up_rows, (j + 1) * TILE // up_rows)
+        return up_w[here, 0, :, :].reshape(TILE, 2 * FF)
+
+    def down_columns(columns):
+        return down_w[:, 0, :, columns].reshape(FF, TILE)
+
+    def down_tile(j):
+        here = slice(j * TILE // down_rows, (j + 1) * TILE // down_rows)
+        return down_w[here, 0, :, :].reshape(TILE, MODEL_WIDTH)
 
     wanted = lax.broadcasted_iota(jnp.int32, (CAP, TILE), 0).astype(f32)
     held = aligned(step * CAP, CAP)
@@ -633,7 +655,7 @@
         d_s[k, held, :] = chosen
         here = slice(k * CAP, (k + 1) * CAP)
         x_s[here, :] = dot_nn(chosen, block_value(pieces, blocks, k)).astype(bf16)
-        upstream = dot_nn(chosen, told[absolute(k), :, :MODEL_WIDTH])
+        upstream = dot_nn(chosen, told[absolute(k)])
         own_gate = jnp.sum(jnp.where(hit, gate, 0.0), axis=1, keepdims=True)
         gates.append(own_gate)
         c_s[here, :] = upstream.astype(bf16)
@@ -641,9 +663,9 @@
 
     for j in range(FF // TILE):
         left, right = slice(j * TILE, (j + 1) * TILE), slice(FF + j * TILE, FF + (j + 1) * TILE)
-        gate_part = dot_nn(x_s[...], up_s[:, left])
-        up_part = dot_nn(x_s[...], up_s[:, right])
-        hidden_grad = dot_nt(ge_s[...], down_s[left, :])
+        gate_part = dot_nn(x_s[...], up_columns(left))
+        up_part = dot_nn(x_s[...], up_columns(right))
+        hidden_grad = dot_nt(ge_s[...], down_tile(j))
         sigmoid_gate = jax.nn.sigmoid(gate_part)
         swish = gate_part * sigmoid_gate
         a_s[:, left] = (swish * up_part).astype(bf16)
@@ -654,9 +676,9 @@
     gate_grad = jnp.zeros((slots, 1), f32)
     for j in range(MODEL_WIDTH // TILE):
         columns = slice(j * TILE, (j + 1) * TILE)
-        produced = dot_nn(a_s[...], down_s[:, columns]).astype(bf16).astype(f32)
+        produced = dot_nn(a_s[...], down_columns(columns)).astype(bf16).astype(f32)
         gate_grad += jnp.sum(res_scale * c_s[:, columns].astype(f32) * produced, axis=1, keepdims=True)
-        input_grad = dot_nt(gu_s[...], up_s[columns, :]).astype(bf16)
+        input_grad = dot_nt(gu_s[...], up_tile(j)).astype(bf16)
         for k in range(count):
             here = slice(k * CAP, (k + 1) * CAP)
             eg_s[k, held, columns] = (gates[k] * produced[here]).astype(bf16)
@@ -668,17 +690,25 @@
 
     for j in range(FF // TILE):
         rows = slice(j * TILE, (j + 1) * TILE)
-        gdown_s[rows, :] = dot_tn(a_s[:, rows], ge_s[...]).astype(bf16)
+        tile = dot_tn(a_s[:, rows], ge_s[...]).astype(bf16)
+        if last:
+            gdown_s[rows, :] = tile
+        else:
+            here = slice(j * TILE // down_rows, (j + 1) * TILE // down_rows)
+            keep_ref[here, 0, up_rows:, :] = tile.reshape(TILE // down_rows, down_rows, MODEL_WIDTH)
     for j in range(MODEL_WIDTH // TILE):
         rows = slice(j * TILE, (j + 1) * TILE)
-        gup_s[rows, :] = dot_tn(x_s[:, rows], gu_s[...]).astype(bf16)
-    for r in range(shards):
+        tile = dot_tn(x_s[:, rows], gu_s[...]).astype(bf16)
         if last:
-            ref, at, owner = (send_ref if r % 2 else keep_ref), r // 2, meta[r]
+            gup_s[rows, :] = tile
         else:
-            ref, at, owner = keep_ref, r, r
-        ref[at, 0, :up_rows, :] = gup_s[aligned(owner * up_rows, up_rows), :]
-        ref[at, 0, up_rows:, :] = gdown_s[aligned(owner * down_rows, down_rows), :]
+            here = slice(j * TILE // up_rows, (j + 1) * TILE // up_rows)
+            keep_ref[here, 0, :up_rows, :] = tile.reshape(TILE // up_rows, up_rows, 2 * FF)
+    if last:
+        for r in range(shards):
+            ref = send_ref if r % 2 else keep_ref
+            ref[r // 2, 0, :up_rows, :] = gup_s[aligned(meta[r] * up_rows, up_rows), :]
+            ref[r // 2, 0, up_rows:, :] = gdown_s[aligned(meta[r] * down_rows, down_rows), :]
 
     @pl.when(step == members - 1)
     def combine():
@@ -704,10 +734,10 @@
                 ring_refs[0][k, :, MODEL_WIDTH:] = tail.astype(bf16)
 
 
-def backward_body(count, pieces, summed, meta, routes_ref, normed_ref, extra_ref, h_ref, c_ref, a_ref, wo_ref, q_ref, lse_ref, cos_ref, sin_ref, *refs):
+def backward_body(count, pieces, summed, meta, routes_ref, normed_ref, extra_ref, h_ref, c_ref, a_ref, wo_ref, q_ref, lse_ref, *refs):
     sums = refs[:summed]
     blocks = refs[summed : summed + len(pieces)]
-    outs = refs[summed + len(pieces) :]
+    cos_ref, sin_ref, *outs = refs[summed + len(pieces) :]
     gh_ref, go_ref, gpq_ref, gex_ref, gain_ref = outs[:5]
     ring_refs, ga_s = outs[5:-1], outs[-1]
     rows = q_ref.shape[0]
@@ -739,7 +769,7 @@
     go = (res_scale * resid_grad).astype(bf16)
     go_ref[...] = go
     ga_s[...] = dot_nt(go, wo_ref[...]).astype(bf16)
-    cosine, sine = cos_ref[...], sin_ref[...]
+    cosine, sine = cos_ref[0], sin_ref[0]
     low = lanes_of((rows, LANES)) < HEAD_SIZE
 
     def variant(seen):
@@ -791,7 +821,7 @@
         sets[r % 2][r // 2, :, columns] = source[aligned(meta[r] * rows, rows), :].astype(bf16)
 
 
-def weights_body(count, shards, pieces, meta, a_ref, go_ref, gpq_ref, gex_ref, gain_ref, wq_ref, wkv_ref, extra_ref, cos_ref, sin_ref, *refs):
+def weights_body(count, shards, pieces, meta, a_ref, go_ref, gpq_ref, gex_ref, gain_ref, cos_ref, sin_ref, *refs):
     blocks, parts = refs[: len(pieces)], refs[len(pieces) : -6]
     *sets, gp_s, normed_s, full_s, extra_s = refs[-6:]
     rows = gpq_ref.shape[0]
@@ -811,22 +841,16 @@
     store_sets(shards, meta, full_s, sets, slice(MODEL_WIDTH, 2 * MODEL_WIDTH))
     full_s[...] = dot_tn(a_ref[...], go_ref[...]).astype(bf16)
     store_sets(shards, meta, full_s, sets, slice(2 * MODEL_WIDTH, 3 * MODEL_WIDTH))
-    gain_grad = jnp.sum(dot_nt(gpq_ref[...], wq_ref[...]) * normed_s[:rows, :].astype(f32), axis=0, keepdims=True)
-    for k in range(count):
-        here = slice(k * rows, (k + 1) * rows)
-        product = dot_nt(gp_s[here, :], wkv_ref[...]) * normed_s[here, :].astype(f32)
-        gain_grad += jnp.sum(product, axis=0, keepdims=True)
-    gain_grad = gain_grad / extra_ref[EXPERTS : EXPERTS + 1, :]
     row_names = lax.broadcasted_iota(jnp.int32, (LANES, MODEL_WIDTH), 0)
-    gains = jnp.where(row_names == EXPERTS, gain_grad, jnp.where(row_names == EXPERTS + 1, gain_ref[0:1, :], 0.0))
+    gains = jnp.where(row_names == EXPERTS + 1, gain_ref[0:1, :], 0.0)
     extra_s[...] = gex_ref[...] + gains.T
     store_sets(shards, meta, extra_s, sets, slice(3 * MODEL_WIDTH, 3 * MODEL_WIDTH + LANES))
 
 
-def tokens_body(meta, x_ref, gpq_ref, wq_ref, wkv_ref, extra_ref, gh_ref, cos_ref, sin_ref, *refs):
-    *sums, grad_ref, gpkv_s = refs
+def tokens_body(meta, x_ref, gpq_ref, wq_ref, wkv_ref, extra_ref, gh_ref, *refs):
+    *sums, cos_ref, sin_ref, grad_ref, gpkv_s = refs
     total = ring_total(sums).astype(bf16).astype(f32)
-    cosine, sine = cos_ref[...], sin_ref[...]
+    cosine, sine = cos_ref[0], sin_ref[0]
     low = lanes_of(cosine.shape) < HEAD_SIZE
     for j in range(MODEL_WIDTH // LANES):
         lanes = slice(j * LANES, (j + 1) * LANES)
@@ -843,18 +867,35 @@
 
 def dense_update_body(count, rates, meta, *refs):
     quarters, refs = refs[:count], refs[count:]
-    ins, outs, total_s = refs[:12], refs[12:28], refs[28]
+    ins, outs, rest_s, gain_s = refs[:12], refs[12:28], refs[28], refs[29]
     rows = quarters[0].shape[0]
+    step = pl.program_id(0)
+
+    def update(i, gradient):
+        weight, first, second = [r[...] for r in ins[3 * i : 3 * i + 3]]
+        values = (gradient, *adam_update(weight, gradient, first, second, rates[i]))
+        for ref, value in zip(outs[4 * i : 4 * i + 4], values):
+            ref[...] = value
+
     for k in range(count):
-        at = lax.rem(meta[0] - k + count, count) * rows
-        total_s[pl.ds(pl.multiple_of(at, rows), rows), :] = quarters[k][...].astype(f32)
-    rest = total_s[:, 3 * MODEL_WIDTH :].T
-    out = total_s[:, 2 * MODEL_WIDTH : 3 * MODEL_WIDTH]
-    gradients = (rest[EXPERTS : EXPERTS + 2], total_s[:, : 2 * MODEL_WIDTH], out, rest[:EXPERTS])
-    for i, (gradient, rate) in enumerate(zip(gradients, rates)):
-        weight, first, second = [r[...] for r in ins[3 * i : 3 * i + 3]]
-        for ref, value in zip(outs[4 * i : 4 * i + 4], (gradient, *adam_update(weight, gradient, first, second, rate))):
-            ref[...] = value
+
+        @pl.when(step == k)
+        def part(k=k):
+            at = pl.ds(pl.multiple_of(lax.rem(meta[0] - k + count, count) * rows, rows), rows)
+            gradient = quarters[k][...].astype(f32)
+            qkv = gradient[:, : 2 * MODEL_WIDTH]
+            product = jnp.sum(qkv * ins[3][...].astype(bf16).astype(f32), axis=1, keepdims=True)
+            gain_s[at, :] = jnp.broadcast_to(product, (rows, LANES))
+            rest_s[at, :] = gradient[:, 3 * MODEL_WIDTH :]
+            update(1, qkv)
+            update(2, gradient[:, 2 * MODEL_WIDTH : 3 * MODEL_WIDTH])
+
+    @pl.when(step == count - 1)
+    def small():
+        rest = rest_s[...].T
+        first = gain_s[...].T[0:1] / ins[0][0:1, :].astype(bf16).astype(f32)
+        update(0, jnp.concatenate([first, rest[EXPERTS + 1 : EXPERTS + 2]], axis=0))
+        update(3, rest[:EXPERTS])
 
 
 def output_body(meta, h_ref, *refs):
@@ -896,7 +937,7 @@
         grid=(members,),
         in_specs=in_specs,
         out_specs=[spec(a) for a in outs],
-        micros=8,
+        limit=60, micros=8,
         after=after,
         aliases=aliases,
     )
@@ -940,7 +981,7 @@
     shards = lax.axis_size("fsdp")
     shard_rows = MODEL_WIDTH // shards
     local = EXPERTS // count
-    early_experts = (5 * local + 4) // 8
+    early_experts = 3 * local // 4
     chunks = [(0, early_experts), (early_experts, local - early_experts)]
     place = lax.axis_index("seq").astype(jnp.int32)
     owners = (lax.axis_index("fsdp") ^ jnp.arange(shards)).astype(jnp.int32)
@@ -948,12 +989,19 @@
     place_meta = place[None]
     x, c, own_routes = tokens[0], cotangent[0], routes[0]
 
-    blank = jnp.zeros((shard_rows, LANES - EXPERTS - 2), f32)
-    dense = jnp.concatenate([qkv_weight, out_weight, router_weight, norm_gains.T, blank], axis=1).astype(bf16)
-    listed = jnp.zeros((rows, LANES), f32).at[:, :TOP].set(own_routes.astype(f32))
-    dense_shards = Gathered(dense)
-    told = lax.all_gather(jnp.concatenate([c, listed.astype(bf16)], axis=1), "seq", axis=0)
-    dense_shards.forward()
+    def dense_part(piece):
+        blank = jnp.zeros((shard_rows // 2, LANES - EXPERTS - 2), f32)
+        parts = [qkv_weight[piece], out_weight[piece], router_weight[piece], norm_gains[:, piece].T, blank]
+        return jnp.concatenate(parts, axis=1).astype(bf16)
+
+    dense_shards = Gathered(dense_part(slice(0, shard_rows // 2)), dense_part(slice(shard_rows // 2, shard_rows)))
+    told = lax.all_gather(c, "seq", axis=0)
+    listed = jnp.concatenate([own_routes.T, jnp.zeros_like(own_routes.T)], axis=0).astype(f32).astype(bf16)
+    routes_by_block = [listed]
+    for k in range(1, count):
+        routes_by_block.append(shift_permute(listed, "seq", k))
+    cosines, sines = angle_tables(rows, jnp.maximum(place - jnp.arange(count), 0) * rows)
+    dense_shards.forward(cosines, sines, *routes_by_block[1:])
     early = dense_shards.arrived()
     dense_pieces = dense_shards.pieces()
     expert_weights = []
@@ -961,8 +1009,6 @@
         mine = slice(start, start + members)
         packed = jnp.concatenate([expert_up[mine], expert_down[mine]], axis=1).astype(bf16)
         expert_weights.append(lax.all_gather(tie(packed, *early), "fsdp", axis=0))
-    cosines, sines = angle_tables(rows, jnp.maximum(place - jnp.arange(count), 0) * rows)
-    cosine, sine = cosines[0], sines[0]
 
     square = shape_of((MODEL_WIDTH, MODEL_WIDTH))
     wide = shape_of((rows, MODEL_WIDTH))
@@ -972,10 +1018,11 @@
     wq, wkv, wo, extra, normed_one, q, kv = kernel_call(
         functools.partial(qkv_body, dense_pieces),
         [square, square, square, extra_shape, wide, wide, wide],
-        [x, cosine, sine] + [a for _, _, a in dense_pieces],
+        [x] + [a for _, _, a in dense_pieces],
         owner_meta,
+        tables=(cosines, sines),
         scratch=[pltpu.VMEM((MODEL_WIDTH, LANES), f32)],
-        micros=8,
+        limit=60, micros=8,
     )
     kv_pieces = ring_gather(kv)
     attended, logsum, resid, normed_two = kernel_call(
@@ -983,7 +1030,7 @@
         [wide, shape_of((KEY_VALUE_HEADS, 2 * rows), f32), wide_f, wide],
         [q, x, wo, extra] + [a for _, _, a in kv_pieces],
         place_meta,
-        micros=12,
+        limit=60, micros=12,
     )
     two_pieces = ring_gather(normed_two)
 
@@ -991,10 +1038,12 @@
     packed_rows = (MODEL_WIDTH + FF) // shards
     part_g = part_m = None
     waited = (cosines, sines)
-    normed_ring = Ringed(tie(normed_one, *[a for _, _, a in two_pieces[1:]]))
+    normed_block = tie(normed_one, *[a for _, _, a in two_pieces[1:]])
+    normed_blocks = tuple(shift_permute(normed_block, "seq", k) for k in range(1, count))
+    normed_pieces = [(k, 0, a) for k, a in enumerate((normed_one,) + normed_blocks)]
     for i, (start, members) in enumerate(chunks):
         last = i == len(chunks) - 1
-        ins = [extra, expert_weights[i]] + [a for _, _, a in two_pieces] + [told]
+        ins = [extra, expert_weights[i], expert_weights[i]] + [a for _, _, a in two_pieces] + [told] + routes_by_block
 
         def still(a):
             return pl.BlockSpec(a.shape, functools.partial(lambda n, e, m: (0,) * n, a.ndim), pipeline_mode=pl.Buffered(1))
@@ -1005,7 +1054,10 @@
         set_specs = [set_spec] * 2
         if not last:
             sets, set_specs = [shape_of((shards, members, packed_rows, MODEL_WIDTH))], [all_spec]
-        in_specs = [still(extra), all_spec] + [still(a) for a in ins[2:]]
+        up_spec = pl.BlockSpec((shards, 1, shard_rows, MODEL_WIDTH), lambda e, m: (0, e, 0, 0))
+        place_down = MODEL_WIDTH // FF
+        down_spec = pl.BlockSpec((shards, 1, FF // shards, MODEL_WIDTH), lambda e, m: (0, e, place_down, 0))
+        in_specs = [still(extra), up_spec, down_spec] + [still(a) for a in ins[3:]]
         if i > 0:
             ins += [part_g, part_m]
             in_specs += [still(part_g), still(part_m)]
@@ -1014,8 +1066,6 @@
         outs = sets + ring(count, rows, MODEL_WIDTH) + ring(count, rows, WIDE)
         out_specs = set_specs + [still(a) for a in outs[len(sets) :]]
         scratch = [
-            pltpu.VMEM((MODEL_WIDTH, 2 * FF), bf16),
-            pltpu.VMEM((FF, MODEL_WIDTH), bf16),
             pltpu.VMEM((slots, MODEL_WIDTH), bf16),
             pltpu.VMEM((slots, MODEL_WIDTH), bf16),
             pltpu.VMEM((slots, MODEL_WIDTH), bf16),
@@ -1042,17 +1092,16 @@
             micros=8 * members,
             after=waited,
         )
-        beside = normed_ring.forward() if last else normed_ring.near()
         results = list(results)
         first_part = len(sets)
         part_m, part_g = results[first_part], results[first_part + ring_count]
         mix_parts, ring_parts = results[first_part : first_part + ring_count], results[first_part + ring_count :]
         if not last:
-            share = tie(results[0], *beside) if beside else results[0]
+            share = tie(results[0], *normed_blocks)
             share = lax.psum_scatter(share, "fsdp", scatter_dimension=0)
 
-    two_ring = RingSum(ring_parts, *beside)
-    late_sum = ScatteredExperts(tie(results[1], *beside, *two_ring.near()), results[0], place_meta)
+    two_ring = RingSum(ring_parts)
+    late_sum = ScatteredExperts(tie(results[1], *two_ring.near()), results[0], place_meta)
     two_sums = two_ring.parts()
     sent = late_sum.first(*two_ring.sent)
     mixing = RingSum(mix_parts, *two_sums[3:], *sent)
@@ -1060,21 +1109,21 @@
     results = kernel_call(
         functools.partial(backward_body, count, kv_pieces, len(two_sums)),
         [wide_f, wide, wide, shape_of((MODEL_WIDTH, LANES), f32), shape_of((8, MODEL_WIDTH), f32)] + ring,
-        [own_routes, normed_two, extra, resid, c, attended, wo, q, logsum, cosine, sine]
+        [own_routes, normed_two, extra, resid, c, attended, wo, q, logsum]
         + list(two_sums)
         + [a for _, _, a in kv_pieces],
         place_meta,
+        tables=(cosines, sines),
         scratch=[pltpu.VMEM((rows, MODEL_WIDTH), bf16)],
-        micros=22,
+        limit=60, micros=22,
     )
     resid_grad, go, gpq, router_grad, gain_grad = results[:5]
     mix_sums = mixing.parts()
-    normed_pieces = normed_ring.pieces()
     dense_set = shape_of((shards // 2, shard_rows, 3 * MODEL_WIDTH + LANES))
     keep, send = kernel_call(
         functools.partial(weights_body, count, shards, normed_pieces),
         [dense_set] * 2,
-        [attended, go, gpq, router_grad, gain_grad, wq, wkv, extra, cosines, sines]
+        [attended, go, gpq, router_grad, gain_grad, cosines, sines]
         + [a for _, _, a in normed_pieces]
         + list(results[5:]),
         owner_meta,
@@ -1084,8 +1133,8 @@
             pltpu.VMEM((MODEL_WIDTH, MODEL_WIDTH), bf16),
             pltpu.VMEM((MODEL_WIDTH, LANES), f32),
         ],
-        after=mixing.near() + late_sum.arrived(),
-        micros=12,
+        after=mixing.near(),
+        limit=60, micros=12,
     )
     dense_sum = Scattered(place_meta)
     dense_sum.add(send, keep, *mix_sums[3:])
@@ -1093,39 +1142,50 @@
     experts = (expert_up, mean_up, square_up, expert_down, mean_down, square_down)
     sent = dense_sum.first()
     kv_ring = RingSum(results[5:], *mix_sums[3:])
-    kv_sums = kv_ring.parts(*sent)
     spec = pl.BlockSpec((1,) + share.shape[1:], lambda e, m: (e, 0, 0))
     total = ([share], [spec], lambda refs: refs[0][0].astype(f32))
-    dense_sum.second()
-    own = dense_sum.total(*kv_sums[3:])
-    updated = experts_update(chunks[0][0], total, experts, rates, None, place_meta, (own,))
-    late_sum.second(own)
-    quarters = own.reshape((count, shard_rows // count, own.shape[1]))
-    quarters = lax.all_to_all(quarters, "seq", split_axis=0, concat_axis=0, tiled=True)
+    updated = experts_update(chunks[0][0], total, experts, rates, None, place_meta, sent)
+    kv_sums = kv_ring.parts(*dense_sum.second(updated[0]))
+    own = dense_sum.total(count, *kv_ring.sent)
+    late_sum.depart(own)
+    quarters = lax.all_to_all(own, "seq", split_axis=0, concat_axis=0, tiled=True)
     (tokens_grad,) = kernel_call(
         tokens_body,
         [wide_f],
-        [x, gpq, wq, wkv, extra, resid_grad, cosine, sine] + list(kv_sums),
+        [x, gpq, wq, wkv, extra, resid_grad] + list(kv_sums),
         place_meta,
+        tables=(cosines, sines),
         scratch=[pltpu.VMEM((rows, MODEL_WIDTH), bf16)],
         after=(own,),
-        micros=6,
+        limit=60, micros=6,
     )
-    (output,) = kernel_call(output_body, [wide], [resid] + mix_sums, place_meta, after=(own,), micros=3)
-    quarter = jnp.sum(tie(quarters, tokens_grad, output, updated[0]).astype(f32), axis=0).astype(bf16)
+    (output,) = kernel_call(output_body, [wide], [resid] + mix_sums, place_meta, after=(own,), limit=60, micros=3)
+    quarter = jnp.sum(tie(quarters, tokens_grad, *late_sum.second(tokens_grad)).astype(f32), axis=0).astype(bf16)
     tokens_grad, output = tokens_grad[None], output[None]
     quarters = [quarter] + [shift_permute(quarter, "seq", k) for k in range(1, count)]
     updated = experts_update(chunks[1][0], late_sum.total(), experts, rates, updated, place_meta, (quarter,))
     dense_ins = [norm_gains, mean_gains, square_gains, qkv_weight, mean_qkv, square_qkv]
     dense_ins += [out_weight, mean_out, square_out, router_weight.T, mean_router.T, square_router.T]
+    part_rows = shard_rows // count
+
+    def whole_spec(a):
+        return pl.BlockSpec(a.shape, lambda k, m: (0,) * a.ndim)
+
+    def part_spec(a):
+        return pl.BlockSpec((part_rows, a.shape[1]), lambda k, m: (lax.rem(m[0] - k + count, count), 0))
+
+    specs = [whole_spec, part_spec, part_spec, whole_spec]
     dense_outs = kernel_call(
         functools.partial(dense_update_body, count, learn_rates[:4]),
         [shape_of(a.shape, f32) for a in dense_ins[::3] for _ in range(4)],
         quarters + dense_ins,
         place_meta,
-        scratch=[pltpu.VMEM((shard_rows, 3 * MODEL_WIDTH + LANES), f32)],
+        scratch=[pltpu.VMEM((shard_rows, LANES), f32), pltpu.VMEM((shard_rows, LANES), f32)],
+        grid=(count,),
+        in_specs=[whole_spec(a) for a in quarters] + [specs[i // 3](a) for i, a in enumerate(dense_ins)],
+        out_specs=[specs[i](dense_ins[3 * i]) for i in range(4) for _ in range(4)],
         after=(updated[0],),
-        micros=5,
+        limit=60, micros=5,
     )
     shard_gains, fresh_gains, momentum_gains, variance_gains = dense_outs[:4]
     shard_qkv, fresh_qkv, momentum_qkv, variance_qkv = dense_outs[4:8]

time: 484 us -> 444 us (0.917)
  the two profiles are of different devices: /device:TPU:12 before, /device:TPU:10 now
where the time goes in v3:
time: 444 us; the launch traced here: 435 us
  Pallas kernels  164 us (37%)
  waiting for transfers between devices  151 us (34%)
  starting transfers between devices  61.1 us (14%)
  local copies, waits for them, and re-layouts  26.9 us (6%)
  other arithmetic  17.3 us (4%)
  between operations  15 us (3%)
    pallas_call x16, Pallas kernels, kernel_call(): pl.pallas_call(ordered_body, out_shape=outs, grid_spec=pltpu.PrefetchScal...  164 us
    ppermute x29, waiting for transfers between devices, shift_permute(): lax.ppermute(value, axis, [(i, (i + step) % size) for i in range(size)])  114 us
    ppermute x29, starting transfers between devices, shift_permute(): lax.ppermute(value, axis, [(i, (i + step) % size) for i in range(size)])  38.1 us
    ppermute x24, waiting for transfers between devices, xor_permute(): lax.ppermute(value, axis, [(i, i ^ mask) for i in range(lax.axis_size(axi...  25.5 us
    unnamed x149, local copies, waits for them, and re-layouts  23.2 us
    ppermute x24, starting transfers between devices, xor_permute(): lax.ppermute(value, axis, [(i, i ^ mask) for i in range(lax.axis_size(axi...  17 us
  transfers between devices with their start and end apart: 58, of which 35 were waited for; matrix products, arithmetic and copies ran while one was open for 5% of the time, Pallas kernels for 36%

profile of v3, /device:TPU:10, one launch (start us, length us, event | category | flops | bytes accessed | tf_op | source)
XLA Modules:
  0.0 434.8 jit_solution(5418495947324427658)
XLA Ops:
  42.3 5.1 %collective-permute-done.4.refs_4_ = bf16[64,3200]{1,0:T(8,128)(2,1)S(1)} collective-permute-done((bf16[64,3200]{1,0:T(8,128)(2,1)S(1)}, bf16[64,3200]{1,0:T(8,128)(2,1)S(1)}, u32[]{:S(2)}, u32[]{:S(2)}) %collective-permute-start.4) | collective-permute-done | bytes 409632 | tf_op jit(solution)/shard_map/ppermute | solution.py:110
  53.1 9.0 %shard_map.406 = (bf16[1024,1024]{1,0:T(8,128)(2,1)}, bf16[1024,1024]{1,0:T(8,128)(2,1)}, bf16[1024,1024]{1,0:T(8,128)(2,1)}, f32[128,1024]{1,0:T(8,128)}, bf16[...) custom-call(s32[9]{0:T(128)} %pad_add_fusion.meta, bf16[256,1024]{1,0:T(8,128)(2,1)} %bitcast.32, ...), custom_call_target="tpu_custom_call" | custom-call | flops 8000000000 | bytes 8000000 | tf_op jit(solution)/shard_map/pallas_call | solution.py:78
  64.2 13.0 %collective-permute-done.17.refs_5_.refs_15_ = bf16[256,1024]{1,0:T(8,128)(2,1)S(1)} collective-permute-done((bf16[256,1024]{1,0:T(8,128)(2,1)}, bf16[256,1024]{1,0:T(8,128)(2,1)S(1)}, u32[]{:S(2)}, u32[]{:S(2)}) %collective-permute-start.17) | collective-permute-done | bytes 524320 | tf_op jit(solution)/shard_map/ppermute | solution.py:115
  77.2 10.5 %collective-permute-done.18.refs_6_.refs_16_ = bf16[256,1024]{1,0:T(8,128)(2,1)S(1)} collective-permute-done((bf16[256,1024]{1,0:T(8,128)(2,1)}, bf16[256,1024]{1,0:T(8,128)(2,1)S(1)}, u32[]{:S(2)}, u32[]{:S(2)}) %collective-permute-start.18) | collective-permute-done | bytes 524320 | tf_op jit(solution)/shard_map/ppermute | solution.py:115
  89.4 4.6 %collective-permute-done.19.refs_7_.refs_17_ = bf16[128,1024]{1,0:T(8,128)(2,1)S(1)} collective-permute-done((bf16[128,1024]{1,0:T(8,128)(2,1)S(1)}, bf16[128,1024]{1,0:T(8,128)(2,1)S(1)}, u32[]{:S(2)}, u32[]{:S(2)}) %collective-permute-start.19) | collective-permute-done | bytes 262176 | tf_op jit(solution)/shard_map/ppermute | solution.py:115
  94.1 6.5 %collective-permute-done.20.refs_8_.refs_18_ = bf16[128,1024]{1,0:T(8,128)(2,1)S(1)} collective-permute-done((bf16[128,1024]{1,0:T(8,128)(2,1)S(1)}, bf16[128,1024]{1,0:T(8,128)(2,1)S(1)}, u32[]{:S(2)}, u32[]{:S(2)}) %collective-permute-start.20) | collective-permute-done | bytes 262176 | tf_op jit(solution)/shard_map/ppermute | solution.py:115
  101.3 12.8 %shard_map.407 = (bf16[256,1024]{1,0:T(8,128)(2,1)}, f32[8,512]{1,0:T(8,128)}, f32[256,1024]{1,0:T(8,128)}, bf16[256,1024]{1,0:T(8,128)(2,1)}) custom-call(s32[1]{0:T(128)} %bitcast.meta, bf16[256,1024]{1,0:T(8,128)(2,1)} %get-tuple-element.106.refs_0_.refs_7_, bf16[256,1024]{1,0:T(8,128)(2,1)} %bitcast.33, ...), custom_call_target="tpu_custom_call" | custom-call | flops 12000000000 | bytes 12000000 | tf_op jit(solution)/shard_map/pallas_call | solution.py:78
  116.1 13.0 %collective-permute-done.21.refs_6_.refs_1_ = bf16[256,1024]{1,0:T(8,128)(2,1)S(1)} collective-permute-done((bf16[256,1024]{1,0:T(8,128)(2,1)}, bf16[256,1024]{1,0:T(8,128)(2,1)S(1)}, u32[]{:S(2)}, u32[]{:S(2)}) %collective-permute-start.21) | collective-permute-done | bytes 524320 | tf_op jit(solution)/shard_map/ppermute | solution.py:115
  129.1 11.2 %collective-permute-done.22.refs_7_.refs_2_ = bf16[256,1024]{1,0:T(8,128)(2,1)S(1)} collective-permute-done((bf16[256,1024]{1,0:T(8,128)(2,1)}, bf16[256,1024]{1,0:T(8,128)(2,1)S(1)}, u32[]{:S(2)}, u32[]{:S(2)}) %collective-permute-start.22) | collective-permute-done | bytes 524320 | tf_op jit(solution)/shard_map/ppermute | solution.py:115
  156.7 41.8 %shard_map.410 = (bf16[8,6,192,1024]{3,2,1,0:T(8,128)(2,1)}, bf16[4,256,1024]{2,1,0:T(8,128)(2,1)}, bf16[4,256,1152]{2,1,0:T(8,128)(2,1)}) custom-call(s32[9]{0:T(128)} %pad_add_fusion.meta, f32[4,256,128]{2,1,0:T(8,128)} %get-tuple-element.197.refs_1_.refs_17_.refs_0_.refs_19_.refs_7_.refs_12_, ...), custom_call_target="tpu_custom_call" | custom-call | flops 48000000000 | bytes 48000000 | tf_op jit(solution)/shard_map/pallas_call | solution.py:78
  204.7 22.1 %shard_map.411 = (bf16[4,2,192,1024]{3,2,1,0:T(8,128)(2,1)}, bf16[4,2,192,1024]{3,2,1,0:T(8,128)(2,1)}, bf16[256,1024]{1,0:T(8,128)(2,1)}, bf16[256,1024]{1,0:T(...) custom-call(s32[9]{0:T(128)} %pad_add_fusion.meta, ...), custom_call_target="tpu_custom_call" | custom-call | flops 16000000000 | bytes 16000000 | tf_op jit(solution)/shard_map/pallas_call | solution.py:78
  229.0 13.7 %collective-permute-done.25.refs_10_.refs_1_ = bf16[256,1152]{1,0:T(8,128)(2,1)S(1)} collective-permute-done((bf16[256,1152]{1,0:T(8,128)(2,1)}, bf16[256,1152]{1,0:T(8,128)(2,1)S(1)}, u32[]{:S(2)}, u32[]{:S(2)}) %collective-permute-start.25) | collective-permute-done | bytes 589856 | tf_op jit(solution)/shard_map/ppermute | solution.py:115
  242.6 14.5 %collective-permute-done.26.refs_11_.refs_2_ = bf16[256,1152]{1,0:T(8,128)(2,1)S(1)} collective-permute-done((bf16[256,1152]{1,0:T(8,128)(2,1)}, bf16[256,1152]{1,0:T(8,128)(2,1)S(1)}, u32[]{:S(2)}, u32[]{:S(2)}) %collective-permute-start.26) | collective-permute-done | bytes 589856 | tf_op jit(solution)/shard_map/ppermute | solution.py:115
  264.0 4.7 %shard_map.414 = (bf16[2,2,96,1024]{3,2,1,0:T(8,128)(2,1)}, bf16[2,2,96,1024]{3,2,1,0:T(8,128)(2,1)}, bf16[4,2,96,1024]{3,2,1,0:T(8,128)(2,1)}) custom-call(s32[1]{0:T(128)} %bitcast.meta, bf16[128,1152]{1,0:T(8,128)(2,1)} %copy-done.42, bf16[128,1152]{1,0:T(8,128)(2,1)} %copy-done.41, bf16[4,2,192,1024]{3,2,1,0:T(8,128)(2,1)} %get-tuple-element.125.refs_2_, ...), custom_call_target="tpu_custom_call" | custom-call | flops 6000000000 | bytes 6000000 | tf_op jit(solution)/shard_map/pallas_call | solution.py:78
  270.0 5.7 %collective-permute-done.27.refs_12_.refs_1_ = bf16[128,1152]{1,0:T(8,128)(2,1)S(1)} collective-permute-done((bf16[128,1152]{1,0:T(8,128)(2,1)S(1)}, bf16[128,1152]{1,0:T(8,128)(2,1)S(1)}, u32[]{:S(2)}, u32[]{:S(2)}) %collective-permute-start.27) | collective-permute-done | bytes 294944 | tf_op jit(solution)/shard_map/ppermute | solution.py:115
  278.4 17.3 %shard_map.412 = (f32[256,1024]{1,0:T(8,128)}, bf16[256,1024]{1,0:T(8,128)(2,1)}, bf16[256,1024]{1,0:T(8,128)(2,1)}, f32[1024,128]{1,0:T(8,128)}, f32[8,1024]{1,...) custom-call(s32[1]{0:T(128)} %bitcast.meta, ...), custom_call_target="tpu_custom_call" | custom-call | flops 22000001024 | bytes 22000000 | tf_op jit(solution)/shard_map/pallas_call | solution.py:78
  303.7 11.6 %shard_map.419 = (bf16[4,128,3200]{2,1,0:T(8,128)(2,1)}, bf16[4,128,3200]{2,1,0:T(8,128)(2,1)}) custom-call(s32[9]{0:T(128)} %pad_add_fusion.meta, bf16[256,1024]{1,0:T(8,128)(2,1)} %copy-done.53, bf16[256,1024]{1,0:T(8,128)(2,1)} %copy-done.52, bf16[256,1024]{1,0:T(8,128)(2,1)} %get-tuple-element.112.refs_5_.refs_2_, ...), custom_call_target="tpu_custom_call" | custom-call | flops 12000000000 | bytes 12000000 | tf_op jit(solution)/shard_map/pallas_call | solution.py:78
  317.3 5.9 %collective-permute-done.38.refs_1_ = bf16[4,128,3200]{2,1,0:T(8,128)(2,1)S(1)} collective-permute-done((bf16[4,128,3200]{2,1,0:T(8,128)(2,1)}, bf16[4,128,3200]{2,1,0:T(8,128)(2,1)S(1)}, u32[]{:S(2)}, u32[]{:S(2)}) %collective-permute-start.38) | collective-permute-done | bytes 3276832 | tf_op jit(solution)/shard_map/ppermute | solution.py:110
  330.9 5.8 %reduce-scatter.2.cloned.1.call-done = bf16[1,6,192,1024]{3,2,1,0:T(8,128)(2,1)} async-done(((bf16[8,6,192,1024]{3,2,1,0:T(8,128)(2,1)}), bf16[1,6,192,1024]{3,2,1,0:T(8,128)(2,1)}) %reduce-scatter.2.cloned.1.call-update) | async-done | bytes 2359312 | tf_op jit(solution)/shard_map/reduce_scatter | solution.py:1101
  336.6 13.8 %shard_map.423 = (f32[8,128,1024]{2,1,0:T(8,128)}, f32[8,128,1024]{2,1,0:T(8,128)}, f32[8,128,1024]{2,1,0:T(8,128)}, f32[8,128,1024]{2,1,0:T(8,128)}, f32[8,64,1...) custom-call(s32[1]{0:T(128)} %bitcast.meta, ...), custom_call_target="tpu_custom_call" | custom-call | flops 8000000000 | bytes 8000000 | tf_op jit(solution)/shard_map/pallas_call | solution.py:78
  374.0 5.9 %all-to-all-start = ((bf16[4,32,3200]{2,1,0:T(8,128)(2,1)}), bf16[4,32,3200]{2,1,0:T(8,128)(2,1)S(1)}, u32[]{:S(2)}, u32[]{:S(2)}) async-start(bf16[4,32,3200]{2,1,0:T(8,128)(2,1)} %shard_map.428.refs_0_.refs_1_), calls=%async_computation.1 | async-start | bytes 1638400 | tf_op jit(solution)/shard_map/all_to_all | solution.py:1151
  379.9 6.3 %shard_map.430.refs_0_.refs_1_ = f32[256,1024]{1,0:T(8,128)} custom-call(s32[1]{0:T(128)} %bitcast.meta, bf16[4,32,3200]{2,1,0:T(8,128)(2,1)} %shard_map.428.refs_0_.refs_1_, bf16[256,1024]{1,0:T(8,128)(2,1)} %bitcast.34, bf16[256,1024]{1,0:T(8,128)(2,1)} %get-tuple-element.132.refs_4_.refs_2_, bf16[1024,1024]{1,0:T(8,128)(2,1)} %get-tuple-element.149.refs_3_, ...), custom_call_target="tpu_custom_call" | custom-call | flops 6000000000 | bytes 6000000 | tf_op jit(solution)/shard_map/pallas_call | solution.py:78
  406.3 5.3 %shard_map.435 = (f32[8,128,1024]{2,1,0:T(8,128)}, f32[8,128,1024]{2,1,0:T(8,128)}, f32[8,128,1024]{2,1,0:T(8,128)}, f32[8,128,1024]{2,1,0:T(8,128)}, f32[8,64,1...) custom-call(s32[1]{0:T(128)} %bitcast.meta, ...), custom_call_target="tpu_custom_call", output_to_operand_aliasing={{0}: (13, {}), {1}: (14, {}), {2}: (15, {}), {3}: (16, {}),... | custom-call | flops 8000000000 | bytes 8000000 | tf_op jit(solution)/shard_map/pallas_call | solution.py:78
  420.5 7.3 %shard_map.436 = (f32[2,128]{1,0:T(2,128)}, f32[2,128]{1,0:T(2,128)}, f32[2,128]{1,0:T(2,128)}, f32[2,128]{1,0:T(2,128)}, f32[128,2048]{1,0:T(8,128)}, /*index=5...) custom-call(s32[1]{0:T(128)} %bitcast.meta, ...), custom_call_target="tpu_custom_call" | custom-call | flops 5000000000 | bytes 5000000 | tf_op jit(solution)/shard_map/pallas_call | solution.py:78
  (321 shorter events, 152.6 us)
Async XLA Ops:
  7.2 148.5 %all-gather.6.cloned.1.call-start = ((), (), s32[]{:S(2)}) async-start(), calls=%async_computation.2 | async-start | bytes 2621440 | tf_op jit(solution)/shard_map/all_gather | solution.py:998
  8.0 148.7 %all-gather.10.cloned.1.call-start = ((), (), s32[]{:S(2)}) async-start(), calls=%async_computation.5 | async-start | bytes 21233664 | tf_op jit(solution)/shard_map/all_gather | solution.py:1011
  37.8 166.9 %all-gather.8.cloned.1.call-start = ((), (), s32[]{:S(2)}) async-start(), calls=%async_computation.4 | async-start | bytes 7077888 | tf_op jit(solution)/shard_map/all_gather | solution.py:1011
  38.9 297.7 %reduce-scatter.2.cloned.1.call-start = ((), (), s32[]{:S(2)}) async-start(), calls=%async_computation.3 | async-start | bytes 21233664 | tf_op jit(solution)/shard_map/reduce_scatter | solution.py:1101
  62.6 25.1 %collective-permute-start.18 = (bf16[256,1024]{1,0:T(8,128)(2,1)}, bf16[256,1024]{1,0:T(8,128)(2,1)S(1)}, u32[]{:S(2)}, u32[]{:S(2)}) collective-permute-start(bf16[256,1024]{1,0:T(8,128)(2,1)} %get-tuple-element.109.refs_4_.refs_14_), channel_id=1, source_target_pairs={{0,24},{8,0},{16,8},{24,16},{1,25},{9,1},{17,9},{25,17},{2,26},{10... | collective-permute-start | bytes 1572872 | tf_op jit(solution)/shard_map/ppermute | solution.py:115
  77.2 16.9 %collective-permute-start.19 = (bf16[128,1024]{1,0:T(8,128)(2,1)S(1)}, bf16[128,1024]{1,0:T(8,128)(2,1)S(1)}, u32[]{:S(2)}, u32[]{:S(2)}) collective-permute-start(bf16[128,1024]{1,0:T(8,128)(2,1)S(1)} %slice.106), channel_id=1, source_target_pairs={{0,8},{8,16},{16,24},{24,0},{1,9},{9,17},{17,25},{25,1},{2,10},{10... | collective-permute-start | bytes 786440 | tf_op jit(solution)/shard_map/ppermute | solution.py:115
  115.6 24.7 %collective-permute-start.22 = (bf16[256,1024]{1,0:T(8,128)(2,1)}, bf16[256,1024]{1,0:T(8,128)(2,1)S(1)}, u32[]{:S(2)}, u32[]{:S(2)}) collective-permute-start(bf16[256,1024]{1,0:T(8,128)(2,1)} %get-tuple-element.110.refs_5_.refs_1_), channel_id=1, source_target_pairs={{0,24},{8,0},{16,8},{24,16},{1,25},{9,1},{17,9},{25,17},{2,26},{10... | collective-permute-start | bytes 1572872 | tf_op jit(solution)/shard_map/ppermute | solution.py:115
  129.1 16.9 %collective-permute-start.23 = (bf16[128,1024]{1,0:T(8,128)(2,1)S(1)}, bf16[128,1024]{1,0:T(8,128)(2,1)S(1)}, u32[]{:S(2)}, u32[]{:S(2)}) collective-permute-start(bf16[128,1024]{1,0:T(8,128)(2,1)S(1)} %slice.110), channel_id=1, source_target_pairs={{0,8},{8,16},{16,24},{24,0},{1,9},{9,17},{17,25},{25,1},{2,10},{10... | collective-permute-start | bytes 786440 | tf_op jit(solution)/shard_map/ppermute | solution.py:115
  151.0 47.4 %collective-permute-start.35 = (bf16[256,1024]{1,0:T(8,128)(2,1)}, bf16[256,1024]{1,0:T(8,128)(2,1)S(1)}, u32[]{:S(2)}, u32[]{:S(2)}) collective-permute-start(bf16[256,1024]{1,0:T(8,128)(2,1)} %shard_map.418), channel_id=1, source_target_pairs={{0,8},{8,16},{16,24},{24,0},{1,9},{9,17},{17,25},{25,1},{2,10},{10... | collective-permute-start | bytes 1572872 | tf_op jit(solution)/shard_map/ppermute | solution.py:115
  151.6 46.9 %collective-permute-start.36 = (bf16[256,1024]{1,0:T(8,128)(2,1)}, bf16[256,1024]{1,0:T(8,128)(2,1)S(1)}, u32[]{:S(2)}, u32[]{:S(2)}) collective-permute-start(bf16[256,1024]{1,0:T(8,128)(2,1)} %shard_map.418), channel_id=1, source_target_pairs={{0,16},{8,24},{16,0},{24,8},{1,17},{9,25},{17,1},{25,9},{2,18},{10... | collective-permute-start | bytes 1572872 | tf_op jit(solution)/shard_map/ppermute | solution.py:115
  154.9 45.0 %collective-permute-start.37 = (bf16[256,1024]{1,0:T(8,128)(2,1)}, bf16[256,1024]{1,0:T(8,128)(2,1)S(1)}, u32[]{:S(2)}, u32[]{:S(2)}) collective-permute-start(bf16[256,1024]{1,0:T(8,128)(2,1)} %shard_map.418), channel_id=1, source_target_pairs={{0,24},{8,0},{16,8},{24,16},{1,25},{9,1},{17,9},{25,17},{2,26},{10... | collective-permute-start | bytes 1572872 | tf_op jit(solution)/shard_map/ppermute | solution.py:115
  227.5 29.7 %collective-permute-start.26 = (bf16[256,1152]{1,0:T(8,128)(2,1)}, bf16[256,1152]{1,0:T(8,128)(2,1)S(1)}, u32[]{:S(2)}, u32[]{:S(2)}) collective-permute-start(bf16[256,1152]{1,0:T(8,128)(2,1)} %get-tuple-element.118), channel_id=1, source_target_pairs={{0,8},{8,16},{16,24},{24,0},{1,9},{9,17},{17,25},{25,1},{2,10},{10... | collective-permute-start | bytes 1769480 | tf_op jit(solution)/shard_map/ppermute | solution.py:115
  276.4 19.3 %collective-permute-start.32 = (bf16[256,1024]{1,0:T(8,128)(2,1)}, bf16[256,1024]{1,0:T(8,128)(2,1)S(1)}, u32[]{:S(2)}, u32[]{:S(2)}) collective-permute-start(bf16[256,1024]{1,0:T(8,128)(2,1)} %shard_map.416), channel_id=1, source_target_pairs={{0,8},{8,16},{16,24},{24,0},{1,9},{9,17},{17,25},{25,1},{2,10},{10... | collective-permute-start | bytes 1572872 | tf_op jit(solution)/shard_map/ppermute | solution.py:115
  277.0 24.8 %collective-permute-start.30 = (bf16[256,1024]{1,0:T(8,128)(2,1)}, bf16[256,1024]{1,0:T(8,128)(2,1)S(1)}, u32[]{:S(2)}, u32[]{:S(2)}) collective-permute-start(bf16[256,1024]{1,0:T(8,128)(2,1)} %shard_map.415), channel_id=1, source_target_pairs={{0,24},{8,0},{16,8},{24,16},{1,25},{9,1},{17,9},{25,17},{2,26},{10... | collective-permute-start | bytes 1572872 | tf_op jit(solution)/shard_map/ppermute | solution.py:115
  295.8 19.4 %collective-permute-start.33 = (bf16[128,1024]{1,0:T(8,128)(2,1)S(1)}, bf16[128,1024]{1,0:T(8,128)(2,1)S(1)}, u32[]{:S(2)}, u32[]{:S(2)}) collective-permute-start(bf16[128,1024]{1,0:T(8,128)(2,1)S(1)} %add_convert_fusion.4), channel_id=1, source_target_pairs={{0,8},{8,16},{16,24},{24,0},{1,9},{9,17},{17,25},{25,1},{2,10},{10... | collective-permute-start | bytes 786440 | tf_op jit(solution)/shard_map/ppermute | solution.py:115
  327.1 23.4 %collective-permute-start.39 = (bf16[2,64,3200]{2,1,0:T(8,128)(2,1)S(1)}, bf16[2,64,3200]{2,1,0:T(8,128)(2,1)S(1)}, u32[]{:S(2)}, u32[]{:S(2)}) collective-permute-start(bf16[2,64,3200]{2,1,0:T(8,128)(2,1)S(1)} %get-tuple-element.141.refs_0_), channel_id=1, source_target_pairs={{0,2},{1,3},{2,0},{3,1},{4,6},{5,7},{6,4},{7,5},{8,10},{9,11},{10,... | collective-permute-start | bytes 2457608 | tf_op jit(solution)/shard_map/ppermute | solution.py:110
  327.7 22.8 %collective-permute-start.40 = (bf16[2,64,3200]{2,1,0:T(8,128)(2,1)S(1)}, bf16[2,64,3200]{2,1,0:T(8,128)(2,1)}, u32[]{:S(2)}, u32[]{:S(2)}) collective-permute-start(bf16[2,64,3200]{2,1,0:T(8,128)(2,1)S(1)} %get-tuple-element.142.refs_1_), channel_id=1, source_target_pairs={{0,4},{1,5},{2,6},{3,7},{4,0},{5,1},{6,2},{7,3},{8,12},{9,13},{10,... | collective-permute-start | bytes 2457608 | tf_op jit(solution)/shard_map/ppermute | solution.py:110
  328.8 28.2 %collective-permute-start.41 = (bf16[256,1024]{1,0:T(8,128)(2,1)}, bf16[256,1024]{1,0:T(8,128)(2,1)S(1)}, u32[]{:S(2)}, u32[]{:S(2)}) collective-permute-start(bf16[256,1024]{1,0:T(8,128)(2,1)} %shard_map.426), channel_id=1, source_target_pairs={{0,8},{8,16},{16,24},{24,0},{1,9},{9,17},{17,25},{25,1},{2,10},{10... | collective-permute-start | bytes 1572872 | tf_op jit(solution)/shard_map/ppermute | solution.py:115
  330.0 30.9 %collective-permute-start.34 = (bf16[256,1024]{1,0:T(8,128)(2,1)}, bf16[256,1024]{1,0:T(8,128)(2,1)S(1)}, u32[]{:S(2)}, u32[]{:S(2)}) collective-permute-start(bf16[256,1024]{1,0:T(8,128)(2,1)} %shard_map.417), channel_id=1, source_target_pairs={{0,24},{8,0},{16,8},{24,16},{1,25},{9,1},{17,9},{25,17},{2,26},{10... | collective-permute-start | bytes 1572872 | tf_op jit(solution)/shard_map/ppermute | solution.py:115
  358.9 21.0 %collective-permute-start.45 = (bf16[128,1024]{1,0:T(8,128)(2,1)S(1)}, bf16[128,1024]{1,0:T(8,128)(2,1)}, u32[]{:S(2)}, u32[]{:S(2)}) collective-permute-start(bf16[128,1024]{1,0:T(8,128)(2,1)S(1)} %add_convert_fusion.2.refs_1_), channel_id=1, source_target_pairs={{0,8},{8,16},{16,24},{24,0},{1,9},{9,17},{17,25},{25,1},{2,10},{10... | collective-permute-start | bytes 786440 | tf_op jit(solution)/shard_map/ppermute | solution.py:115
  363.4 16.6 %collective-permute-start.44 = (bf16[128,1024]{1,0:T(8,128)(2,1)}, bf16[128,1024]{1,0:T(8,128)(2,1)}, u32[]{:S(2)}, u32[]{:S(2)}) collective-permute-start(bf16[128,1024]{1,0:T(8,128)(2,1)} %add_convert_fusion.3.refs_0_), channel_id=1, source_target_pairs={{0,24},{8,0},{16,8},{24,16},{1,25},{9,1},{17,9},{25,17},{2,26},{10... | collective-permute-start | bytes 786440 | tf_op jit(solution)/shard_map/ppermute | solution.py:115
  371.3 18.0 %collective-permute-start.47 = (bf16[2,2,96,1024]{3,2,1,0:T(8,128)(2,1)S(1)}, bf16[2,2,96,1024]{3,2,1,0:T(8,128)(2,1)S(1)}, u32[]{:S(2)}, u32[]{:S(2)}) collective-permute-start(bf16[2,2,96,1024]{3,2,1,0:T(8,128)(2,1)S(1)} %copy-done.6), channel_id=1, source_target_pairs={{0,4},{1,5},{2,6},{3,7},{4,0},{5,1},{6,2},{7,3},{8,12},{9,13},{10,... | collective-permute-start | bytes 2359304 | tf_op jit(solution)/shard_map/ppermute | solution.py:110
  373.0 17.7 %collective-permute-start.46 = (bf16[2,2,96,1024]{3,2,1,0:T(8,128)(2,1)}, bf16[2,2,96,1024]{3,2,1,0:T(8,128)(2,1)S(1)}, u32[]{:S(2)}, u32[]{:S(2)}) collective-permute-start(bf16[2,2,96,1024]{3,2,1,0:T(8,128)(2,1)} %shard_map.431), channel_id=1, source_target_pairs={{0,2},{1,3},{2,0},{3,1},{4,6},{5,7},{6,4},{7,5},{8,10},{9,11},{10,... | collective-permute-start | bytes 2359304 | tf_op jit(solution)/shard_map/ppermute | solution.py:110
  374.0 24.2 %all-to-all-start = ((bf16[4,32,3200]{2,1,0:T(8,128)(2,1)}), bf16[4,32,3200]{2,1,0:T(8,128)(2,1)S(1)}, u32[]{:S(2)}, u32[]{:S(2)}) async-start(bf16[4,32,3200]{2,1,0:T(8,128)(2,1)} %shard_map.428.refs_0_.refs_1_), calls=%async_computation.1 | async-start | bytes 1638400 | tf_op jit(solution)/shard_map/all_to_all | solution.py:1151
  (107 other events, 749.7 us)
Sparse Core Ops, SparseCore 0:
  9.6 45.4 all-gather.5
  57.6 99.0 all-gather.9
  159.1 45.5 all-gather.7
  208.2 128.4 reduce-scatter.1

commit v4 on v3

--- a/solution.py
+++ b/solution.py
@@ -173,21 +173,6 @@
             ref[place, :, lanes] = value
 
 
-def passed_body(meta, rest, over_x, over_y, then_x, then_y):
-    then_x[...] = (rest[2].astype(f32) + over_y[0].astype(f32)).astype(bf16)
-    then_y[...] = (rest[3].astype(f32) + over_x[0].astype(f32)).astype(bf16)
-
-
-def summed_body(meta, rest, over_x, over_y, then_x, then_y, total):
-    half = rest.shape[1]
-    first = (rest[0].astype(f32) + over_x[1].astype(f32) + then_y[...].astype(f32)).astype(bf16)
-    second = (rest[1].astype(f32) + over_y[1].astype(f32) + then_x[...].astype(f32)).astype(bf16)
-    places, rows = total.shape[:2]
-    for k in range(places):
-        source, row = (first, k * rows) if k * rows < half else (second, k * rows - half)
-        total[k] = source[row : row + rows]
-
-
 class Scattered:
     def __init__(self, scalars):
         self.plain = lax.axis_size("fsdp") != 8
@@ -216,9 +201,10 @@
     def second(self, *earlier):
         if self.plain:
             return ()
-        one = shape_of(self.rest.shape[1:])
-        ins = [self.rest, self.over_x, self.over_y]
-        sent_x, sent_y = kernel_call(passed_body, [one, one], ins, self.scalars, after=earlier, limit=60, micros=2)
+        if earlier:
+            self.over_x, self.over_y = tie(self.over_x, *earlier), tie(self.over_y, *earlier)
+        sent_x = (self.rest[2].astype(f32) + self.over_y[0].astype(f32)).astype(bf16)
+        sent_y = (self.rest[3].astype(f32) + self.over_x[0].astype(f32)).astype(bf16)
         self.then_x = xor_permute(sent_x, "fsdp", 2)
         self.then_y = xor_permute(sent_y, "fsdp", 4)
         return (sent_x, sent_y)
@@ -231,9 +217,11 @@
             both = jnp.take(both, lax.axis_index("fsdp") ^ jnp.arange(count), axis=0)
             total = lax.psum_scatter(both, "fsdp", scatter_dimension=0)
             return total.reshape((places, -1, total.shape[1]))
-        ins = [self.rest, self.over_x, self.over_y, self.then_x, self.then_y]
-        outs = [shape_of((places, 2 * self.rest.shape[1] // places, self.rest.shape[2]))]
-        return kernel_call(summed_body, outs, ins, self.scalars, after=earlier, limit=60, micros=2)[0]
+        if earlier:
+            self.then_x = tie(self.then_x, *earlier)
+        first = self.rest[0].astype(f32) + self.over_x[1].astype(f32) + self.then_y.astype(f32)
+        second = self.rest[1].astype(f32) + self.over_y[1].astype(f32) + self.then_x.astype(f32)
+        return jnp.concatenate([first, second]).astype(bf16).reshape((places, -1, first.shape[1]))
 
 
 def expert_pairs_body(meta, keep, got, sent_x, sent_y, rest):
@@ -1159,8 +1147,8 @@
         after=(own,),
         limit=60, micros=6,
     )
-    (output,) = kernel_call(output_body, [wide], [resid] + mix_sums, place_meta, after=(own,), limit=60, micros=3)
     quarter = jnp.sum(tie(quarters, tokens_grad, *late_sum.second(tokens_grad)).astype(f32), axis=0).astype(bf16)
+    (output,) = kernel_call(output_body, [wide], [resid] + mix_sums, place_meta, after=(quarter,), micros=3)
     tokens_grad, output = tokens_grad[None], output[None]
     quarters = [quarter] + [shift_permute(quarter, "seq", k) for k in range(1, count)]
     updated = experts_update(chunks[1][0], late_sum.total(), experts, rates, updated, place_meta, (quarter,))

time: 444 us -> 440 us (level)
  the two profiles are of different devices: /device:TPU:10 before, /device:TPU:12 now
where the time goes in v4:
time: 440 us; the launch traced here: 432 us
  Pallas kernels  158 us (36%)
  waiting for transfers between devices  155 us (35%)
  starting transfers between devices  61.3 us (14%)
  local copies, waits for them, and re-layouts  22.1 us (5%)
  other arithmetic  20.7 us (5%)
  between operations  15.1 us (3%)
    pallas_call x14, Pallas kernels, kernel_call(): pl.pallas_call(ordered_body, out_shape=outs, grid_spec=pltpu.PrefetchScal...  158 us
    ppermute x29, waiting for transfers between devices, shift_permute(): lax.ppermute(value, axis, [(i, (i + step) % size) for i in range(size)])  114 us
    ppermute x29, starting transfers between devices, shift_permute(): lax.ppermute(value, axis, [(i, (i + step) % size) for i in range(size)])  38.6 us
    ppermute x24, waiting for transfers between devices, xor_permute(): lax.ppermute(value, axis, [(i, i ^ mask) for i in range(lax.axis_size(axi...  28.2 us
    unnamed x141, local copies, waits for them, and re-layouts  18.4 us
    ppermute x24, starting transfers between devices, xor_permute(): lax.ppermute(value, axis, [(i, i ^ mask) for i in range(lax.axis_size(axi...  16.5 us
  transfers between devices with their start and end apart: 58, of which 32 were waited for; matrix products, arithmetic and copies ran while one was open for 6% of the time, Pallas kernels for 35%

profile of v4, /device:TPU:12, one launch (start us, length us, event | category | flops | bytes accessed | tf_op | source)
XLA Modules:
  0.0 431.6 jit_solution(6741884196700744380)
XLA Ops:
  41.6 6.5 %collective-permute-done.4.refs_4_ = bf16[64,3200]{1,0:T(8,128)(2,1)S(1)} collective-permute-done((bf16[64,3200]{1,0:T(8,128)(2,1)S(1)}, bf16[64,3200]{1,0:T(8,128)(2,1)S(1)}, u32[]{:S(2)}, u32[]{:S(2)}) %collective-permute-start.4) | collective-permute-done | bytes 409632 | tf_op jit(solution)/shard_map/ppermute | solution.py:110
  53.2 9.0 %shard_map.406 = (bf16[1024,1024]{1,0:T(8,128)(2,1)}, bf16[1024,1024]{1,0:T(8,128)(2,1)}, bf16[1024,1024]{1,0:T(8,128)(2,1)}, f32[128,1024]{1,0:T(8,128)}, bf16[...) custom-call(s32[9]{0:T(128)} %pad_add_fusion.meta, bf16[256,1024]{1,0:T(8,128)(2,1)} %bitcast.45, ...), custom_call_target="tpu_custom_call" | custom-call | flops 8000000000 | bytes 8000000 | tf_op jit(solution)/shard_map/pallas_call | solution.py:78
  64.2 12.9 %collective-permute-done.17.refs_5_.refs_15_ = bf16[256,1024]{1,0:T(8,128)(2,1)S(1)} collective-permute-done((bf16[256,1024]{1,0:T(8,128)(2,1)}, bf16[256,1024]{1,0:T(8,128)(2,1)S(1)}, u32[]{:S(2)}, u32[]{:S(2)}) %collective-permute-start.17) | collective-permute-done | bytes 524320 | tf_op jit(solution)/shard_map/ppermute | solution.py:115
  77.3 10.6 %collective-permute-done.18.refs_6_.refs_16_ = bf16[256,1024]{1,0:T(8,128)(2,1)S(1)} collective-permute-done((bf16[256,1024]{1,0:T(8,128)(2,1)}, bf16[256,1024]{1,0:T(8,128)(2,1)S(1)}, u32[]{:S(2)}, u32[]{:S(2)}) %collective-permute-start.18) | collective-permute-done | bytes 524320 | tf_op jit(solution)/shard_map/ppermute | solution.py:115
  94.1 6.6 %collective-permute-done.20.refs_8_.refs_18_ = bf16[128,1024]{1,0:T(8,128)(2,1)S(1)} collective-permute-done((bf16[128,1024]{1,0:T(8,128)(2,1)S(1)}, bf16[128,1024]{1,0:T(8,128)(2,1)S(1)}, u32[]{:S(2)}, u32[]{:S(2)}) %collective-permute-start.20) | collective-permute-done | bytes 262176 | tf_op jit(solution)/shard_map/ppermute | solution.py:115
  101.4 12.8 %shard_map.408 = (bf16[256,1024]{1,0:T(8,128)(2,1)}, f32[8,512]{1,0:T(8,128)}, f32[256,1024]{1,0:T(8,128)}, bf16[256,1024]{1,0:T(8,128)(2,1)}) custom-call(s32[1]{0:T(128)} %bitcast.meta, bf16[256,1024]{1,0:T(8,128)(2,1)} %get-tuple-element.105.refs_0_.refs_7_, bf16[256,1024]{1,0:T(8,128)(2,1)} %bitcast.46, ...), custom_call_target="tpu_custom_call" | custom-call | flops 12000000000 | bytes 12000000 | tf_op jit(solution)/shard_map/pallas_call | solution.py:78
  116.2 13.0 %collective-permute-done.21.refs_6_.refs_1_ = bf16[256,1024]{1,0:T(8,128)(2,1)S(1)} collective-permute-done((bf16[256,1024]{1,0:T(8,128)(2,1)}, bf16[256,1024]{1,0:T(8,128)(2,1)S(1)}, u32[]{:S(2)}, u32[]{:S(2)}) %collective-permute-start.21) | collective-permute-done | bytes 524320 | tf_op jit(solution)/shard_map/ppermute | solution.py:115
  129.3 11.3 %collective-permute-done.22.refs_7_.refs_2_ = bf16[256,1024]{1,0:T(8,128)(2,1)S(1)} collective-permute-done((bf16[256,1024]{1,0:T(8,128)(2,1)}, bf16[256,1024]{1,0:T(8,128)(2,1)S(1)}, u32[]{:S(2)}, u32[]{:S(2)}) %collective-permute-start.22) | collective-permute-done | bytes 524320 | tf_op jit(solution)/shard_map/ppermute | solution.py:115
  146.1 4.6 %collective-permute-done.24.refs_9_.refs_4_ = bf16[128,1024]{1,0:T(8,128)(2,1)S(1)} collective-permute-done((bf16[128,1024]{1,0:T(8,128)(2,1)S(1)}, bf16[128,1024]{1,0:T(8,128)(2,1)S(1)}, u32[]{:S(2)}, u32[]{:S(2)}) %collective-permute-start.24) | collective-permute-done | bytes 262176 | tf_op jit(solution)/shard_map/ppermute | solution.py:115
  155.9 41.8 %shard_map.410 = (bf16[8,6,192,1024]{3,2,1,0:T(8,128)(2,1)}, bf16[4,256,1024]{2,1,0:T(8,128)(2,1)}, bf16[4,256,1152]{2,1,0:T(8,128)(2,1)}) custom-call(s32[9]{0:T(128)} %pad_add_fusion.meta, f32[4,256,128]{2,1,0:T(8,128)} %get-tuple-element.197.refs_1_.refs_17_.refs_0_.refs_19_.refs_7_.refs_12_, ...), custom_call_target="tpu_custom_call" | custom-call | flops 48000000000 | bytes 48000000 | tf_op jit(solution)/shard_map/pallas_call | solution.py:78
  204.5 22.0 %shard_map.411 = (bf16[4,2,192,1024]{3,2,1,0:T(8,128)(2,1)}, bf16[4,2,192,1024]{3,2,1,0:T(8,128)(2,1)}, bf16[256,1024]{1,0:T(8,128)(2,1)}, bf16[256,1024]{1,0:T(...) custom-call(s32[9]{0:T(128)} %pad_add_fusion.meta, ...), custom_call_target="tpu_custom_call" | custom-call | flops 16000000000 | bytes 16000000 | tf_op jit(solution)/shard_map/pallas_call | solution.py:78
  228.5 13.7 %collective-permute-done.25.refs_1_.refs_10_ = bf16[256,1152]{1,0:T(8,128)(2,1)S(1)} collective-permute-done((bf16[256,1152]{1,0:T(8,128)(2,1)}, bf16[256,1152]{1,0:T(8,128)(2,1)S(1)}, u32[]{:S(2)}, u32[]{:S(2)}) %collective-permute-start.25) | collective-permute-done | bytes 589856 | tf_op jit(solution)/shard_map/ppermute | solution.py:115
  242.2 14.5 %collective-permute-done.27.refs_2_.refs_11_ = bf16[256,1152]{1,0:T(8,128)(2,1)S(1)} collective-permute-done((bf16[256,1152]{1,0:T(8,128)(2,1)}, bf16[256,1152]{1,0:T(8,128)(2,1)S(1)}, u32[]{:S(2)}, u32[]{:S(2)}) %collective-permute-start.27) | collective-permute-done | bytes 589856 | tf_op jit(solution)/shard_map/ppermute | solution.py:115
  263.6 4.7 %shard_map.413 = (bf16[2,2,96,1024]{3,2,1,0:T(8,128)(2,1)}, bf16[2,2,96,1024]{3,2,1,0:T(8,128)(2,1)}, bf16[4,2,96,1024]{3,2,1,0:T(8,128)(2,1)}) custom-call(s32[1]{0:T(128)} %bitcast.meta, bf16[128,1152]{1,0:T(8,128)(2,1)} %copy-done.42, bf16[128,1152]{1,0:T(8,128)(2,1)} %copy-done.41, bf16[4,2,192,1024]{3,2,1,0:T(8,128)(2,1)} %get-tuple-element.116.refs_2_, ...), custom_call_target="tpu_custom_call" | custom-call | flops 6000000000 | bytes 6000000 | tf_op jit(solution)/shard_map/pallas_call | solution.py:78
  269.6 5.7 %collective-permute-done.26.refs_1_.refs_12_ = bf16[128,1152]{1,0:T(8,128)(2,1)S(1)} collective-permute-done((bf16[128,1152]{1,0:T(8,128)(2,1)S(1)}, bf16[128,1152]{1,0:T(8,128)(2,1)S(1)}, u32[]{:S(2)}, u32[]{:S(2)}) %collective-permute-start.26) | collective-permute-done | bytes 294944 | tf_op jit(solution)/shard_map/ppermute | solution.py:115
  278.0 17.2 %shard_map.416 = (f32[256,1024]{1,0:T(8,128)}, bf16[256,1024]{1,0:T(8,128)(2,1)}, bf16[256,1024]{1,0:T(8,128)(2,1)}, f32[1024,128]{1,0:T(8,128)}, f32[8,1024]{1,...) custom-call(s32[1]{0:T(128)} %bitcast.meta, ...), custom_call_target="tpu_custom_call" | custom-call | flops 22000001024 | bytes 22000000 | tf_op jit(solution)/shard_map/pallas_call | solution.py:78
  303.3 11.6 %shard_map.418 = (bf16[4,128,3200]{2,1,0:T(8,128)(2,1)}, bf16[4,128,3200]{2,1,0:T(8,128)(2,1)}) custom-call(s32[9]{0:T(128)} %pad_add_fusion.meta, bf16[256,1024]{1,0:T(8,128)(2,1)} %copy-done.51, bf16[256,1024]{1,0:T(8,128)(2,1)} %copy-done.50, bf16[256,1024]{1,0:T(8,128)(2,1)} %get-tuple-element.121.refs_5_.refs_2_, ...), custom_call_target="tpu_custom_call" | custom-call | flops 12000000000 | bytes 12000000 | tf_op jit(solution)/shard_map/pallas_call | solution.py:78
  317.0 5.9 %collective-permute-done.37.refs_1_ = bf16[4,128,3200]{2,1,0:T(8,128)(2,1)S(1)} collective-permute-done((bf16[4,128,3200]{2,1,0:T(8,128)(2,1)}, bf16[4,128,3200]{2,1,0:T(8,128)(2,1)S(1)}, u32[]{:S(2)}, u32[]{:S(2)}) %collective-permute-start.37) | collective-permute-done | bytes 3276832 | tf_op jit(solution)/shard_map/ppermute | solution.py:110
  330.0 7.7 %reduce-scatter.2.cloned.1.call-done = bf16[1,6,192,1024]{3,2,1,0:T(8,128)(2,1)} async-done(((bf16[8,6,192,1024]{3,2,1,0:T(8,128)(2,1)}), bf16[1,6,192,1024]{3,2,1,0:T(8,128)(2,1)}) %reduce-scatter.2.cloned.1.call-update) | async-done | bytes 2359312 | tf_op jit(solution)/shard_map/reduce_scatter | solution.py:1089
  337.7 13.8 %shard_map.422 = (f32[8,128,1024]{2,1,0:T(8,128)}, f32[8,128,1024]{2,1,0:T(8,128)}, f32[8,128,1024]{2,1,0:T(8,128)}, f32[8,128,1024]{2,1,0:T(8,128)}, f32[8,64,1...) custom-call(s32[1]{0:T(128)} %bitcast.meta, ...), custom_call_target="tpu_custom_call" | custom-call | flops 8000000000 | bytes 8000000 | tf_op jit(solution)/shard_map/pallas_call | solution.py:78
  370.7 6.0 %all-to-all-start = ((bf16[4,32,3200]{2,1,0:T(8,128)(2,1)}), bf16[4,32,3200]{2,1,0:T(8,128)(2,1)S(1)}, u32[]{:S(2)}, u32[]{:S(2)}) async-start(bf16[4,32,3200]{2,1,0:T(8,128)(2,1)} %bitcast.14.refs_0_.refs_1_), calls=%async_computation.1 | async-start | bytes 1638400 | tf_op jit(solution)/shard_map/all_to_all | solution.py:1139
  376.8 6.3 %shard_map.430.refs_0_.refs_1_ = f32[256,1024]{1,0:T(8,128)} custom-call(s32[1]{0:T(128)} %bitcast.meta, bf16[4,32,3200]{2,1,0:T(8,128)(2,1)} %bitcast.14.refs_0_.refs_1_, bf16[256,1024]{1,0:T(8,128)(2,1)} %bitcast.47, bf16[256,1024]{1,0:T(8,128)(2,1)} %get-tuple-element.126.refs_4_.refs_2_, bf16[1024,1024]{1,0:T(8,128)(2,1)} %get-tuple-element.144.refs_3_, ...), custom_call_target="tpu_custom_call" | custom-call | flops 6000000000 | bytes 6000000 | tf_op jit(solution)/shard_map/pallas_call | solution.py:78
  401.2 5.3 %shard_map.436 = (f32[8,128,1024]{2,1,0:T(8,128)}, f32[8,128,1024]{2,1,0:T(8,128)}, f32[8,128,1024]{2,1,0:T(8,128)}, f32[8,128,1024]{2,1,0:T(8,128)}, f32[8,64,1...) custom-call(s32[1]{0:T(128)} %bitcast.meta, ...), custom_call_target="tpu_custom_call", output_to_operand_aliasing={{0}: (13, {}), {1}: (14, {}), {2}: (15, {}), {3}: (16, {}),... | custom-call | flops 8000000000 | bytes 8000000 | tf_op jit(solution)/shard_map/pallas_call | solution.py:78
  417.3 7.3 %shard_map.437 = (f32[2,128]{1,0:T(2,128)}, f32[2,128]{1,0:T(2,128)}, f32[2,128]{1,0:T(2,128)}, f32[2,128]{1,0:T(2,128)}, f32[128,2048]{1,0:T(8,128)}, /*index=5...) custom-call(s32[1]{0:T(128)} %bitcast.meta, ...), custom_call_target="tpu_custom_call" | custom-call | flops 5000000000 | bytes 5000000 | tf_op jit(solution)/shard_map/pallas_call | solution.py:78
  (317 shorter events, 145.7 us)
Async XLA Ops:
  7.2 148.6 %all-gather.6.cloned.1.call-start = ((), (), s32[]{:S(2)}) async-start(), calls=%async_computation.2 | async-start | bytes 2621440 | tf_op jit(solution)/shard_map/all_gather | solution.py:986
  8.0 147.9 %all-gather.10.cloned.1.call-start = ((), (), s32[]{:S(2)}) async-start(), calls=%async_computation.5 | async-start | bytes 21233664 | tf_op jit(solution)/shard_map/all_gather | solution.py:999
  38.5 166.0 %all-gather.8.cloned.1.call-start = ((), (), s32[]{:S(2)}) async-start(), calls=%async_computation.4 | async-start | bytes 7077888 | tf_op jit(solution)/shard_map/all_gather | solution.py:999
  39.6 298.1 %reduce-scatter.2.cloned.1.call-start = ((), (), s32[]{:S(2)}) async-start(), calls=%async_computation.3 | async-start | bytes 21233664 | tf_op jit(solution)/shard_map/reduce_scatter | solution.py:1089
  62.6 25.2 %collective-permute-start.18 = (bf16[256,1024]{1,0:T(8,128)(2,1)}, bf16[256,1024]{1,0:T(8,128)(2,1)S(1)}, u32[]{:S(2)}, u32[]{:S(2)}) collective-permute-start(bf16[256,1024]{1,0:T(8,128)(2,1)} %get-tuple-element.107.refs_4_.refs_14_), channel_id=1, source_target_pairs={{0,24},{8,0},{16,8},{24,16},{1,25},{9,1},{17,9},{25,17},{2,26},{10... | collective-permute-start | bytes 1572872 | tf_op jit(solution)/shard_map/ppermute | solution.py:115
  77.2 16.9 %collective-permute-start.19 = (bf16[128,1024]{1,0:T(8,128)(2,1)S(1)}, bf16[128,1024]{1,0:T(8,128)(2,1)S(1)}, u32[]{:S(2)}, u32[]{:S(2)}) collective-permute-start(bf16[128,1024]{1,0:T(8,128)(2,1)S(1)} %slice.140), channel_id=1, source_target_pairs={{0,8},{8,16},{16,24},{24,0},{1,9},{9,17},{17,25},{25,1},{2,10},{10... | collective-permute-start | bytes 786440 | tf_op jit(solution)/shard_map/ppermute | solution.py:115
  115.9 24.6 %collective-permute-start.22 = (bf16[256,1024]{1,0:T(8,128)(2,1)}, bf16[256,1024]{1,0:T(8,128)(2,1)S(1)}, u32[]{:S(2)}, u32[]{:S(2)}) collective-permute-start(bf16[256,1024]{1,0:T(8,128)(2,1)} %get-tuple-element.108.refs_5_.refs_1_), channel_id=1, source_target_pairs={{0,24},{8,0},{16,8},{24,16},{1,25},{9,1},{17,9},{25,17},{2,26},{10... | collective-permute-start | bytes 1572872 | tf_op jit(solution)/shard_map/ppermute | solution.py:115
  129.2 16.9 %collective-permute-start.23 = (bf16[128,1024]{1,0:T(8,128)(2,1)S(1)}, bf16[128,1024]{1,0:T(8,128)(2,1)S(1)}, u32[]{:S(2)}, u32[]{:S(2)}) collective-permute-start(bf16[128,1024]{1,0:T(8,128)(2,1)S(1)} %slice.142), channel_id=1, source_target_pairs={{0,8},{8,16},{16,24},{24,0},{1,9},{9,17},{17,25},{25,1},{2,10},{10... | collective-permute-start | bytes 786440 | tf_op jit(solution)/shard_map/ppermute | solution.py:115
  151.4 46.2 %collective-permute-start.32 = (bf16[256,1024]{1,0:T(8,128)(2,1)}, bf16[256,1024]{1,0:T(8,128)(2,1)S(1)}, u32[]{:S(2)}, u32[]{:S(2)}) collective-permute-start(bf16[256,1024]{1,0:T(8,128)(2,1)} %shard_map.417), channel_id=1, source_target_pairs={{0,8},{8,16},{16,24},{24,0},{1,9},{9,17},{17,25},{25,1},{2,10},{10... | collective-permute-start | bytes 1572872 | tf_op jit(solution)/shard_map/ppermute | solution.py:115
  152.0 45.7 %collective-permute-start.33 = (bf16[256,1024]{1,0:T(8,128)(2,1)}, bf16[256,1024]{1,0:T(8,128)(2,1)S(1)}, u32[]{:S(2)}, u32[]{:S(2)}) collective-permute-start(bf16[256,1024]{1,0:T(8,128)(2,1)} %shard_map.417), channel_id=1, source_target_pairs={{0,16},{8,24},{16,0},{24,8},{1,17},{9,25},{17,1},{25,9},{2,18},{10... | collective-permute-start | bytes 1572872 | tf_op jit(solution)/shard_map/ppermute | solution.py:115
  155.2 45.2 %collective-permute-start.34 = (bf16[256,1024]{1,0:T(8,128)(2,1)}, bf16[256,1024]{1,0:T(8,128)(2,1)S(1)}, u32[]{:S(2)}, u32[]{:S(2)}) collective-permute-start(bf16[256,1024]{1,0:T(8,128)(2,1)} %shard_map.417), channel_id=1, source_target_pairs={{0,24},{8,0},{16,8},{24,16},{1,25},{9,1},{17,9},{25,17},{2,26},{10... | collective-permute-start | bytes 1572872 | tf_op jit(solution)/shard_map/ppermute | solution.py:115
  227.0 29.7 %collective-permute-start.27 = (bf16[256,1152]{1,0:T(8,128)(2,1)}, bf16[256,1152]{1,0:T(8,128)(2,1)S(1)}, u32[]{:S(2)}, u32[]{:S(2)}) collective-permute-start(bf16[256,1152]{1,0:T(8,128)(2,1)} %get-tuple-element.115), channel_id=1, source_target_pairs={{0,8},{8,16},{16,24},{24,0},{1,9},{9,17},{17,25},{25,1},{2,10},{10... | collective-permute-start | bytes 1769480 | tf_op jit(solution)/shard_map/ppermute | solution.py:115
  276.0 19.3 %collective-permute-start.31 = (bf16[256,1024]{1,0:T(8,128)(2,1)}, bf16[256,1024]{1,0:T(8,128)(2,1)S(1)}, u32[]{:S(2)}, u32[]{:S(2)}) collective-permute-start(bf16[256,1024]{1,0:T(8,128)(2,1)} %shard_map.415), channel_id=1, source_target_pairs={{0,8},{8,16},{16,24},{24,0},{1,9},{9,17},{17,25},{25,1},{2,10},{10... | collective-permute-start | bytes 1572872 | tf_op jit(solution)/shard_map/ppermute | solution.py:115
  276.6 24.8 %collective-permute-start.30 = (bf16[256,1024]{1,0:T(8,128)(2,1)}, bf16[256,1024]{1,0:T(8,128)(2,1)S(1)}, u32[]{:S(2)}, u32[]{:S(2)}) collective-permute-start(bf16[256,1024]{1,0:T(8,128)(2,1)} %shard_map.414), channel_id=1, source_target_pairs={{0,24},{8,0},{16,8},{24,16},{1,25},{9,1},{17,9},{25,17},{2,26},{10... | collective-permute-start | bytes 1572872 | tf_op jit(solution)/shard_map/ppermute | solution.py:115
  295.4 19.5 %collective-permute-start.36 = (bf16[128,1024]{1,0:T(8,128)(2,1)S(1)}, bf16[128,1024]{1,0:T(8,128)(2,1)S(1)}, u32[]{:S(2)}, u32[]{:S(2)}) collective-permute-start(bf16[128,1024]{1,0:T(8,128)(2,1)S(1)} %add_convert_fusion.6), channel_id=1, source_target_pairs={{0,8},{8,16},{16,24},{24,0},{1,9},{9,17},{17,25},{25,1},{2,10},{10... | collective-permute-start | bytes 786440 | tf_op jit(solution)/shard_map/ppermute | solution.py:115
  325.6 26.0 %collective-permute-start.40 = (bf16[2,64,3200]{2,1,0:T(8,128)(2,1)S(1)}, bf16[2,64,3200]{2,1,0:T(8,128)(2,1)}, u32[]{:S(2)}, u32[]{:S(2)}) collective-permute-start(bf16[2,64,3200]{2,1,0:T(8,128)(2,1)S(1)} %get-tuple-element.141.refs_1_), channel_id=1, source_target_pairs={{0,4},{1,5},{2,6},{3,7},{4,0},{5,1},{6,2},{7,3},{8,12},{9,13},{10,... | collective-permute-start | bytes 2457608 | tf_op jit(solution)/shard_map/ppermute | solution.py:110
  326.6 25.0 %collective-permute-start.38 = (bf16[2,64,3200]{2,1,0:T(8,128)(2,1)S(1)}, bf16[2,64,3200]{2,1,0:T(8,128)(2,1)}, u32[]{:S(2)}, u32[]{:S(2)}) collective-permute-start(bf16[2,64,3200]{2,1,0:T(8,128)(2,1)S(1)} %get-tuple-element.140.refs_0_), channel_id=1, source_target_pairs={{0,2},{1,3},{2,0},{3,1},{4,6},{5,7},{6,4},{7,5},{8,10},{9,11},{10,... | collective-permute-start | bytes 2457608 | tf_op jit(solution)/shard_map/ppermute | solution.py:110
  328.0 27.5 %collective-permute-start.43 = (bf16[256,1024]{1,0:T(8,128)(2,1)}, bf16[256,1024]{1,0:T(8,128)(2,1)}, u32[]{:S(2)}, u32[]{:S(2)}) collective-permute-start(bf16[256,1024]{1,0:T(8,128)(2,1)} %shard_map.427), channel_id=1, source_target_pairs={{0,8},{8,16},{16,24},{24,0},{1,9},{9,17},{17,25},{25,1},{2,10},{10... | collective-permute-start | bytes 1572872 | tf_op jit(solution)/shard_map/ppermute | solution.py:115
  328.9 29.7 %collective-permute-start.42 = (bf16[256,1024]{1,0:T(8,128)(2,1)}, bf16[256,1024]{1,0:T(8,128)(2,1)}, u32[]{:S(2)}, u32[]{:S(2)}) collective-permute-start(bf16[256,1024]{1,0:T(8,128)(2,1)} %shard_map.425), channel_id=1, source_target_pairs={{0,24},{8,0},{16,8},{24,16},{1,25},{9,1},{17,9},{25,17},{2,26},{10... | collective-permute-start | bytes 1572872 | tf_op jit(solution)/shard_map/ppermute | solution.py:115
  356.5 20.2 %collective-permute-start.45 = (bf16[128,1024]{1,0:T(8,128)(2,1)S(1)}, bf16[128,1024]{1,0:T(8,128)(2,1)}, u32[]{:S(2)}, u32[]{:S(2)}) collective-permute-start(bf16[128,1024]{1,0:T(8,128)(2,1)S(1)} %add_convert_fusion.4.refs_2_), channel_id=1, source_target_pairs={{0,8},{8,16},{16,24},{24,0},{1,9},{9,17},{17,25},{25,1},{2,10},{10... | collective-permute-start | bytes 786440 | tf_op jit(solution)/shard_map/ppermute | solution.py:115
  359.8 17.0 %collective-permute-start.44 = (bf16[128,1024]{1,0:T(8,128)(2,1)S(1)}, bf16[128,1024]{1,0:T(8,128)(2,1)}, u32[]{:S(2)}, u32[]{:S(2)}) collective-permute-start(bf16[128,1024]{1,0:T(8,128)(2,1)S(1)} %add_convert_fusion.5.refs_1_), channel_id=1, source_target_pairs={{0,24},{8,0},{16,8},{24,16},{1,25},{9,1},{17,9},{25,17},{2,26},{10... | collective-permute-start | bytes 786440 | tf_op jit(solution)/shard_map/ppermute | solution.py:115
  368.4 18.0 %collective-permute-start.47 = (bf16[2,2,96,1024]{3,2,1,0:T(8,128)(2,1)S(1)}, bf16[2,2,96,1024]{3,2,1,0:T(8,128)(2,1)S(1)}, u32[]{:S(2)}, u32[]{:S(2)}) collective-permute-start(bf16[2,2,96,1024]{3,2,1,0:T(8,128)(2,1)S(1)} %copy-done.5), channel_id=1, source_target_pairs={{0,4},{1,5},{2,6},{3,7},{4,0},{5,1},{6,2},{7,3},{8,12},{9,13},{10,... | collective-permute-start | bytes 2359304 | tf_op jit(solution)/shard_map/ppermute | solution.py:110
  369.8 17.6 %collective-permute-start.46 = (bf16[2,2,96,1024]{3,2,1,0:T(8,128)(2,1)}, bf16[2,2,96,1024]{3,2,1,0:T(8,128)(2,1)}, u32[]{:S(2)}, u32[]{:S(2)}) collective-permute-start(bf16[2,2,96,1024]{3,2,1,0:T(8,128)(2,1)} %shard_map.431), channel_id=1, source_target_pairs={{0,2},{1,3},{2,0},{3,1},{4,6},{5,7},{6,4},{7,5},{8,10},{9,11},{10,... | collective-permute-start | bytes 2359304 | tf_op jit(solution)/shard_map/ppermute | solution.py:110
  370.7 21.7 %all-to-all-start = ((bf16[4,32,3200]{2,1,0:T(8,128)(2,1)}), bf16[4,32,3200]{2,1,0:T(8,128)(2,1)S(1)}, u32[]{:S(2)}, u32[]{:S(2)}) async-start(bf16[4,32,3200]{2,1,0:T(8,128)(2,1)} %bitcast.14.refs_0_.refs_1_), calls=%async_computation.1 | async-start | bytes 1638400 | tf_op jit(solution)/shard_map/all_to_all | solution.py:1139
  (103 other events, 758.3 us)
Sparse Core Ops, SparseCore 0:
  9.6 45.4 all-gather.5
  57.6 98.2 all-gather.9
  158.3 46.1 all-gather.7
  207.9 129.7 reduce-scatter.1

commit v5 on v4

--- a/solution.py
+++ b/solution.py
@@ -36,8 +36,8 @@
 def adam_update(weight, gradient, first, second, rate):
     first_new = beta_one * first + (1.0 - beta_one) * gradient
     second_new = beta_two * second + (1.0 - beta_two) * gradient * gradient
-    first_hat = first_new / (1.0 - beta_one**STEP)
-    second_hat = second_new / (1.0 - beta_two**STEP)
+    first_hat = first_new * (1.0 / (1.0 - beta_one**STEP))
+    second_hat = second_new * (1.0 / (1.0 - beta_two**STEP))
     fresh = weight - rate * (first_hat / (jnp.sqrt(second_hat) + adam_eps) + weight_decay * weight)
     return (fresh, first_new, second_new)
 
@@ -91,6 +91,56 @@
     )(scalars, *after, *ins)
 
 
+def streamed_call(body, outs, ins, scalars, scratch=(), after=(), micros=10, sends=32):
+    shapes = [a.shape for a in ins]
+    count, made = len(ins), len(outs)
+    anywhere = pl.BlockSpec(memory_space=pl.ANY)
+
+    def kernel(meta, *refs):
+        refs = refs[len(after) :]
+        source, target, refs = refs[:count], refs[count : count + made], refs[count + made :]
+        held, rest = refs[:count], refs[count:-2]
+        arrive, leave = refs[-2:]
+        inbound = [pltpu.make_async_copy(a, b, arrive.at[i]) for i, (a, b) in enumerate(zip(source, held))]
+        for copy in inbound:
+            copy.start()
+        waited, outbound = set(), []
+
+        def need(*wanted):
+            for ref in wanted:
+                i = next(i for i, b in enumerate(held) if b is ref)
+                if i not in waited:
+                    waited.add(i)
+                    inbound[i].wait()
+
+        def send(ref, place, columns=None):
+            to = target[place] if columns is None else target[place].at[:, :, columns]
+            copy = pltpu.make_async_copy(ref, to, leave.at[len(outbound)])
+            copy.start()
+            outbound.append(copy)
+
+        body(meta, need, send, *held, *rest)
+        need(*held)
+        for copy in outbound:
+            copy.wait()
+
+    return pl.pallas_call(
+        kernel,
+        out_shape=outs,
+        grid_spec=pltpu.PrefetchScalarGridSpec(
+            num_scalar_prefetch=1,
+            grid=(1,),
+            in_specs=[anywhere] * (len(after) + count),
+            out_specs=[anywhere] * made,
+            scratch_shapes=[pltpu.VMEM(shape, a.dtype) for shape, a in zip(shapes, ins)]
+            + list(scratch)
+            + [pltpu.SemaphoreType.DMA((count,)), pltpu.SemaphoreType.DMA((sends,))],
+        ),
+        compiler_params=pltpu.CompilerParams(vmem_limit_bytes=60 * 1024 * 1024),
+        cost_estimate=pl.CostEstimate(flops=micros * 10**9, bytes_accessed=micros * 10**6, transcendentals=0),
+    )(scalars, *after, *ins)
+
+
 def tie(value, *earlier):
     anywhere = pl.BlockSpec(memory_space=pl.ANY)
     return pl.pallas_call(
@@ -171,6 +221,21 @@
             (rest, 3, pair(2, 0)),
         ):
             ref[place, :, lanes] = value
+
+
+def passed_body(meta, rest, over_x, over_y, then_x, then_y):
+    then_x[...] = (rest[2].astype(f32) + over_y[0].astype(f32)).astype(bf16)
+    then_y[...] = (rest[3].astype(f32) + over_x[0].astype(f32)).astype(bf16)
+
+
+def summed_body(meta, rest, over_x, over_y, then_x, then_y, total):
+    half = rest.shape[1]
+    first = (rest[0].astype(f32) + over_x[1].astype(f32) + then_y[...].astype(f32)).astype(bf16)
+    second = (rest[1].astype(f32) + over_y[1].astype(f32) + then_x[...].astype(f32)).astype(bf16)
+    places, rows = total.shape[:2]
+    for k in range(places):
+        source, row = (first, k * rows) if k * rows < half else (second, k * rows - half)
+        total[k] = source[row : row + rows]
 
 
 class Scattered:
@@ -853,37 +918,33 @@
     grad_ref[...] = gh_ref[...] + part
 
 
-def dense_update_body(count, rates, meta, *refs):
+def dense_update_body(count, rates, meta, need, send, *refs):
     quarters, refs = refs[:count], refs[count:]
-    ins, outs, rest_s, gain_s = refs[:12], refs[12:28], refs[28], refs[29]
+    ins, outs, total_s = refs[:12], refs[12:28], refs[28]
     rows = quarters[0].shape[0]
-    step = pl.program_id(0)
 
     def update(i, gradient):
         weight, first, second = [r[...] for r in ins[3 * i : 3 * i + 3]]
         values = (gradient, *adam_update(weight, gradient, first, second, rates[i]))
-        for ref, value in zip(outs[4 * i : 4 * i + 4], values):
+        for at, (ref, value) in enumerate(zip(outs[4 * i : 4 * i + 4], values)):
             ref[...] = value
-
+            send(ref, 4 * i + at)
+
+    need(*quarters)
     for k in range(count):
-
-        @pl.when(step == k)
-        def part(k=k):
-            at = pl.ds(pl.multiple_of(lax.rem(meta[0] - k + count, count) * rows, rows), rows)
-            gradient = quarters[k][...].astype(f32)
-            qkv = gradient[:, : 2 * MODEL_WIDTH]
-            product = jnp.sum(qkv * ins[3][...].astype(bf16).astype(f32), axis=1, keepdims=True)
-            gain_s[at, :] = jnp.broadcast_to(product, (rows, LANES))
-            rest_s[at, :] = gradient[:, 3 * MODEL_WIDTH :]
-            update(1, qkv)
-            update(2, gradient[:, 2 * MODEL_WIDTH : 3 * MODEL_WIDTH])
-
-    @pl.when(step == count - 1)
-    def small():
-        rest = rest_s[...].T
-        first = gain_s[...].T[0:1] / ins[0][0:1, :].astype(bf16).astype(f32)
-        update(0, jnp.concatenate([first, rest[EXPERTS + 1 : EXPERTS + 2]], axis=0))
-        update(3, rest[:EXPERTS])
+        at = pl.ds(pl.multiple_of(lax.rem(meta[0] - k + count, count) * rows, rows), rows)
+        total_s[at, :] = quarters[k][...].astype(f32)
+    need(*ins[3:6])
+    qkv = total_s[:, : 2 * MODEL_WIDTH]
+    update(1, qkv)
+    product = jnp.sum(qkv * ins[3][...].astype(bf16).astype(f32), axis=1, keepdims=True)
+    need(*ins[6:9])
+    update(2, total_s[:, 2 * MODEL_WIDTH : 3 * MODEL_WIDTH])
+    need(*ins[:3], *ins[9:])
+    rest = total_s[:, 3 * MODEL_WIDTH :].T
+    first = jnp.broadcast_to(product, (product.shape[0], LANES)).T[0:1] / ins[0][0:1, :].astype(bf16).astype(f32)
+    update(0, jnp.concatenate([first, rest[EXPERTS + 1 : EXPERTS + 2]], axis=0))
+    update(3, rest[:EXPERTS])
 
 
 def output_body(meta, h_ref, *refs):
@@ -1154,26 +1215,16 @@
     updated = experts_update(chunks[1][0], late_sum.total(), experts, rates, updated, place_meta, (quarter,))
     dense_ins = [norm_gains, mean_gains, square_gains, qkv_weight, mean_qkv, square_qkv]
     dense_ins += [out_weight, mean_out, square_out, router_weight.T, mean_router.T, square_router.T]
-    part_rows = shard_rows // count
-
-    def whole_spec(a):
-        return pl.BlockSpec(a.shape, lambda k, m: (0,) * a.ndim)
-
-    def part_spec(a):
-        return pl.BlockSpec((part_rows, a.shape[1]), lambda k, m: (lax.rem(m[0] - k + count, count), 0))
-
-    specs = [whole_spec, part_spec, part_spec, whole_spec]
-    dense_outs = kernel_call(
+    dense_shapes = [shape_of(a.shape, f32) for a in dense_ins[::3] for _ in range(4)]
+    dense_outs = streamed_call(
         functools.partial(dense_update_body, count, learn_rates[:4]),
-        [shape_of(a.shape, f32) for a in dense_ins[::3] for _ in range(4)],
+        dense_shapes,
         quarters + dense_ins,
         place_meta,
-        scratch=[pltpu.VMEM((shard_rows, LANES), f32), pltpu.VMEM((shard_rows, LANES), f32)],
-        grid=(count,),
-        in_specs=[whole_spec(a) for a in quarters] + [specs[i // 3](a) for i, a in enumerate(dense_ins)],
-        out_specs=[specs[i](dense_ins[3 * i]) for i in range(4) for _ in range(4)],
+        scratch=[pltpu.VMEM(a.shape, f32) for a in dense_shapes]
+        + [pltpu.VMEM((shard_rows, 3 * MODEL_WIDTH + LANES), f32)],
         after=(updated[0],),
-        limit=60, micros=5,
+        micros=5,
     )
     shard_gains, fresh_gains, momentum_gains, variance_gains = dense_outs[:4]
     shard_qkv, fresh_qkv, momentum_qkv, variance_qkv = dense_outs[4:8]

time: 440 us -> 440 us (level)
    pallas_call x14 -> x13, Pallas kernels: 158 us -> 150 us  [kernel_call(): pl.pallas_call(ordered_body, out_shape=outs, grid_spec=pltpu.PrefetchScal...]
    pallas_call x0 -> x1, Pallas kernels: none -> 6.67 us  [streamed_call(): pl.pallas_call(kernel, out_shape=outs, grid_spec=pltpu.PrefetchScalarGrid...]
where the time goes in v5:
time: 440 us; the launch traced here: 431 us
  Pallas kernels  157 us (36%)
  waiting for transfers between devices  155 us (35%)
  starting transfers between devices  61.3 us (14%)
  local copies, waits for them, and re-layouts  22.1 us (5%)
  other arithmetic  20.7 us (5%)
  between operations  15.1 us (3%)
    pallas_call x13, Pallas kernels, kernel_call(): pl.pallas_call(ordered_body, out_shape=outs, grid_spec=pltpu.PrefetchScal...  150 us
    ppermute x29, waiting for transfers between devices, shift_permute(): lax.ppermute(value, axis, [(i, (i + step) % size) for i in range(size)])  114 us
    ppermute x29, starting transfers between devices, shift_permute(): lax.ppermute(value, axis, [(i, (i + step) % size) for i in range(size)])  38.6 us
    ppermute x24, waiting for transfers between devices, xor_permute(): lax.ppermute(value, axis, [(i, i ^ mask) for i in range(lax.axis_size(axi...  28.2 us
    unnamed x141, local copies, waits for them, and re-layouts  18.4 us
    ppermute x24, starting transfers between devices, xor_permute(): lax.ppermute(value, axis, [(i, i ^ mask) for i in range(lax.axis_size(axi...  16.5 us
  transfers between devices with their start and end apart: 58, of which 32 were waited for; matrix products, arithmetic and copies ran while one was open for 6% of the time, Pallas kernels for 35%

profile of v5, /device:TPU:12, one launch (start us, length us, event | category | flops | bytes accessed | tf_op | source)
XLA Modules:
  0.0 431.0 jit_solution(5647700734752314087)
XLA Ops:
  41.6 6.5 %collective-permute-done.4.refs_4_ = bf16[64,3200]{1,0:T(8,128)(2,1)S(1)} collective-permute-done((bf16[64,3200]{1,0:T(8,128)(2,1)S(1)}, bf16[64,3200]{1,0:T(8,128)(2,1)S(1)}, u32[]{:S(2)}, u32[]{:S(2)}) %collective-permute-start.4) | collective-permute-done | bytes 409632 | tf_op jit(solution)/shard_map/ppermute | solution.py:160
  53.2 9.0 %shard_map.406 = (bf16[1024,1024]{1,0:T(8,128)(2,1)}, bf16[1024,1024]{1,0:T(8,128)(2,1)}, bf16[1024,1024]{1,0:T(8,128)(2,1)}, f32[128,1024]{1,0:T(8,128)}, bf16[...) custom-call(s32[9]{0:T(128)} %pad_add_fusion.meta, bf16[256,1024]{1,0:T(8,128)(2,1)} %bitcast.45, ...), custom_call_target="tpu_custom_call" | custom-call | flops 8000000000 | bytes 8000000 | tf_op jit(solution)/shard_map/pallas_call | solution.py:78
  64.2 12.9 %collective-permute-done.17.refs_5_.refs_15_ = bf16[256,1024]{1,0:T(8,128)(2,1)S(1)} collective-permute-done((bf16[256,1024]{1,0:T(8,128)(2,1)}, bf16[256,1024]{1,0:T(8,128)(2,1)S(1)}, u32[]{:S(2)}, u32[]{:S(2)}) %collective-permute-start.17) | collective-permute-done | bytes 524320 | tf_op jit(solution)/shard_map/ppermute | solution.py:165
  77.3 10.6 %collective-permute-done.18.refs_6_.refs_16_ = bf16[256,1024]{1,0:T(8,128)(2,1)S(1)} collective-permute-done((bf16[256,1024]{1,0:T(8,128)(2,1)}, bf16[256,1024]{1,0:T(8,128)(2,1)S(1)}, u32[]{:S(2)}, u32[]{:S(2)}) %collective-permute-start.18) | collective-permute-done | bytes 524320 | tf_op jit(solution)/shard_map/ppermute | solution.py:165
  94.1 6.6 %collective-permute-done.20.refs_8_.refs_18_ = bf16[128,1024]{1,0:T(8,128)(2,1)S(1)} collective-permute-done((bf16[128,1024]{1,0:T(8,128)(2,1)S(1)}, bf16[128,1024]{1,0:T(8,128)(2,1)S(1)}, u32[]{:S(2)}, u32[]{:S(2)}) %collective-permute-start.20) | collective-permute-done | bytes 262176 | tf_op jit(solution)/shard_map/ppermute | solution.py:165
  101.4 12.8 %shard_map.408 = (bf16[256,1024]{1,0:T(8,128)(2,1)}, f32[8,512]{1,0:T(8,128)}, f32[256,1024]{1,0:T(8,128)}, bf16[256,1024]{1,0:T(8,128)(2,1)}) custom-call(s32[1]{0:T(128)} %bitcast.meta, bf16[256,1024]{1,0:T(8,128)(2,1)} %get-tuple-element.105.refs_0_.refs_7_, bf16[256,1024]{1,0:T(8,128)(2,1)} %bitcast.46, ...), custom_call_target="tpu_custom_call" | custom-call | flops 12000000000 | bytes 12000000 | tf_op jit(solution)/shard_map/pallas_call | solution.py:78
  116.2 13.0 %collective-permute-done.21.refs_6_.refs_1_ = bf16[256,1024]{1,0:T(8,128)(2,1)S(1)} collective-permute-done((bf16[256,1024]{1,0:T(8,128)(2,1)}, bf16[256,1024]{1,0:T(8,128)(2,1)S(1)}, u32[]{:S(2)}, u32[]{:S(2)}) %collective-permute-start.21) | collective-permute-done | bytes 524320 | tf_op jit(solution)/shard_map/ppermute | solution.py:165
  129.3 11.3 %collective-permute-done.22.refs_7_.refs_2_ = bf16[256,1024]{1,0:T(8,128)(2,1)S(1)} collective-permute-done((bf16[256,1024]{1,0:T(8,128)(2,1)}, bf16[256,1024]{1,0:T(8,128)(2,1)S(1)}, u32[]{:S(2)}, u32[]{:S(2)}) %collective-permute-start.22) | collective-permute-done | bytes 524320 | tf_op jit(solution)/shard_map/ppermute | solution.py:165
  146.1 4.6 %collective-permute-done.24.refs_9_.refs_4_ = bf16[128,1024]{1,0:T(8,128)(2,1)S(1)} collective-permute-done((bf16[128,1024]{1,0:T(8,128)(2,1)S(1)}, bf16[128,1024]{1,0:T(8,128)(2,1)S(1)}, u32[]{:S(2)}, u32[]{:S(2)}) %collective-permute-start.24) | collective-permute-done | bytes 262176 | tf_op jit(solution)/shard_map/ppermute | solution.py:165
  155.9 41.8 %shard_map.410 = (bf16[8,6,192,1024]{3,2,1,0:T(8,128)(2,1)}, bf16[4,256,1024]{2,1,0:T(8,128)(2,1)}, bf16[4,256,1152]{2,1,0:T(8,128)(2,1)}) custom-call(s32[9]{0:T(128)} %pad_add_fusion.meta, f32[4,256,128]{2,1,0:T(8,128)} %get-tuple-element.197.refs_1_.refs_17_.refs_0_.refs_19_.refs_7_.refs_12_, ...), custom_call_target="tpu_custom_call" | custom-call | flops 48000000000 | bytes 48000000 | tf_op jit(solution)/shard_map/pallas_call | solution.py:78
  204.5 22.0 %shard_map.411 = (bf16[4,2,192,1024]{3,2,1,0:T(8,128)(2,1)}, bf16[4,2,192,1024]{3,2,1,0:T(8,128)(2,1)}, bf16[256,1024]{1,0:T(8,128)(2,1)}, bf16[256,1024]{1,0:T(...) custom-call(s32[9]{0:T(128)} %pad_add_fusion.meta, ...), custom_call_target="tpu_custom_call" | custom-call | flops 16000000000 | bytes 16000000 | tf_op jit(solution)/shard_map/pallas_call | solution.py:78
  228.5 13.7 %collective-permute-done.25.refs_1_.refs_10_ = bf16[256,1152]{1,0:T(8,128)(2,1)S(1)} collective-permute-done((bf16[256,1152]{1,0:T(8,128)(2,1)}, bf16[256,1152]{1,0:T(8,128)(2,1)S(1)}, u32[]{:S(2)}, u32[]{:S(2)}) %collective-permute-start.25) | collective-permute-done | bytes 589856 | tf_op jit(solution)/shard_map/ppermute | solution.py:165
  242.2 14.5 %collective-permute-done.27.refs_2_.refs_11_ = bf16[256,1152]{1,0:T(8,128)(2,1)S(1)} collective-permute-done((bf16[256,1152]{1,0:T(8,128)(2,1)}, bf16[256,1152]{1,0:T(8,128)(2,1)S(1)}, u32[]{:S(2)}, u32[]{:S(2)}) %collective-permute-start.27) | collective-permute-done | bytes 589856 | tf_op jit(solution)/shard_map/ppermute | solution.py:165
  263.6 4.7 %shard_map.413 = (bf16[2,2,96,1024]{3,2,1,0:T(8,128)(2,1)}, bf16[2,2,96,1024]{3,2,1,0:T(8,128)(2,1)}, bf16[4,2,96,1024]{3,2,1,0:T(8,128)(2,1)}) custom-call(s32[1]{0:T(128)} %bitcast.meta, bf16[128,1152]{1,0:T(8,128)(2,1)} %copy-done.42, bf16[128,1152]{1,0:T(8,128)(2,1)} %copy-done.41, bf16[4,2,192,1024]{3,2,1,0:T(8,128)(2,1)} %get-tuple-element.116.refs_2_, ...), custom_call_target="tpu_custom_call" | custom-call | flops 6000000000 | bytes 6000000 | tf_op jit(solution)/shard_map/pallas_call | solution.py:78
  269.6 5.7 %collective-permute-done.26.refs_1_.refs_12_ = bf16[128,1152]{1,0:T(8,128)(2,1)S(1)} collective-permute-done((bf16[128,1152]{1,0:T(8,128)(2,1)S(1)}, bf16[128,1152]{1,0:T(8,128)(2,1)S(1)}, u32[]{:S(2)}, u32[]{:S(2)}) %collective-permute-start.26) | collective-permute-done | bytes 294944 | tf_op jit(solution)/shard_map/ppermute | solution.py:165
  278.0 17.2 %shard_map.416 = (f32[256,1024]{1,0:T(8,128)}, bf16[256,1024]{1,0:T(8,128)(2,1)}, bf16[256,1024]{1,0:T(8,128)(2,1)}, f32[1024,128]{1,0:T(8,128)}, f32[8,1024]{1,...) custom-call(s32[1]{0:T(128)} %bitcast.meta, ...), custom_call_target="tpu_custom_call" | custom-call | flops 22000001024 | bytes 22000000 | tf_op jit(solution)/shard_map/pallas_call | solution.py:78
  303.3 11.6 %shard_map.418 = (bf16[4,128,3200]{2,1,0:T(8,128)(2,1)}, bf16[4,128,3200]{2,1,0:T(8,128)(2,1)}) custom-call(s32[9]{0:T(128)} %pad_add_fusion.meta, bf16[256,1024]{1,0:T(8,128)(2,1)} %copy-done.51, bf16[256,1024]{1,0:T(8,128)(2,1)} %copy-done.50, bf16[256,1024]{1,0:T(8,128)(2,1)} %get-tuple-element.121.refs_5_.refs_2_, ...), custom_call_target="tpu_custom_call" | custom-call | flops 12000000000 | bytes 12000000 | tf_op jit(solution)/shard_map/pallas_call | solution.py:78
  317.0 5.9 %collective-permute-done.37.refs_1_ = bf16[4,128,3200]{2,1,0:T(8,128)(2,1)S(1)} collective-permute-done((bf16[4,128,3200]{2,1,0:T(8,128)(2,1)}, bf16[4,128,3200]{2,1,0:T(8,128)(2,1)S(1)}, u32[]{:S(2)}, u32[]{:S(2)}) %collective-permute-start.37) | collective-permute-done | bytes 3276832 | tf_op jit(solution)/shard_map/ppermute | solution.py:160
  330.0 7.7 %reduce-scatter.2.cloned.1.call-done = bf16[1,6,192,1024]{3,2,1,0:T(8,128)(2,1)} async-done(((bf16[8,6,192,1024]{3,2,1,0:T(8,128)(2,1)}), bf16[1,6,192,1024]{3,2,1,0:T(8,128)(2,1)}) %reduce-scatter.2.cloned.1.call-update) | async-done | bytes 2359312 | tf_op jit(solution)/shard_map/reduce_scatter | solution.py:1150
  337.7 13.8 %shard_map.422 = (f32[8,128,1024]{2,1,0:T(8,128)}, f32[8,128,1024]{2,1,0:T(8,128)}, f32[8,128,1024]{2,1,0:T(8,128)}, f32[8,128,1024]{2,1,0:T(8,128)}, f32[8,64,1...) custom-call(s32[1]{0:T(128)} %bitcast.meta, ...), custom_call_target="tpu_custom_call" | custom-call | flops 8000000000 | bytes 8000000 | tf_op jit(solution)/shard_map/pallas_call | solution.py:78
  370.7 6.0 %all-to-all-start = ((bf16[4,32,3200]{2,1,0:T(8,128)(2,1)}), bf16[4,32,3200]{2,1,0:T(8,128)(2,1)S(1)}, u32[]{:S(2)}, u32[]{:S(2)}) async-start(bf16[4,32,3200]{2,1,0:T(8,128)(2,1)} %bitcast.14.refs_0_.refs_1_), calls=%async_computation.1 | async-start | bytes 1638400 | tf_op jit(solution)/shard_map/all_to_all | solution.py:1200
  376.8 6.3 %shard_map.430.refs_0_.refs_1_ = f32[256,1024]{1,0:T(8,128)} custom-call(s32[1]{0:T(128)} %bitcast.meta, bf16[4,32,3200]{2,1,0:T(8,128)(2,1)} %bitcast.14.refs_0_.refs_1_, bf16[256,1024]{1,0:T(8,128)(2,1)} %bitcast.47, bf16[256,1024]{1,0:T(8,128)(2,1)} %get-tuple-element.126.refs_4_.refs_2_, bf16[1024,1024]{1,0:T(8,128)(2,1)} %get-tuple-element.144.refs_3_, ...), custom_call_target="tpu_custom_call" | custom-call | flops 6000000000 | bytes 6000000 | tf_op jit(solution)/shard_map/pallas_call | solution.py:78
  401.2 5.3 %shard_map.436 = (f32[8,128,1024]{2,1,0:T(8,128)}, f32[8,128,1024]{2,1,0:T(8,128)}, f32[8,128,1024]{2,1,0:T(8,128)}, f32[8,128,1024]{2,1,0:T(8,128)}, f32[8,64,1...) custom-call(s32[1]{0:T(128)} %bitcast.meta, ...), custom_call_target="tpu_custom_call", output_to_operand_aliasing={{0}: (13, {}), {1}: (14, {}), {2}: (15, {}), {3}: (16, {}),... | custom-call | flops 8000000000 | bytes 8000000 | tf_op jit(solution)/shard_map/pallas_call | solution.py:78
  417.3 6.7 %shard_map.437 = (f32[2,128]{1,0:T(2,128)}, f32[2,128]{1,0:T(2,128)}, f32[2,128]{1,0:T(2,128)}, f32[2,128]{1,0:T(2,128)}, f32[128,2048]{1,0:T(8,128)}, /*index=5...) custom-call(s32[1]{0:T(128)} %bitcast.meta, ...), custom_call_target="tpu_custom_call" | custom-call | flops 5000000000 | bytes 5000000 | tf_op jit(solution)/shard_map/pallas_call | solution.py:127
  (317 shorter events, 145.7 us)
Async XLA Ops:
  7.2 148.6 %all-gather.6.cloned.1.call-start = ((), (), s32[]{:S(2)}) async-start(), calls=%async_computation.2 | async-start | bytes 2621440 | tf_op jit(solution)/shard_map/all_gather | solution.py:1047
  8.0 147.9 %all-gather.10.cloned.1.call-start = ((), (), s32[]{:S(2)}) async-start(), calls=%async_computation.5 | async-start | bytes 21233664 | tf_op jit(solution)/shard_map/all_gather | solution.py:1060
  38.5 166.0 %all-gather.8.cloned.1.call-start = ((), (), s32[]{:S(2)}) async-start(), calls=%async_computation.4 | async-start | bytes 7077888 | tf_op jit(solution)/shard_map/all_gather | solution.py:1060
  39.6 298.1 %reduce-scatter.2.cloned.1.call-start = ((), (), s32[]{:S(2)}) async-start(), calls=%async_computation.3 | async-start | bytes 21233664 | tf_op jit(solution)/shard_map/reduce_scatter | solution.py:1150
  62.6 25.2 %collective-permute-start.18 = (bf16[256,1024]{1,0:T(8,128)(2,1)}, bf16[256,1024]{1,0:T(8,128)(2,1)S(1)}, u32[]{:S(2)}, u32[]{:S(2)}) collective-permute-start(bf16[256,1024]{1,0:T(8,128)(2,1)} %get-tuple-element.107.refs_4_.refs_14_), channel_id=1, source_target_pairs={{0,24},{8,0},{16,8},{24,16},{1,25},{9,1},{17,9},{25,17},{2,26},{10... | collective-permute-start | bytes 1572872 | tf_op jit(solution)/shard_map/ppermute | solution.py:165
  77.2 16.9 %collective-permute-start.19 = (bf16[128,1024]{1,0:T(8,128)(2,1)S(1)}, bf16[128,1024]{1,0:T(8,128)(2,1)S(1)}, u32[]{:S(2)}, u32[]{:S(2)}) collective-permute-start(bf16[128,1024]{1,0:T(8,128)(2,1)S(1)} %slice.140), channel_id=1, source_target_pairs={{0,8},{8,16},{16,24},{24,0},{1,9},{9,17},{17,25},{25,1},{2,10},{10... | collective-permute-start | bytes 786440 | tf_op jit(solution)/shard_map/ppermute | solution.py:165
  115.9 24.6 %collective-permute-start.22 = (bf16[256,1024]{1,0:T(8,128)(2,1)}, bf16[256,1024]{1,0:T(8,128)(2,1)S(1)}, u32[]{:S(2)}, u32[]{:S(2)}) collective-permute-start(bf16[256,1024]{1,0:T(8,128)(2,1)} %get-tuple-element.108.refs_5_.refs_1_), channel_id=1, source_target_pairs={{0,24},{8,0},{16,8},{24,16},{1,25},{9,1},{17,9},{25,17},{2,26},{10... | collective-permute-start | bytes 1572872 | tf_op jit(solution)/shard_map/ppermute | solution.py:165
  129.2 16.9 %collective-permute-start.23 = (bf16[128,1024]{1,0:T(8,128)(2,1)S(1)}, bf16[128,1024]{1,0:T(8,128)(2,1)S(1)}, u32[]{:S(2)}, u32[]{:S(2)}) collective-permute-start(bf16[128,1024]{1,0:T(8,128)(2,1)S(1)} %slice.142), channel_id=1, source_target_pairs={{0,8},{8,16},{16,24},{24,0},{1,9},{9,17},{17,25},{25,1},{2,10},{10... | collective-permute-start | bytes 786440 | tf_op jit(solution)/shard_map/ppermute | solution.py:165
  151.4 46.2 %collective-permute-start.32 = (bf16[256,1024]{1,0:T(8,128)(2,1)}, bf16[256,1024]{1,0:T(8,128)(2,1)S(1)}, u32[]{:S(2)}, u32[]{:S(2)}) collective-permute-start(bf16[256,1024]{1,0:T(8,128)(2,1)} %shard_map.417), channel_id=1, source_target_pairs={{0,8},{8,16},{16,24},{24,0},{1,9},{9,17},{17,25},{25,1},{2,10},{10... | collective-permute-start | bytes 1572872 | tf_op jit(solution)/shard_map/ppermute | solution.py:165
  152.0 45.7 %collective-permute-start.33 = (bf16[256,1024]{1,0:T(8,128)(2,1)}, bf16[256,1024]{1,0:T(8,128)(2,1)S(1)}, u32[]{:S(2)}, u32[]{:S(2)}) collective-permute-start(bf16[256,1024]{1,0:T(8,128)(2,1)} %shard_map.417), channel_id=1, source_target_pairs={{0,16},{8,24},{16,0},{24,8},{1,17},{9,25},{17,1},{25,9},{2,18},{10... | collective-permute-start | bytes 1572872 | tf_op jit(solution)/shard_map/ppermute | solution.py:165
  155.2 45.2 %collective-permute-start.34 = (bf16[256,1024]{1,0:T(8,128)(2,1)}, bf16[256,1024]{1,0:T(8,128)(2,1)S(1)}, u32[]{:S(2)}, u32[]{:S(2)}) collective-permute-start(bf16[256,1024]{1,0:T(8,128)(2,1)} %shard_map.417), channel_id=1, source_target_pairs={{0,24},{8,0},{16,8},{24,16},{1,25},{9,1},{17,9},{25,17},{2,26},{10... | collective-permute-start | bytes 1572872 | tf_op jit(solution)/shard_map/ppermute | solution.py:165
  227.0 29.7 %collective-permute-start.27 = (bf16[256,1152]{1,0:T(8,128)(2,1)}, bf16[256,1152]{1,0:T(8,128)(2,1)S(1)}, u32[]{:S(2)}, u32[]{:S(2)}) collective-permute-start(bf16[256,1152]{1,0:T(8,128)(2,1)} %get-tuple-element.115), channel_id=1, source_target_pairs={{0,8},{8,16},{16,24},{24,0},{1,9},{9,17},{17,25},{25,1},{2,10},{10... | collective-permute-start | bytes 1769480 | tf_op jit(solution)/shard_map/ppermute | solution.py:165
  276.0 19.3 %collective-permute-start.31 = (bf16[256,1024]{1,0:T(8,128)(2,1)}, bf16[256,1024]{1,0:T(8,128)(2,1)S(1)}, u32[]{:S(2)}, u32[]{:S(2)}) collective-permute-start(bf16[256,1024]{1,0:T(8,128)(2,1)} %shard_map.415), channel_id=1, source_target_pairs={{0,8},{8,16},{16,24},{24,0},{1,9},{9,17},{17,25},{25,1},{2,10},{10... | collective-permute-start | bytes 1572872 | tf_op jit(solution)/shard_map/ppermute | solution.py:165
  276.6 24.8 %collective-permute-start.30 = (bf16[256,1024]{1,0:T(8,128)(2,1)}, bf16[256,1024]{1,0:T(8,128)(2,1)S(1)}, u32[]{:S(2)}, u32[]{:S(2)}) collective-permute-start(bf16[256,1024]{1,0:T(8,128)(2,1)} %shard_map.414), channel_id=1, source_target_pairs={{0,24},{8,0},{16,8},{24,16},{1,25},{9,1},{17,9},{25,17},{2,26},{10... | collective-permute-start | bytes 1572872 | tf_op jit(solution)/shard_map/ppermute | solution.py:165
  295.4 19.5 %collective-permute-start.36 = (bf16[128,1024]{1,0:T(8,128)(2,1)S(1)}, bf16[128,1024]{1,0:T(8,128)(2,1)S(1)}, u32[]{:S(2)}, u32[]{:S(2)}) collective-permute-start(bf16[128,1024]{1,0:T(8,128)(2,1)S(1)} %add_convert_fusion.6), channel_id=1, source_target_pairs={{0,8},{8,16},{16,24},{24,0},{1,9},{9,17},{17,25},{25,1},{2,10},{10... | collective-permute-start | bytes 786440 | tf_op jit(solution)/shard_map/ppermute | solution.py:165
  325.6 26.0 %collective-permute-start.40 = (bf16[2,64,3200]{2,1,0:T(8,128)(2,1)S(1)}, bf16[2,64,3200]{2,1,0:T(8,128)(2,1)}, u32[]{:S(2)}, u32[]{:S(2)}) collective-permute-start(bf16[2,64,3200]{2,1,0:T(8,128)(2,1)S(1)} %get-tuple-element.141.refs_1_), channel_id=1, source_target_pairs={{0,4},{1,5},{2,6},{3,7},{4,0},{5,1},{6,2},{7,3},{8,12},{9,13},{10,... | collective-permute-start | bytes 2457608 | tf_op jit(solution)/shard_map/ppermute | solution.py:160
  326.6 25.0 %collective-permute-start.38 = (bf16[2,64,3200]{2,1,0:T(8,128)(2,1)S(1)}, bf16[2,64,3200]{2,1,0:T(8,128)(2,1)}, u32[]{:S(2)}, u32[]{:S(2)}) collective-permute-start(bf16[2,64,3200]{2,1,0:T(8,128)(2,1)S(1)} %get-tuple-element.140.refs_0_), channel_id=1, source_target_pairs={{0,2},{1,3},{2,0},{3,1},{4,6},{5,7},{6,4},{7,5},{8,10},{9,11},{10,... | collective-permute-start | bytes 2457608 | tf_op jit(solution)/shard_map/ppermute | solution.py:160
  328.0 27.5 %collective-permute-start.43 = (bf16[256,1024]{1,0:T(8,128)(2,1)}, bf16[256,1024]{1,0:T(8,128)(2,1)}, u32[]{:S(2)}, u32[]{:S(2)}) collective-permute-start(bf16[256,1024]{1,0:T(8,128)(2,1)} %shard_map.427), channel_id=1, source_target_pairs={{0,8},{8,16},{16,24},{24,0},{1,9},{9,17},{17,25},{25,1},{2,10},{10... | collective-permute-start | bytes 1572872 | tf_op jit(solution)/shard_map/ppermute | solution.py:165
  328.9 29.7 %collective-permute-start.42 = (bf16[256,1024]{1,0:T(8,128)(2,1)}, bf16[256,1024]{1,0:T(8,128)(2,1)}, u32[]{:S(2)}, u32[]{:S(2)}) collective-permute-start(bf16[256,1024]{1,0:T(8,128)(2,1)} %shard_map.425), channel_id=1, source_target_pairs={{0,24},{8,0},{16,8},{24,16},{1,25},{9,1},{17,9},{25,17},{2,26},{10... | collective-permute-start | bytes 1572872 | tf_op jit(solution)/shard_map/ppermute | solution.py:165
  356.5 20.2 %collective-permute-start.45 = (bf16[128,1024]{1,0:T(8,128)(2,1)S(1)}, bf16[128,1024]{1,0:T(8,128)(2,1)}, u32[]{:S(2)}, u32[]{:S(2)}) collective-permute-start(bf16[128,1024]{1,0:T(8,128)(2,1)S(1)} %add_convert_fusion.4.refs_2_), channel_id=1, source_target_pairs={{0,8},{8,16},{16,24},{24,0},{1,9},{9,17},{17,25},{25,1},{2,10},{10... | collective-permute-start | bytes 786440 | tf_op jit(solution)/shard_map/ppermute | solution.py:165
  359.8 17.0 %collective-permute-start.44 = (bf16[128,1024]{1,0:T(8,128)(2,1)S(1)}, bf16[128,1024]{1,0:T(8,128)(2,1)}, u32[]{:S(2)}, u32[]{:S(2)}) collective-permute-start(bf16[128,1024]{1,0:T(8,128)(2,1)S(1)} %add_convert_fusion.5.refs_1_), channel_id=1, source_target_pairs={{0,24},{8,0},{16,8},{24,16},{1,25},{9,1},{17,9},{25,17},{2,26},{10... | collective-permute-start | bytes 786440 | tf_op jit(solution)/shard_map/ppermute | solution.py:165
  368.4 18.0 %collective-permute-start.47 = (bf16[2,2,96,1024]{3,2,1,0:T(8,128)(2,1)S(1)}, bf16[2,2,96,1024]{3,2,1,0:T(8,128)(2,1)S(1)}, u32[]{:S(2)}, u32[]{:S(2)}) collective-permute-start(bf16[2,2,96,1024]{3,2,1,0:T(8,128)(2,1)S(1)} %copy-done.5), channel_id=1, source_target_pairs={{0,4},{1,5},{2,6},{3,7},{4,0},{5,1},{6,2},{7,3},{8,12},{9,13},{10,... | collective-permute-start | bytes 2359304 | tf_op jit(solution)/shard_map/ppermute | solution.py:160
  369.8 17.6 %collective-permute-start.46 = (bf16[2,2,96,1024]{3,2,1,0:T(8,128)(2,1)}, bf16[2,2,96,1024]{3,2,1,0:T(8,128)(2,1)}, u32[]{:S(2)}, u32[]{:S(2)}) collective-permute-start(bf16[2,2,96,1024]{3,2,1,0:T(8,128)(2,1)} %shard_map.431), channel_id=1, source_target_pairs={{0,2},{1,3},{2,0},{3,1},{4,6},{5,7},{6,4},{7,5},{8,10},{9,11},{10,... | collective-permute-start | bytes 2359304 | tf_op jit(solution)/shard_map/ppermute | solution.py:160
  370.7 21.7 %all-to-all-start = ((bf16[4,32,3200]{2,1,0:T(8,128)(2,1)}), bf16[4,32,3200]{2,1,0:T(8,128)(2,1)S(1)}, u32[]{:S(2)}, u32[]{:S(2)}) async-start(bf16[4,32,3200]{2,1,0:T(8,128)(2,1)} %bitcast.14.refs_0_.refs_1_), calls=%async_computation.1 | async-start | bytes 1638400 | tf_op jit(solution)/shard_map/all_to_all | solution.py:1200
  (103 other events, 758.3 us)
Sparse Core Ops, SparseCore 0:
  9.6 45.4 all-gather.5
  57.6 98.2 all-gather.9
  158.3 46.1 all-gather.7
  207.9 129.7 reduce-scatter.1
